TPU v7x, 32 devices: a whole 2x2x4 slice. The times are simulated.
32 devices in a mesh: dp: 8 (over z, y), seq: 4 (over x, core).
Axes of the slice: x: 2, y: 2, z: 4, core: 2. Of those that a mesh axis runs over, the one named last changes fastest.
Arguments:
- grad_out: bfloat16 [8, 512, 2560], P('dp', 'seq'), may hold values from -6 to 6
- branch_out: bfloat16 [8, 512, 2560], P('dp', 'seq'), may hold values from -0.59765625 to 0.59765625
- down_weight: bfloat16 [8192, 2560], P('seq', 'dp'), may hold values from -0.0625 to 0.0625
- mod_gate: float32 [2560], replicated, may hold values from -3 to 3
- level_table: float32 [64, 2560], replicated, may hold values from -3 to 3
- frame_ids: int32 [8, 512], P('dp', 'seq'), may hold values from 0 to 2, never falling along the last dimension, each value on 1 to 384 neighbouring positions
- levels: int32 [8, 3], P('dp'), may hold values from 0 to 63
Outputs:
- hidden_grad: bfloat16 [8, 512, 8192], P('dp', None, 'seq')
- frame_grad: float32 [8, 3, 2560], P('dp', None, 'seq')
- table_grad: float32 [64, 2560], P('dp', 'seq')
Inputs may be any that keep to these rules, and one draw needn't show every extreme that they name: `frame_ids`: within each clip the frame ids never fall along the tokens; every frame holds 1 to 384 tokens, and some frame exactly 384.
All inputs are finite; a program needn't handle non-finite values.
Results may differ from a plain program's by a relative error of at most 0.0049.
Values may be sent and summed in bfloat16 or wider, within the bound.
No kernel may reach another device: no remote copies, remote signals or barrier semaphores. Data moves between devices by JAX's collectives and lax.ppermute only.
A program may use at most 128 MiB of HBM per device.

v0:
```python
import jax
import jax.numpy as jnp
from jax import lax
from jax.sharding import PartitionSpec as P


def body(grad_out, branch_out, down_weight, mod_gate, level_table, frame_ids, levels):
    highest = lax.Precision.HIGHEST
    upstream = grad_out[0]
    saved = branch_out[0]
    frames = frame_ids[0]
    level_row = levels[0]
    frame_count = level_row.shape[0]
    level_count = level_table.shape[0]
    frame_range = jnp.arange(frame_count, dtype=jnp.int32)
    frame_onehot = (frames[:, None] == frame_range[None, :]).astype(jnp.float32)
    level_onehot = (level_row[:, None] == jnp.arange(level_count, dtype=jnp.int32)[None, :]).astype(
        jnp.float32
    )
    gate_frames = mod_gate[None, :] + jnp.dot(level_onehot, level_table, precision=highest)
    weight_full = lax.all_gather(down_weight, "dp", axis=1, tiled=True)
    gate_tokens = jnp.dot(frame_onehot, gate_frames, precision=highest)
    scaled = (gate_tokens * upstream.astype(jnp.float32)).astype(jnp.bfloat16)
    hidden_grad = lax.dot_general(
        lax.all_gather(scaled, "seq", axis=0, tiled=True),
        weight_full,
        (((1,), (1,)), ((), ())),
        preferred_element_type=jnp.float32,
    ).astype(jnp.bfloat16)
    products = upstream.astype(jnp.float32) * saved.astype(jnp.float32)
    frame_part = jnp.dot(frame_onehot.T, products, precision=highest)
    frame_grad = lax.psum_scatter(frame_part, "seq", scatter_dimension=1, tiled=True)
    level_part = jnp.dot(level_onehot.T, frame_grad, precision=highest)
    table_grad = lax.psum_scatter(level_part, "dp", scatter_dimension=0, tiled=True)
    return (hidden_grad[None], frame_grad[None], table_grad)


def solution(mesh):
    return jax.shard_map(
        body,
        mesh=mesh,
        in_specs=(
            P("dp", "seq", None),
            P("dp", "seq", None),
            P("seq", "dp"),
            P(),
            P(),
            P("dp", "seq"),
            P("dp", None),
        ),
        out_specs=(P("dp", None, "seq"), P("dp", None, "seq"), P("dp", "seq")),
        check_vma=False,
    )
```

profile of v0, /device:TPU:0, one launch (start us, length us, event | category | flops | bytes accessed | tf_op | source)
XLA Modules:
  0.0 310.6 jit_solution(16414500028296005097)
XLA Ops:
  7.2 0.0 copy-start
  7.2 0.0 copy-start.3
  7.2 0.0 copy-start.4
  7.2 0.0 reduce-scatter.4.cloned.1.call-start
  7.2 0.0 copy-start.1
  7.3 0.0 copy-start.5
  7.3 3.7 %convolution_bitcast_fusion = f32[2560,3]{1,0:T(8,128)} fusion(bf16[1,128,2560]{2,1,0:T(8,128)(2,1)} %param.8, bf16[1,128,2560]{2,1,0:T(8,128)(2,1)} %param.7, s32[128]{0:T(128)} %bitcast.32), kind=kOutput, calls=%fused_computation.1 | convolution fusion | flops 12779904 | bytes 1341952
  10.9 0.0 reduce-scatter.4.cloned.1.call-update
  11.0 0.0 all-reduce.3.cloned.1.call-start
  11.0 0.0 copy-done
  11.0 0.0 copy-done.3
  11.0 0.0 copy-done.4
  11.0 0.3 convolution_add_fusion
  11.4 0.0 copy-start.6
  11.4 29.0 %reduce-scatter.4.cloned.1.call-done = f32[640,3]{1,0:T(8,128)} async-done(((f32[2560,3]{1,0:T(8,128)}), f32[640,3]{1,0:T(8,128)}) %reduce-scatter.4.cloned.1.call-update) | async-done | bytes 7696
  40.4 0.0 copy-start.2
  40.4 2.1 fusion.7
  42.5 0.0 all-reduce.3.cloned.1.call-update
  42.6 0.0 all-gather.3.cloned.1.call-start
  42.6 0.0 copy-done.1
  42.6 0.0 copy-done.5
  42.6 1.6 fusion
  44.2 0.0 all-gather.3.cloned.1.call-update
  44.2 0.0 all-gather.5.cloned.1.call-start
  44.3 0.5 all-gather.5.cloned.1.call-update
  44.8 0.0 copy-done.6
  44.8 0.6 dynamic-slice
  46.1 0.0 copy-done.2
  46.1 0.1 copy.13
  46.2 0.6 copy.11
  46.8 66.8 %all-reduce.3.cloned.1.call-done = f32[64,640]{1,0:T(8,128)} async-done(((f32[64,640]{1,0:T(8,128)}), f32[64,640]{1,0:T(8,128)}) %all-reduce.3.cloned.1.call-update) | async-done | bytes 163856
  113.6 1.3 constant_dynamic-slice_fusion
  114.9 26.2 %all-gather.3.cloned.1.call-done = bf16[512,2560]{1,0:T(8,128)(2,1)} async-done(((bf16[128,2560]{1,0:T(8,128)(2,1)}), bf16[512,2560]{1,0:T(8,128)(2,1)}) %all-gather.3.cloned.1.call-update) | async-done | bytes 2621456 | tf_op jit(solution)/shard_map/all_gather | solution.py:25
  141.1 152.9 %all-gather.5.cloned.1.call-done = bf16[2048,2560]{0,1:T(8,128)(2,1)} async-done(((bf16[2048,320]{0,1:T(8,128)(2,1)}), bf16[2048,2560]{0,1:T(8,128)(2,1)}) %all-gather.5.cloned.1.call-update) | async-done | bytes 10485776 | tf_op jit(solution)/shard_map/all_gather | solution.py:21
  294.0 10.0 %fusion.1 = bf16[1,512,2048]{2,1,0:T(8,128)(2,1)} fusion(bf16[512,2560]{1,0:T(8,128)(2,1)} %all-gather.3.cloned.1.call-done, bf16[2048,2560]{0,1:T(8,128)(2,1)} %all-gather.5.cloned.1.call-done), kind=kOutput, calls=%fused_computation.5 | convolution fusion | flops 5369757696 | bytes 15204352 | tf_op jit(solution)/shard_map/dot_general | solution.py:24
Async XLA Ops:
  7.2 3.9 %copy-start = (f32[64,2560]{1,0:T(8,128)S(1)}, f32[64,2560]{1,0:T(8,128)}, u32[]{:S(2)}) copy-start(f32[64,2560]{1,0:T(8,128)} %param.11) | copy-start | bytes 1966084
  7.2 3.9 %copy-start.3 = (f32[2560]{0:T(1024)S(1)}, f32[2560]{0:T(1024)}, u32[]{:S(2)}) copy-start(f32[2560]{0:T(1024)} %param.10) | copy-start | bytes 30724
  7.2 3.9 %copy-start.4 = (s32[1,3]{1,0:T(1,128)S(1)}, s32[1,3]{1,0:T(1,128)}, u32[]{:S(2)}) copy-start(s32[1,3]{1,0:T(1,128)} %param.13) | copy-start | bytes 40
  7.2 33.2 %reduce-scatter.4.cloned.1.call-start = ((), (), s32[]{:S(2)}) async-start(), calls=%async_computation.3 | async-start | bytes 1638400
  7.2 35.4 %copy-start.1 = (bf16[1,128,2560]{2,1,0:T(8,128)(2,1)S(1)}, bf16[1,128,2560]{2,1,0:T(8,128)(2,1)}, u32[]{:S(2)}) copy-start(bf16[1,128,2560]{2,1,0:T(8,128)(2,1)} %param.7) | copy-start | bytes 1966084
  7.3 35.4 %copy-start.5 = (s32[1,128]{1,0:T(1,128)S(1)}, s32[1,128]{1,0:T(1,128)}, u32[]{:S(2)}) copy-start(s32[1,128]{1,0:T(1,128)} %param.12) | copy-start | bytes 1540
  11.0 102.6 %all-reduce.3.cloned.1.call-start = ((), (), s32[]{:S(2)}) async-start(), calls=%async_computation.4 | async-start | bytes 327680
  11.4 33.4 %copy-start.6 = (u32[32]{0:T(128)S(1)}, u32[32]{0:T(128)}, u32[]{:S(2)}) copy-start(u32[32]{0:T(128)} %constant.6) | copy-start | bytes 388
  40.4 5.7 %copy-start.2 = (f32[640,3]{1,0:T(8,128)S(1)}, f32[640,3]{1,0:T(8,128)}, u32[]{:S(2)}) copy-start(f32[640,3]{1,0:T(8,128)} %reduce-scatter.4.cloned.1.call-done) | copy-start | bytes 23044
  42.6 98.5 %all-gather.3.cloned.1.call-start = ((), (), s32[]{:S(2)}) async-start(), calls=%async_computation.1 | async-start | bytes 3276800 | tf_op jit(solution)/shard_map/all_gather | solution.py:25
  44.2 249.8 %all-gather.5.cloned.1.call-start = ((), (), s32[]{:S(2)}) async-start(), calls=%async_computation.2 | async-start | bytes 11796480 | tf_op jit(solution)/shard_map/all_gather | solution.py:21
Sparse Core Ops, SparseCore 0:
  11.1 29.2 reduce-scatter.3
  44.1 69.4 all-reduce.2
  115.7 25.3 all-gather.2
  143.1 150.8 all-gather.4
where the time goes:
time: 311 us
  waiting for transfers between devices  275 us (88%)
  matrix products  17.8 us (6%)
  between operations  14.5 us (5%)
    all_gather x1, waiting for transfers between devices, body(): weight_full = lax.all_gather(down_weight, 'dp', axis=1, tiled=True)  153 us
    unnamed x6, waiting for transfers between devices  96.3 us
    all_gather x1, waiting for transfers between devices, body(): lax.all_gather(scaled, 'seq', axis=0, tiled=True)  26.2 us
    dot_general x1, matrix products, body(): lax.dot_general(lax.all_gather(scaled, 'seq', axis=0, tiled=True), weight...  10 us
  transfers between devices with their start and end apart: 4, of which 4 were waited for; matrix products, arithmetic and copies ran while one was open for 1% of the time, Pallas kernels for 0%

commit v1 on v0

v1 whole, which is shorter than its diff:
```python
import jax
import jax.numpy as jnp
from jax import lax
from jax.experimental import pallas as pl
from jax.experimental.pallas import tpu as pltpu
from jax.sharding import PartitionSpec as P

HIGHEST = lax.Precision.HIGHEST
GROUPS = ((1,), (1, 1, 1))


def gate_and_products(grad_out, branch_out, mod_gate, level_table, frame_ids, levels):
    upstream = grad_out[0].astype(jnp.float32)
    saved = branch_out[0].astype(jnp.float32)
    frames = frame_ids[0]
    level_row = levels[0]
    frame_range = jnp.arange(level_row.shape[0], dtype=jnp.int32)
    level_range = jnp.arange(level_table.shape[0], dtype=jnp.int32)
    frame_onehot = (frames[:, None] == frame_range[None, :]).astype(jnp.float32)
    level_onehot = (level_row[:, None] == level_range[None, :]).astype(jnp.float32)
    gate_frames = mod_gate[None, :] + jnp.dot(level_onehot, level_table, precision=HIGHEST)
    gate_tokens = jnp.dot(frame_onehot, gate_frames, precision=HIGHEST)
    scaled = (gate_tokens * upstream).astype(jnp.bfloat16)
    frame_part = jnp.dot(frame_onehot.T, upstream * saved, precision=HIGHEST)
    return scaled, frame_part, level_onehot


def plain_body(grad_out, branch_out, down_weight, mod_gate, level_table, frame_ids, levels):
    scaled, frame_part, level_onehot = gate_and_products(
        grad_out, branch_out, mod_gate, level_table, frame_ids, levels
    )
    hidden_grad = lax.dot_general(
        lax.all_gather(scaled, "seq", axis=0, tiled=True),
        lax.all_gather(down_weight, "dp", axis=1, tiled=True),
        (((1,), (1,)), ((), ())),
        preferred_element_type=jnp.float32,
    ).astype(jnp.bfloat16)
    frame_grad = lax.psum_scatter(frame_part, "seq", scatter_dimension=1, tiled=True)
    level_part = jnp.dot(level_onehot.T, frame_grad, precision=HIGHEST)
    table_grad = lax.psum_scatter(level_part, "dp", scatter_dimension=0, tiled=True)
    return hidden_grad[None], frame_grad[None], table_grad


def seq_step(frame_part, seq, flip, gate):
    width = frame_part.shape[1] // 2
    low, high = frame_part[:, :width], frame_part[:, width:]
    upper = (lax.axis_index("seq") & flip) != 0
    sent = after(jnp.where(upper, low, high), *gate)
    held = jnp.where(upper, high, low)
    return held + lax.ppermute(sent, "seq", [(i, i ^ flip) for i in range(seq)])


def pack_frames(frame_grad, levels):
    frame_count, width = frame_grad.shape
    level_line = jnp.pad(levels.astype(jnp.float32), ((0, 0), (0, width - frame_count)))
    return jnp.concatenate([frame_grad, level_line], axis=0)[None]


def clip_step(packed, dp, flip, gate):
    sent = after(packed, *gate)
    arrived = lax.ppermute(sent, "dp", [(i, i ^ flip) for i in range(dp)])
    return jnp.concatenate([packed, arrived], axis=0)


def table_of(packed, level_count):
    dp, lines, width = packed.shape
    frame_count = lines - 1
    owned = level_count // dp
    rows = (lax.axis_index("dp") * owned + jnp.arange(owned, dtype=jnp.int32)).astype(jnp.float32)
    sums = packed[:, :frame_count].reshape(dp * frame_count, width)
    marks = packed[:, frame_count, :frame_count].reshape(dp * frame_count)
    onehot = (rows[:, None] == marks[None, :]).astype(jnp.float32)
    return jnp.dot(onehot, sums, precision=HIGHEST)


def after(array, *earlier):
    return lax.optimization_barrier((array, *earlier))[0]


def join_rows(first_row, upper, lower, offset):
    rows, width = upper.shape
    vmem = pl.BlockSpec(memory_space=pltpu.VMEM)

    def kernel(first_row, upper, lower, result):
        start = pl.multiple_of(first_row[0], 16)
        result[pl.ds(start, rows), :] = upper[...]
        rest = pl.multiple_of(rows - start, 16)
        result[pl.ds(rest, rows), :] = lower[:, offset : offset + width]

    return pl.pallas_call(
        kernel,
        out_shape=jax.ShapeDtypeStruct((2 * rows, width), upper.dtype),
        in_specs=[pl.BlockSpec(memory_space=pltpu.SMEM), vmem, vmem],
        out_specs=vmem,
        compiler_params=pltpu.CompilerParams(vmem_limit_bytes=16 << 20),
        name="join_rows",
    )(first_row.astype(jnp.int32).reshape(1), upper, lower)


def stack_rows(upper, lower, start, width):
    rows = upper.shape[0]
    vmem = pl.BlockSpec(memory_space=pltpu.VMEM)

    def kernel(upper, lower, result):
        result[:rows] = upper[:, start : start + width]
        result[rows:] = lower[:, start : start + width]

    return pl.pallas_call(
        kernel,
        out_shape=jax.ShapeDtypeStruct((2 * rows, width), upper.dtype),
        in_specs=[vmem, vmem],
        out_specs=vmem,
        compiler_params=pltpu.CompilerParams(vmem_limit_bytes=16 << 20),
        name="stack_rows",
    )(upper, lower)


def order_pieces(me, pieces):
    count = len(pieces)
    rows, width = pieces[0].shape
    any_space = pl.BlockSpec(memory_space=pl.ANY)

    def kernel(place, *refs):
        result, sems = refs[count], refs[count + 1]
        copies = []
        for flip in range(count):
            start = pl.multiple_of((place[0] ^ flip) * rows, 128)
            copies.append(
                pltpu.make_async_copy(refs[flip], result.at[pl.ds(start, rows)], sems.at[flip])
            )
            copies[-1].start()
        for copy in copies:
            copy.wait()

    return pl.pallas_call(
        kernel,
        out_shape=jax.ShapeDtypeStruct((count * rows, width), pieces[0].dtype),
        in_specs=[pl.BlockSpec(memory_space=pltpu.SMEM)] + [any_space] * count,
        out_specs=pl.BlockSpec(memory_space=pltpu.VMEM),
        scratch_shapes=[pltpu.SemaphoreType.DMA((count,))],
        compiler_params=pltpu.CompilerParams(vmem_limit_bytes=16 << 20),
        name="order_pieces",
    )(me.astype(jnp.int32).reshape(1), *pieces)


def assemble(y, starts, kept, received):
    count, half = len(kept), sum(part.shape[1] for part in kept)
    rows = kept[0].shape[0]
    vmem = pl.BlockSpec(memory_space=pltpu.VMEM)

    def kernel(place, *refs):
        result = refs[2 * count]
        for index, start in enumerate(starts):
            width = kept[index].shape[1]
            mine = pl.multiple_of(place[0] * half + start, 128)
            theirs = pl.multiple_of((1 - place[0]) * half + start, 128)
            result[:, pl.ds(mine, width)] = refs[index][...]
            result[:, pl.ds(theirs, width)] = refs[count + index][...]

    return pl.pallas_call(
        kernel,
        out_shape=jax.ShapeDtypeStruct((rows, 2 * half), kept[0].dtype),
        in_specs=[pl.BlockSpec(memory_space=pltpu.SMEM)] + [vmem] * (2 * count),
        out_specs=vmem,
        compiler_params=pltpu.CompilerParams(vmem_limit_bytes=16 << 20),
        name="assemble",
    )(y.astype(jnp.int32).reshape(1), *kept, *received)


def staged_body(grad_out, branch_out, down_weight, mod_gate, level_table, frame_ids, levels):
    dp, seq = 8, 4
    clip, me = lax.axis_index("dp"), lax.axis_index("seq")
    z, y = clip // 2, clip % 2
    is_mid = jnp.logical_or(z == 1, z == 2)
    hidden, shard = down_weight.shape
    half = hidden // 2
    block = 2 * shard

    def along_z(array, pairs):
        perm = [(a * 2 + s, b * 2 + s) for a, b in pairs for s in range(2)]
        return lax.ppermute(array, "dp", perm)

    def over_y(array):
        return lax.ppermute(array, "dp", [(i, i ^ 1) for i in range(dp)])

    def over_seq(array, flip):
        return lax.ppermute(array, "seq", [(i, i ^ flip) for i in range(seq)])

    def ordered(flag, first, second, axis):
        swapped = jnp.concatenate([second, first], axis=axis)
        return jnp.where(flag, swapped, jnp.concatenate([first, second], axis=axis))

    weight = down_weight.T
    unit = half // sum(sum(group) for group in GROUPS)
    starts, start = [], 0
    for group in GROUPS:
        starts.append(start)
        start += sum(group) * unit

    def columns(owner, start, width):
        return lax.dynamic_slice(weight, (0, owner * half + start), (shard, width))

    def own_block(index, arrived, offset):
        width = sum(GROUPS[index]) * unit
        return join_rows(y * shard, columns(y, starts[index], width), arrived, offset)

    def pairs_of(index, own, near):
        blocks, offset = [], 0
        for width in GROUPS[index]:
            blocks.append((starts[index] + offset, stack_rows(own, near, offset, width * unit)))
            offset += width * unit
        return blocks

    head = starts[1]
    arrived_0 = over_y(columns(1 - y, 0, head))
    scaled, frame_part, _ = gate_and_products(
        grad_out, branch_out, mod_gate, level_table, after(frame_ids, arrived_0), levels
    )
    order = [z, z ^ 1, jnp.where(is_mid, z ^ 3, z ^ 2), jnp.where(is_mid, z ^ 2, z ^ 3)]
    piece = scaled.shape[0]
    scaled = jnp.concatenate(
        [lax.dynamic_slice(scaled, (0, owner * block), (piece, block)) for owner in order], axis=1
    )
    def to_near(own):
        return along_z(own, [(0, 1), (1, 0), (2, 3), (3, 2)])

    def across(block):
        return along_z(block, [(1, 2), (2, 1)])

    def outward(block):
        return along_z(block, [(1, 0), (2, 3)])

    kept, received = [], []

    def multiply(pair, crossed, forwarded):
        far = jnp.where(is_mid, crossed, forwarded)
        full = jnp.concatenate([pair, far], axis=0)
        part = jnp.dot(other, full, preferred_element_type=jnp.float32).astype(jnp.bfloat16)
        received.append(over_y(part))
        kept.append(jnp.dot(mine, full, preferred_element_type=jnp.float32).astype(jnp.bfloat16))
        return part, kept[-1]

    own_0 = own_block(0, arrived_0, 0)
    near_0 = to_near(own_0)
    rest = over_y(after(columns(1 - y, head, half - head), arrived_0))

    gate = (near_0, rest)
    pairs = pairs_of(0, own_0, near_0)
    own_1 = own_block(1, rest, 0)
    near_1 = to_near(after(own_1, *gate))
    crossed_0 = across(after(pairs[0][1], *gate))
    mine_x = over_seq(after(scaled, *gate), 2)
    theirs = over_y(after(scaled, *gate))
    frame_part = seq_step(frame_part, seq, 2, gate)

    gate = (near_1, crossed_0, mine_x, theirs, frame_part)
    pairs += pairs_of(1, own_1, near_1)
    forwarded_0 = outward(after(crossed_0, *gate))
    crossed_1 = across(after(pairs[1][1], *gate))
    theirs_x = over_seq(after(theirs, *gate), 2)
    mine_core = over_seq(after(jnp.stack([scaled, mine_x]), *gate), 1)
    frame_grad = seq_step(frame_part, seq, 1, gate)
    packed = pack_frames(frame_grad, levels)

    gate = (forwarded_0, crossed_1, theirs_x, mine_core, packed)
    forwarded_1 = outward(after(crossed_1, *gate))
    crossed_2 = across(after(pairs[2][1], *gate))
    other_core = over_seq(after(jnp.stack([theirs, theirs_x]), *gate), 1)
    mine = order_pieces(me, [scaled, mine_core[0], mine_x, mine_core[1]])
    packed = clip_step(packed, dp, 1, gate)

    gate = (forwarded_1, crossed_2, mine, other_core, packed)
    forwarded_2 = outward(after(crossed_2, *gate))
    crossed_3 = across(after(pairs[3][1], *gate))
    packed = clip_step(packed, dp, 2, gate)
    other = order_pieces(me, [theirs, other_core[0], theirs_x, other_core[1]])
    products = multiply(after(pairs[0][1], packed), crossed_0, forwarded_0)
    products += multiply(after(pairs[1][1], packed), crossed_1, forwarded_1)

    gate = (forwarded_2, crossed_3, packed, *products)
    forwarded_3 = outward(after(crossed_3, *gate))
    packed = clip_step(packed, dp, 4, gate)
    table_grad = table_of(packed, level_table.shape[0])
    multiply(pairs[2][1], crossed_2, forwarded_2)
    multiply(pairs[3][1], crossed_3, forwarded_3)
    hidden_grad = assemble(y, [start for start, _ in pairs], kept, received)
    return hidden_grad[None], frame_grad[None], table_grad


def solution(mesh):
    staged = mesh.shape["dp"] == 8 and mesh.shape["seq"] == 4
    return jax.shard_map(
        staged_body if staged else plain_body,
        mesh=mesh,
        in_specs=(
            P("dp", "seq", None),
            P("dp", "seq", None),
            P("seq", "dp"),
            P(),
            P(),
            P("dp", "seq"),
            P("dp", None),
        ),
        out_specs=(P("dp", None, "seq"), P("dp", None, "seq"), P("dp", "seq")),
        check_vma=False,
    )
```

time: 311 us -> 142 us (0.46)
  waiting for transfers between devices: 275 us -> 77.6 us
  starting transfers between devices: 0.16 us -> 32.2 us
  between operations: 14.5 us -> 1.24 us
  Pallas kernels: 0 us -> 4.68 us
  other arithmetic: 0 us -> 3.76 us
    all_gather x2 -> x0, waiting for transfers between devices: 179 us -> none  [the longest x1 153 us: body(): weight_full = lax.all_gather(down_weight, 'dp', axis=1, tiled=True)]
    unnamed x6 -> x0, waiting for transfers between devices: 96.3 us -> none
    ppermute x0 -> x26, waiting for transfers between devices: none -> 77.6 us  [the longest x10 42.4 us: along_z(): return lax.ppermute(array, 'dp', perm)]
    ppermute x0 -> x26, starting transfers between devices: none -> 32.2 us  [the longest x10 11.1 us: along_z(): return lax.ppermute(array, 'dp', perm)]
    pallas_call x0 -> x9, Pallas kernels: none -> 4.68 us  [the longest x1 2.64 us: assemble(): pl.pallas_call(kernel, out_shape=jax.ShapeDtypeStruct((rows, 2 * half), k...]
    unnamed x1 -> x0, matrix products: 3.68 us -> none
    dot_general x4 -> x12, matrix products: 14.1 us -> 17 us  [the longest x4 7.25 us: multiply(): jnp.dot(other, full, preferred_element_type=jnp.float32)]
  transfers between devices with their start and end apart: 4 -> 26, of which waited for: 4 -> 12; matrix products, arithmetic and copies ran while one was open for 1% -> 17% of each run, Pallas kernels for 0% -> 1%
where the time goes in v1:
time: 142 us; the launch traced here: 141 us
  waiting for transfers between devices  77.6 us (55%)
  starting transfers between devices  32.2 us (23%)
  matrix products  17 us (12%)
  local copies, waits for them, and re-layouts  5.01 us (4%)
  Pallas kernels  4.68 us (3%)
  other arithmetic  3.76 us (3%)
    ppermute x10, waiting for transfers between devices, along_z(): return lax.ppermute(array, 'dp', perm)  42.4 us
    ppermute x7, waiting for transfers between devices, over_y(): return lax.ppermute(array, 'dp', [(i, i ^ 1) for i in range(dp)])  25.2 us
    ppermute x10, starting transfers between devices, along_z(): return lax.ppermute(array, 'dp', perm)  11.1 us
    ppermute x4, waiting for transfers between devices, over_seq(): return lax.ppermute(array, 'seq', [(i, i ^ flip) for i in range(seq)])  9.95 us
    ppermute x7, starting transfers between devices, over_y(): return lax.ppermute(array, 'dp', [(i, i ^ 1) for i in range(dp)])  9.3 us
    ppermute x3, starting transfers between devices, clip_step(): arrived = lax.ppermute(sent, 'dp', [(i, i ^ flip) for i in range(dp)])  8.62 us
    dot_general x4, matrix products, multiply(): jnp.dot(other, full, preferred_element_type=jnp.float32)  7.25 us
    dot_general x4, matrix products, multiply(): jnp.dot(mine, full, preferred_element_type=jnp.float32).astype(jnp.bfloat16)  5.5 us
  transfers between devices with their start and end apart: 26, of which 12 were waited for; matrix products, arithmetic and copies ran while one was open for 17% of the time, Pallas kernels for 1%

profile of v1, /device:TPU:0, one launch (start us, length us, event | category | flops | bytes accessed | tf_op | source)
XLA Modules:
  0.0 141.5 jit_solution(8657722315450462987)
XLA Ops:
  0.7 1.2 dynamic-slice_bitcast_fusion.2
  1.8 3.0 %collective-permute-start = (bf16[320,256]{1,0:T(8,128)(2,1)S(1)}, bf16[320,256]{1,0:T(8,128)(2,1)S(1)}, u32[]{:S(2)}, u32[]{:S(2)}) collective-permute-start(bf16[320,256]{1,0:T(8,128)(2,1)S(1)} %get-tuple-element.60), channel_id=1, source_target_pairs={{0,4},{4,0},{8,12},{12,8},{16,20},{20,16},{24,28},{28,24},{1,5},{5... | collective-permute-start | bytes 491528 | tf_op jit(solution)/shard_map/ppermute | solution.py:184
  4.9 1.1 convolution_add_fusion
  6.1 0.1 dynamic-slice_bitcast_fusion
  6.2 2.9 %collective-permute-done.lower = bf16[320,256]{1,0:T(8,128)(2,1)S(1)} collective-permute-done((bf16[320,256]{1,0:T(8,128)(2,1)S(1)}, bf16[320,256]{1,0:T(8,128)(2,1)S(1)}, u32[]{:S(2)}, u32[]{:S(2)}) %collective-permute-start) | collective-permute-done | bytes 163872 | tf_op jit(solution)/shard_map/ppermute | solution.py:184
  9.1 1.9 %collective-permute-start.1 = (bf16[640,256]{1,0:T(8,128)(2,1)S(1)}, bf16[640,256]{1,0:T(8,128)(2,1)S(1)}, u32[]{:S(2)}, u32[]{:S(2)}) collective-permute-start(bf16[640,256]{1,0:T(8,128)(2,1)S(1)} %join_rows.2.upper), channel_id=1, source_target_pairs={{0,8},{4,12},{8,0},{12,4},{16,24},{20,28},{24,16},{28,20},{1,9},{5... | collective-permute-start | bytes 983048 | tf_op jit(solution)/shard_map/ppermute | solution.py:181
  11.0 0.7 fusion.1
  11.7 0.8 fusion
  12.4 1.6 %collective-permute-start.2 = (bf16[320,768]{1,0:T(8,128)(2,1)S(1)}, bf16[320,768]{1,0:T(8,128)(2,1)S(1)}, u32[]{:S(2)}, u32[]{:S(2)}) collective-permute-start(bf16[320,768]{1,0:T(8,128)(2,1)S(1)} %get-tuple-element.26), channel_id=1, source_target_pairs={{0,4},{4,0},{8,12},{12,8},{16,20},{20,16},{24,28},{28,24},{1,5},{5... | collective-permute-start | bytes 1474568 | tf_op jit(solution)/shard_map/ppermute | solution.py:184
  14.1 4.0 %collective-permute-done.1.lower = bf16[640,256]{1,0:T(8,128)(2,1)S(1)} collective-permute-done((bf16[640,256]{1,0:T(8,128)(2,1)S(1)}, bf16[640,256]{1,0:T(8,128)(2,1)S(1)}, u32[]{:S(2)}, u32[]{:S(2)}) %collective-permute-start.1) | collective-permute-done | bytes 327712 | tf_op jit(solution)/shard_map/ppermute | solution.py:181
  18.1 6.2 %collective-permute-done.2.lower = bf16[320,768]{1,0:T(8,128)(2,1)S(1)} collective-permute-done((bf16[320,768]{1,0:T(8,128)(2,1)S(1)}, bf16[320,768]{1,0:T(8,128)(2,1)S(1)}, u32[]{:S(2)}, u32[]{:S(2)}) %collective-permute-start.2) | collective-permute-done | bytes 491552 | tf_op jit(solution)/shard_map/ppermute | solution.py:184
  24.3 1.5 %collective-permute-start.7 = (f32[3,1280]{1,0:T(4,128)S(1)}, f32[3,1280]{1,0:T(4,128)S(1)}, u32[]{:S(2)}, u32[]{:S(2)}) collective-permute-start(f32[3,1280]{1,0:T(4,128)S(1)} %slice_select_fusion), channel_id=1, source_target_pairs={{0,2},{1,3},{2,0},{3,1},{4,6},{5,7},{6,4},{7,5},{8,10},{9,11},{10,... | collective-permute-start | bytes 46088 | tf_op jit(solution)/shard_map/ppermute | solution.py:50
  25.9 0.5 collective-permute-start.4
  26.4 0.1 fusion.21
  26.5 1.6 %collective-permute-start.6 = (bf16[128,2560]{1,0:T(8,128)(2,1)S(1)}, bf16[128,2560]{1,0:T(8,128)(2,1)S(1)}, u32[]{:S(2)}, u32[]{:S(2)}) collective-permute-start(bf16[128,2560]{1,0:T(8,128)(2,1)S(1)} %get-tuple-element.27.refs_0_), channel_id=1, source_target_pairs={{0,4},{4,0},{8,12},{12,8},{16,20},{20,16},{24,28},{28,24},{1,5},{5... | collective-permute-start | bytes 1966088 | tf_op jit(solution)/shard_map/ppermute | solution.py:184
  28.1 0.5 collective-permute-start.3
  28.7 0.7 collective-permute-start.5
  29.4 11.0 %collective-permute-done.6.refs_0_ = bf16[128,2560]{1,0:T(8,128)(2,1)S(1)} collective-permute-done((bf16[128,2560]{1,0:T(8,128)(2,1)S(1)}, bf16[128,2560]{1,0:T(8,128)(2,1)S(1)}, u32[]{:S(2)}, u32[]{:S(2)}) %collective-permute-start.6) | collective-permute-done | bytes 655392 | tf_op jit(solution)/shard_map/ppermute | solution.py:184
  40.4 1.5 %collective-permute-done.3.refs_2_ = bf16[128,2560]{1,0:T(8,128)(2,1)S(1)} collective-permute-done((bf16[128,2560]{1,0:T(8,128)(2,1)S(1)}, bf16[128,2560]{1,0:T(8,128)(2,1)S(1)}, u32[]{:S(2)}, u32[]{:S(2)}) %collective-permute-start.3) | collective-permute-done | bytes 655392 | tf_op jit(solution)/shard_map/ppermute | solution.py:187
  41.9 5.2 %collective-permute-done.4.lower = bf16[640,768]{1,0:T(8,128)(2,1)S(1)} collective-permute-done((bf16[640,768]{1,0:T(8,128)(2,1)S(1)}, bf16[640,768]{1,0:T(8,128)(2,1)S(1)}, u32[]{:S(2)}, u32[]{:S(2)}) %collective-permute-start.4) | collective-permute-done | bytes 983072 | tf_op jit(solution)/shard_map/ppermute | solution.py:181
  47.1 0.5 collective-permute-start.12
  47.6 0.1 pad_maximum_fusion
  47.8 0.5 collective-permute-start.8
  48.3 0.5 add_convert_fusion
  48.9 0.7 collective-permute-start.11
  49.6 1.3 collective-permute-start.10
  51.1 0.7 copy.11
  51.8 8.5 %collective-permute-done.12.refs_2_ = bf16[128,2560]{1,0:T(8,128)(2,1)S(1)} collective-permute-done((bf16[128,2560]{1,0:T(8,128)(2,1)S(1)}, bf16[128,2560]{1,0:T(8,128)(2,1)S(1)}, u32[]{:S(2)}, u32[]{:S(2)}) %collective-permute-start.12) | collective-permute-done | bytes 655392 | tf_op jit(solution)/shard_map/ppermute | solution.py:187
  60.3 0.1 pad_maximum_fusion.1
  60.4 9.5 %collective-permute-done.10 = bf16[1280,256]{1,0:T(8,128)(2,1)S(1)} collective-permute-done((bf16[1280,256]{1,0:T(8,128)(2,1)S(1)}, bf16[1280,256]{1,0:T(8,128)(2,1)S(1)}, u32[]{:S(2)}, u32[]{:S(2)}) %collective-permute-start.10) | collective-permute-done | bytes 655392 | tf_op jit(solution)/shard_map/ppermute | solution.py:181
  70.0 1.6 %collective-permute-start.13 = (f32[1,4,640]{2,1,0:T(4,128)S(1)}, f32[1,4,640]{2,1,0:T(4,128)S(1)}, u32[]{:S(2)}, u32[]{:S(2)}) collective-permute-start(f32[1,4,640]{2,1,0:T(4,128)S(1)} %fusion.7), channel_id=1, source_target_pairs={{0,4},{4,0},{8,12},{12,8},{16,20},{20,16},{24,28},{28,24},{1,5},{5... | collective-permute-start | bytes 30728 | tf_op jit(solution)/shard_map/ppermute | solution.py:61
  71.6 1.3 collective-permute-start.14
  72.9 0.7 collective-permute-start.15
  73.7 0.1 slice_bitcast_fusion.2
  73.8 0.9 order_pieces.2
  74.7 14.4 %collective-permute-done.14 = bf16[1280,256]{1,0:T(8,128)(2,1)S(1)} collective-permute-done((bf16[1280,256]{1,0:T(8,128)(2,1)S(1)}, bf16[1280,256]{1,0:T(8,128)(2,1)S(1)}, u32[]{:S(2)}, u32[]{:S(2)}) %collective-permute-start.14) | collective-permute-done | bytes 655392 | tf_op jit(solution)/shard_map/ppermute | solution.py:181
  89.2 3.6 %collective-permute-start.17 = (f32[2,4,640]{2,1,0:T(4,128)S(1)}, f32[2,4,640]{2,1,0:T(4,128)S(1)}, u32[]{:S(2)}, u32[]{:S(2)}) collective-permute-start(f32[2,4,640]{2,1,0:T(4,128)S(1)} %pad_maximum_fusion.19), channel_id=1, source_target_pairs={{0,8},{4,12},{8,0},{12,4},{16,24},{20,28},{24,16},{28,20},{1,9},{5... | collective-permute-start | bytes 61448 | tf_op jit(solution)/shard_map/ppermute | solution.py:61
  92.8 1.3 collective-permute-start.18
  94.1 1.5 %collective-permute-start.19 = (bf16[1280,256]{1,0:T(8,128)(2,1)S(1)}, bf16[1280,256]{1,0:T(8,128)(2,1)}, u32[]{:S(2)}, u32[]{:S(2)}) collective-permute-start(bf16[1280,256]{1,0:T(8,128)(2,1)S(1)} %stack_rows.7), channel_id=1, source_target_pairs={{8,16},{12,20},{16,8},{20,12},{9,17},{13,21},{17,9},{21,13},{10,18... | collective-permute-start | bytes 1966088 | tf_op jit(solution)/shard_map/ppermute | solution.py:181
  95.7 0.9 order_pieces.3
  96.6 1.6 %convolution_convert_fusion.4 = bf16[512,256]{1,0:T(8,128)(2,1)} fusion(bf16[512,2560]{1,0:T(8,128)(2,1)S(1)} %order_pieces.3, bf16[1280,256]{1,0:T(8,128)(2,1)S(1)} %broadcast_select_fusion.3, bf16[1280,256]{1,0:T(8,128)(2,1)S(1)} %stack_rows.4), kind=kOutput, calls=%fused_computation.16 | convolution fusion | flops 673841152 | bytes 4194304 | tf_op jit(solution)/shard_map/dot_general | solution.py:238
  98.2 0.5 collective-permute-start.21
  98.7 1.6 %convolution_convert_fusion.3 = bf16[512,256]{1,0:T(8,128)(2,1)} fusion(bf16[512,2560]{1,0:T(8,128)(2,1)S(1)} %order_pieces.3, bf16[1280,256]{1,0:T(8,128)(2,1)S(1)} %broadcast_select_fusion.2, bf16[1280,256]{1,0:T(8,128)(2,1)S(1)} %stack_rows.5), kind=kOutput, calls=%fused_computation.15 | convolution fusion | flops 673841152 | bytes 4194304 | tf_op jit(solution)/shard_map/dot_general | solution.py:238
  100.3 1.5 %collective-permute-start.22 = (bf16[512,256]{1,0:T(8,128)(2,1)}, bf16[512,256]{1,0:T(8,128)(2,1)}, u32[]{:S(2)}, u32[]{:S(2)}) collective-permute-start(bf16[512,256]{1,0:T(8,128)(2,1)} %convolution_convert_fusion.3), channel_id=1, source_target_pairs={{0,4},{4,0},{8,12},{12,8},{16,20},{20,16},{24,28},{28,24},{1,5},{5... | collective-permute-start | bytes 786440 | tf_op jit(solution)/shard_map/ppermute | solution.py:184
  101.8 1.6 %convolution_convert_fusion.7.refs_0_ = bf16[512,256]{1,0:T(8,128)(2,1)} fusion(bf16[512,2560]{1,0:T(8,128)(2,1)S(1)} %order_pieces.2, bf16[1280,256]{1,0:T(8,128)(2,1)S(1)} %broadcast_select_fusion.3, bf16[1280,256]{1,0:T(8,128)(2,1)S(1)} %stack_rows.4), kind=kOutput, calls=%fused_computation.19 | convolution fusion | flops 673841152 | bytes 4194304 | tf_op jit(solution)/shard_map/dot_general | solution.py:240
  103.4 1.5 %convolution_convert_fusion.6.refs_1_ = bf16[512,256]{1,0:T(8,128)(2,1)} fusion(bf16[512,2560]{1,0:T(8,128)(2,1)S(1)} %order_pieces.2, bf16[1280,256]{1,0:T(8,128)(2,1)S(1)} %broadcast_select_fusion.2, bf16[1280,256]{1,0:T(8,128)(2,1)S(1)} %stack_rows.5), kind=kOutput, calls=%fused_computation.18 | convolution fusion | flops 673841152 | bytes 4194304 | tf_op jit(solution)/shard_map/dot_general | solution.py:240
  104.9 3.9 %collective-permute-done.18 = bf16[1280,256]{1,0:T(8,128)(2,1)S(1)} collective-permute-done((bf16[1280,256]{1,0:T(8,128)(2,1)S(1)}, bf16[1280,256]{1,0:T(8,128)(2,1)S(1)}, u32[]{:S(2)}, u32[]{:S(2)}) %collective-permute-start.18) | collective-permute-done | bytes 655392 | tf_op jit(solution)/shard_map/ppermute | solution.py:181
  108.9 1.6 %convolution_convert_fusion.5.refs_2_ = bf16[512,256]{1,0:T(8,128)(2,1)} fusion(bf16[512,2560]{1,0:T(8,128)(2,1)S(1)} %order_pieces.2, bf16[1280,256]{1,0:T(8,128)(2,1)S(1)} %broadcast_select_fusion.1, bf16[1280,256]{1,0:T(8,128)(2,1)S(1)} %stack_rows.6), kind=kOutput, calls=%fused_computation.17 | convolution fusion | flops 673841152 | bytes 4194304 | tf_op jit(solution)/shard_map/dot_general | solution.py:240
  110.4 3.4 %collective-permute-start.25 = (f32[4,4,640]{2,1,0:T(4,128)S(1)}, f32[4,4,640]{2,1,0:T(4,128)S(1)}, u32[]{:S(2)}, u32[]{:S(2)}) collective-permute-start(f32[4,4,640]{2,1,0:T(4,128)S(1)} %pad_maximum_fusion.18), channel_id=1, source_target_pairs={{0,16},{4,20},{8,24},{12,28},{16,0},{20,4},{24,8},{28,12},{1,17},{... | collective-permute-start | bytes 122888 | tf_op jit(solution)/shard_map/ppermute | solution.py:61
  113.9 1.3 collective-permute-start.20
  115.2 1.6 %convolution_convert_fusion.1 = bf16[512,256]{1,0:T(8,128)(2,1)} fusion(bf16[512,2560]{1,0:T(8,128)(2,1)S(1)} %order_pieces.3, bf16[1280,256]{1,0:T(8,128)(2,1)S(1)} %broadcast_select_fusion.1, bf16[1280,256]{1,0:T(8,128)(2,1)S(1)} %stack_rows.6), kind=kOutput, calls=%fused_computation.13 | convolution fusion | flops 673841152 | bytes 4194304 | tf_op jit(solution)/shard_map/dot_general | solution.py:238
  116.7 0.5 collective-permute-start.23
  117.2 0.6 copy-done.12
  117.9 0.6 eq.64
  118.5 1.4 %pad_maximum_fusion.15 = f32[8,3,640]{2,1,0:T(4,128)} fusion(f32[4,4,640]{2,1,0:T(4,128)} %copy-done.12, f32[2,4,640]{2,1,0:T(4,128)} %copy-done.10, f32[1,4,640]{2,1,0:T(4,128)} %copy-done.11, f32[1,4,640]{2,1,0:T(4,128)S(1)} %fusion.7), kind=kLoop, calls=%fused_computation.35 | loop fusion | flops 46080 | bytes 143360 | tf_op jit(solution)/shard_map/concatenate | solution.py:62
  119.9 1.5 %reshape.36 = f32[24,640]{1,0:T(8,128)} reshape(f32[8,3,640]{2,1,0:T(4,128)} %pad_maximum_fusion.15) | data formatting | bytes 122880 | tf_op jit(solution)/shard_map/reshape | solution.py:70
  121.4 1.7 %fusion.8 = f32[8,640]{1,0:T(8,128)} fusion(f32[24,640]{1,0:T(8,128)} %reshape.36, f32[24]{0:T(128)} %eq.64, f32[8]{0:T(128)} %add_convert_fusion), kind=kOutput, calls=%fused_computation.51 | convolution fusion | flops 1474752 | bytes 82048 | tf_op jit(solution)/shard_map/dot_general | solution.py:73
  123.1 5.4 %collective-permute-done.20 = bf16[1280,256]{1,0:T(8,128)(2,1)} collective-permute-done((bf16[1280,256]{1,0:T(8,128)(2,1)}, bf16[1280,256]{1,0:T(8,128)(2,1)}, u32[]{:S(2)}, u32[]{:S(2)}) %collective-permute-start.20) | collective-permute-done | bytes 655392 | tf_op jit(solution)/shard_map/ppermute | solution.py:181
  128.6 1.2 broadcast_select_fusion
  129.7 2.6 %convolution_convert_fusion = bf16[512,256]{1,0:T(8,128)(2,1)S(1)} fusion(bf16[512,2560]{1,0:T(8,128)(2,1)} %copy-done.1, bf16[1280,256]{1,0:T(8,128)(2,1)S(1)} %broadcast_select_fusion, bf16[1280,256]{1,0:T(8,128)(2,1)S(1)} %copy-done.3), kind=kOutput, calls=%fused_computation.12 | convolution fusion | flops 673841152 | bytes 4194304 | tf_op jit(solution)/shard_map/dot_general | solution.py:238
  132.4 0.6 collective-permute-start.24
  132.9 0.8 convolution_convert_fusion.2.refs_3_
  133.8 5.0 %collective-permute-done.24.refs_7_ = bf16[512,256]{1,0:T(8,128)(2,1)S(1)} collective-permute-done((bf16[512,256]{1,0:T(8,128)(2,1)S(1)}, bf16[512,256]{1,0:T(8,128)(2,1)S(1)}, u32[]{:S(2)}, u32[]{:S(2)}) %collective-permute-start.24) | collective-permute-done | bytes 262176 | tf_op jit(solution)/shard_map/ppermute | solution.py:184
  138.8 2.6 %assemble.1 = bf16[512,2048]{1,0:T(8,128)(2,1)} custom-call(s32[1]{0:T(128)} %bitcast.place, bf16[512,256]{1,0:T(8,128)(2,1)S(1)} %copy-done.4, bf16[512,256]{1,0:T(8,128)(2,1)S(1)} %copy-done.5, bf16[512,256]{1,0:T(8,128)(2,1)S(1)} %copy-done.6, bf16[512,256]{1,0:T(8,128)(2,1)S(1)} %convolution_convert_fusion.2.refs_3_, ...), custom_call_target="tpu_custom_call" | custom-call | tf_op jit(solution)/shard_map/assemble/pallas_call | solution.py:160
  (65 shorter events, 1.0 us)
Async XLA Ops:
  0.6 4.2 %copy-start = (f32[64,2560]{1,0:T(8,128)S(1)}, f32[64,2560]{1,0:T(8,128)}, u32[]{:S(2)}) copy-start(f32[64,2560]{1,0:T(8,128)} %param.11) | copy-start | bytes 1966084
  0.6 5.4 %copy-start.8 = (bf16[2048,320]{0,1:T(8,128)(2,1)S(1)}, bf16[2048,320]{0,1:T(8,128)(2,1)}, u32[]{:S(2)}) copy-start(bf16[2048,320]{0,1:T(8,128)(2,1)} %param.9) | copy-start | bytes 3932164
  1.8 7.2 %collective-permute-start = (bf16[320,256]{1,0:T(8,128)(2,1)S(1)}, bf16[320,256]{1,0:T(8,128)(2,1)S(1)}, u32[]{:S(2)}, u32[]{:S(2)}) collective-permute-start(bf16[320,256]{1,0:T(8,128)(2,1)S(1)} %get-tuple-element.60), channel_id=1, source_target_pairs={{0,4},{4,0},{8,12},{12,8},{16,20},{20,16},{24,28},{28,24},{1,5},{5... | collective-permute-start | bytes 491528 | tf_op jit(solution)/shard_map/ppermute | solution.py:184
  6.0 4.9 %copy-start.7 = (bf16[1,128,2560]{2,1,0:T(8,128)(2,1)S(1)}, bf16[1,128,2560]{2,1,0:T(8,128)(2,1)}, u32[]{:S(2)}) copy-start(bf16[1,128,2560]{2,1,0:T(8,128)(2,1)} %param.7) | copy-start | bytes 1966084
  6.0 4.9 %copy-start.9 = (bf16[1,128,2560]{2,1,0:T(8,128)(2,1)S(1)}, bf16[1,128,2560]{2,1,0:T(8,128)(2,1)}, u32[]{:S(2)}) copy-start(bf16[1,128,2560]{2,1,0:T(8,128)(2,1)} %param.8) | copy-start | bytes 1966084
  6.0 4.9 %copy-start.13 = (s32[1,128]{1,0:T(1,128)S(1)}, s32[1,128]{1,0:T(1,128)}, u32[]{:S(2)}) copy-start(s32[1,128]{1,0:T(1,128)} %param.12) | copy-start | bytes 1540
  9.1 9.0 %collective-permute-start.1 = (bf16[640,256]{1,0:T(8,128)(2,1)S(1)}, bf16[640,256]{1,0:T(8,128)(2,1)S(1)}, u32[]{:S(2)}, u32[]{:S(2)}) collective-permute-start(bf16[640,256]{1,0:T(8,128)(2,1)S(1)} %join_rows.2.upper), channel_id=1, source_target_pairs={{0,8},{4,12},{8,0},{12,4},{16,24},{20,28},{24,16},{28,20},{1,9},{5... | collective-permute-start | bytes 983048 | tf_op jit(solution)/shard_map/ppermute | solution.py:181
  12.4 11.9 %collective-permute-start.2 = (bf16[320,768]{1,0:T(8,128)(2,1)S(1)}, bf16[320,768]{1,0:T(8,128)(2,1)S(1)}, u32[]{:S(2)}, u32[]{:S(2)}) collective-permute-start(bf16[320,768]{1,0:T(8,128)(2,1)S(1)} %get-tuple-element.26), channel_id=1, source_target_pairs={{0,4},{4,0},{8,12},{12,8},{16,20},{20,16},{24,28},{28,24},{1,5},{5... | collective-permute-start | bytes 1474568 | tf_op jit(solution)/shard_map/ppermute | solution.py:184
  24.3 5.0 %collective-permute-start.7 = (f32[3,1280]{1,0:T(4,128)S(1)}, f32[3,1280]{1,0:T(4,128)S(1)}, u32[]{:S(2)}, u32[]{:S(2)}) collective-permute-start(f32[3,1280]{1,0:T(4,128)S(1)} %slice_select_fusion), channel_id=1, source_target_pairs={{0,2},{1,3},{2,0},{3,1},{4,6},{5,7},{6,4},{7,5},{8,10},{9,11},{10,... | collective-permute-start | bytes 46088 | tf_op jit(solution)/shard_map/ppermute | solution.py:50
  25.9 21.2 %collective-permute-start.4 = (bf16[640,768]{1,0:T(8,128)(2,1)S(1)}, bf16[640,768]{1,0:T(8,128)(2,1)S(1)}, u32[]{:S(2)}, u32[]{:S(2)}) collective-permute-start(bf16[640,768]{1,0:T(8,128)(2,1)S(1)} %join_rows.3.upper), channel_id=1, source_target_pairs={{0,8},{4,12},{8,0},{12,4},{16,24},{20,28},{24,16},{28,20},{1,9},{5... | collective-permute-start | bytes 2949128 | tf_op jit(solution)/shard_map/ppermute | solution.py:181
  26.5 13.9 %collective-permute-start.6 = (bf16[128,2560]{1,0:T(8,128)(2,1)S(1)}, bf16[128,2560]{1,0:T(8,128)(2,1)S(1)}, u32[]{:S(2)}, u32[]{:S(2)}) collective-permute-start(bf16[128,2560]{1,0:T(8,128)(2,1)S(1)} %get-tuple-element.27.refs_0_), channel_id=1, source_target_pairs={{0,4},{4,0},{8,12},{12,8},{16,20},{20,16},{24,28},{28,24},{1,5},{5... | collective-permute-start | bytes 1966088 | tf_op jit(solution)/shard_map/ppermute | solution.py:184
  28.1 13.8 %collective-permute-start.3 = (bf16[128,2560]{1,0:T(8,128)(2,1)S(1)}, bf16[128,2560]{1,0:T(8,128)(2,1)S(1)}, u32[]{:S(2)}, u32[]{:S(2)}) collective-permute-start(bf16[128,2560]{1,0:T(8,128)(2,1)S(1)} %get-tuple-element.27.refs_0_), channel_id=1, source_target_pairs={{0,2},{1,3},{2,0},{3,1},{4,6},{5,7},{6,4},{7,5},{8,10},{9,11},{10,... | collective-permute-start | bytes 1966088 | tf_op jit(solution)/shard_map/ppermute | solution.py:187
  28.7 13.2 %collective-permute-start.5 = (bf16[1280,256]{1,0:T(8,128)(2,1)S(1)}, bf16[1280,256]{1,0:T(8,128)(2,1)S(1)}, u32[]{:S(2)}, u32[]{:S(2)}) collective-permute-start(bf16[1280,256]{1,0:T(8,128)(2,1)S(1)} %stack_rows.4), channel_id=1, source_target_pairs={{8,16},{12,20},{16,8},{20,12},{9,17},{13,21},{17,9},{21,13},{10,18... | collective-permute-start | bytes 1966088 | tf_op jit(solution)/shard_map/ppermute | solution.py:181
  47.1 13.2 %collective-permute-start.12 = (bf16[128,2560]{1,0:T(8,128)(2,1)S(1)}, bf16[128,2560]{1,0:T(8,128)(2,1)S(1)}, u32[]{:S(2)}, u32[]{:S(2)}) collective-permute-start(bf16[128,2560]{1,0:T(8,128)(2,1)S(1)} %collective-permute-done.6.refs_0_), channel_id=1, source_target_pairs={{0,2},{1,3},{2,0},{3,1},{4,6},{5,7},{6,4},{7,5},{8,10},{9,11},{10,... | collective-permute-start | bytes 1966088 | tf_op jit(solution)/shard_map/ppermute | solution.py:187
  47.6 1.2 copy-start.14
  47.7 3.3 %collective-permute-start.9 = (f32[3,640]{1,0:T(4,128)S(1)}, f32[3,640]{1,0:T(4,128)S(1)}, u32[]{:S(2)}, u32[]{:S(2)}) collective-permute-start(f32[3,640]{1,0:T(4,128)S(1)} %slice_select_fusion.1), channel_id=1, source_target_pairs={{0,1},{1,0},{2,3},{3,2},{4,5},{5,4},{6,7},{7,6},{8,9},{9,8},{10,11... | collective-permute-start | bytes 23048 | tf_op jit(solution)/shard_map/ppermute | solution.py:50
  47.8 22.2 %collective-permute-start.8 = (bf16[2,128,2560]{2,1,0:T(8,128)(2,1)S(1)}, bf16[2,128,2560]{2,1,0:T(8,128)(2,1)S(1)}, u32[]{:S(2)}, u32[]{:S(2)}) collective-permute-start(bf16[2,128,2560]{2,1,0:T(8,128)(2,1)S(1)} %pad_maximum_fusion), channel_id=1, source_target_pairs={{0,1},{1,0},{2,3},{3,2},{4,5},{5,4},{6,7},{7,6},{8,9},{9,8},{10,11... | collective-permute-start | bytes 3932168 | tf_op jit(solution)/shard_map/ppermute | solution.py:187
  48.9 21.1 %collective-permute-start.11 = (bf16[1280,256]{1,0:T(8,128)(2,1)S(1)}, bf16[1280,256]{1,0:T(8,128)(2,1)S(1)}, u32[]{:S(2)}, u32[]{:S(2)}) collective-permute-start(bf16[1280,256]{1,0:T(8,128)(2,1)S(1)} %stack_rows.5), channel_id=1, source_target_pairs={{8,16},{12,20},{16,8},{20,12},{9,17},{13,21},{17,9},{21,13},{10,18... | collective-permute-start | bytes 1966088 | tf_op jit(solution)/shard_map/ppermute | solution.py:181
  49.6 20.3 %collective-permute-start.10 = (bf16[1280,256]{1,0:T(8,128)(2,1)S(1)}, bf16[1280,256]{1,0:T(8,128)(2,1)S(1)}, u32[]{:S(2)}, u32[]{:S(2)}) collective-permute-start(bf16[1280,256]{1,0:T(8,128)(2,1)S(1)} %collective-permute-done.5), channel_id=1, source_target_pairs={{8,0},{12,4},{16,24},{20,28},{9,1},{13,5},{17,25},{21,29},{10,2},{... | collective-permute-start | bytes 1966088 | tf_op jit(solution)/shard_map/ppermute | solution.py:181
  51.0 43.1 %copy-start.2 = (bf16[1280,256]{1,0:T(8,128)(2,1)}, bf16[1280,256]{1,0:T(8,128)(2,1)S(1)}, u32[]{:S(2)}) copy-start(bf16[1280,256]{1,0:T(8,128)(2,1)S(1)} %stack_rows.7) | copy-start | bytes 1966084
  70.0 4.7 %collective-permute-start.13 = (f32[1,4,640]{2,1,0:T(4,128)S(1)}, f32[1,4,640]{2,1,0:T(4,128)S(1)}, u32[]{:S(2)}, u32[]{:S(2)}) collective-permute-start(f32[1,4,640]{2,1,0:T(4,128)S(1)} %fusion.7), channel_id=1, source_target_pairs={{0,4},{4,0},{8,12},{12,8},{16,20},{20,16},{24,28},{28,24},{1,5},{5... | collective-permute-start | bytes 30728 | tf_op jit(solution)/shard_map/ppermute | solution.py:61
  71.6 17.5 %collective-permute-start.14 = (bf16[1280,256]{1,0:T(8,128)(2,1)S(1)}, bf16[1280,256]{1,0:T(8,128)(2,1)S(1)}, u32[]{:S(2)}, u32[]{:S(2)}) collective-permute-start(bf16[1280,256]{1,0:T(8,128)(2,1)S(1)} %collective-permute-done.11), channel_id=1, source_target_pairs={{8,0},{12,4},{16,24},{20,28},{9,1},{13,5},{17,25},{21,29},{10,2},{... | collective-permute-start | bytes 1966088 | tf_op jit(solution)/shard_map/ppermute | solution.py:181
  72.9 16.3 %collective-permute-start.15 = (bf16[1280,256]{1,0:T(8,128)(2,1)S(1)}, bf16[1280,256]{1,0:T(8,128)(2,1)S(1)}, u32[]{:S(2)}, u32[]{:S(2)}) collective-permute-start(bf16[1280,256]{1,0:T(8,128)(2,1)S(1)} %stack_rows.6), channel_id=1, source_target_pairs={{8,16},{12,20},{16,8},{20,12},{9,17},{13,21},{17,9},{21,13},{10,18... | collective-permute-start | bytes 1966088 | tf_op jit(solution)/shard_map/ppermute | solution.py:181
  73.6 15.6 %collective-permute-start.16 = (bf16[2,128,2560]{2,1,0:T(8,128)(2,1)S(1)}, bf16[2,128,2560]{2,1,0:T(8,128)(2,1)S(1)}, u32[]{:S(2)}, u32[]{:S(2)}) collective-permute-start(bf16[2,128,2560]{2,1,0:T(8,128)(2,1)S(1)} %pad_maximum_fusion.1), channel_id=1, source_target_pairs={{0,1},{1,0},{2,3},{3,2},{4,5},{5,4},{6,7},{7,6},{8,9},{9,8},{10,11... | collective-permute-start | bytes 3932168 | tf_op jit(solution)/shard_map/ppermute | solution.py:187
  74.7 42.5 %copy-start.11 = (f32[1,4,640]{2,1,0:T(4,128)}, f32[1,4,640]{2,1,0:T(4,128)S(1)}, u32[]{:S(2)}) copy-start(f32[1,4,640]{2,1,0:T(4,128)S(1)} %collective-permute-done.13) | copy-start | bytes 30724
  89.2 7.4 %collective-permute-start.17 = (f32[2,4,640]{2,1,0:T(4,128)S(1)}, f32[2,4,640]{2,1,0:T(4,128)S(1)}, u32[]{:S(2)}, u32[]{:S(2)}) collective-permute-start(f32[2,4,640]{2,1,0:T(4,128)S(1)} %pad_maximum_fusion.19), channel_id=1, source_target_pairs={{0,8},{4,12},{8,0},{12,4},{16,24},{20,28},{24,16},{28,20},{1,9},{5... | collective-permute-start | bytes 61448 | tf_op jit(solution)/shard_map/ppermute | solution.py:61
  92.8 16.0 %collective-permute-start.18 = (bf16[1280,256]{1,0:T(8,128)(2,1)S(1)}, bf16[1280,256]{1,0:T(8,128)(2,1)S(1)}, u32[]{:S(2)}, u32[]{:S(2)}) collective-permute-start(bf16[1280,256]{1,0:T(8,128)(2,1)S(1)} %collective-permute-done.15), channel_id=1, source_target_pairs={{8,0},{12,4},{16,24},{20,28},{9,1},{13,5},{17,25},{21,29},{10,2},{... | collective-permute-start | bytes 1966088 | tf_op jit(solution)/shard_map/ppermute | solution.py:181
  94.1 16.3 %collective-permute-start.19 = (bf16[1280,256]{1,0:T(8,128)(2,1)S(1)}, bf16[1280,256]{1,0:T(8,128)(2,1)}, u32[]{:S(2)}, u32[]{:S(2)}) collective-permute-start(bf16[1280,256]{1,0:T(8,128)(2,1)S(1)} %stack_rows.7), channel_id=1, source_target_pairs={{8,16},{12,20},{16,8},{20,12},{9,17},{13,21},{17,9},{21,13},{10,18... | collective-permute-start | bytes 1966088 | tf_op jit(solution)/shard_map/ppermute | solution.py:181
  96.6 18.6 %copy-start.1 = (bf16[512,2560]{1,0:T(8,128)(2,1)}, bf16[512,2560]{1,0:T(8,128)(2,1)S(1)}, u32[]{:S(2)}) copy-start(bf16[512,2560]{1,0:T(8,128)(2,1)S(1)} %order_pieces.3) | copy-start | bytes 7864324
  96.6 20.6 %copy-start.10 = (f32[2,4,640]{2,1,0:T(4,128)}, f32[2,4,640]{2,1,0:T(4,128)S(1)}, u32[]{:S(2)}) copy-start(f32[2,4,640]{2,1,0:T(4,128)S(1)} %collective-permute-done.17) | copy-start | bytes 61444
  98.2 35.6 %collective-permute-start.21 = (bf16[512,256]{1,0:T(8,128)(2,1)}, bf16[512,256]{1,0:T(8,128)(2,1)S(1)}, u32[]{:S(2)}, u32[]{:S(2)}) collective-permute-start(bf16[512,256]{1,0:T(8,128)(2,1)} %convolution_convert_fusion.4), channel_id=1, source_target_pairs={{0,4},{4,0},{8,12},{12,8},{16,20},{20,16},{24,28},{28,24},{1,5},{5... | collective-permute-start | bytes 786440 | tf_op jit(solution)/shard_map/ppermute | solution.py:184
  100.3 33.5 %collective-permute-start.22 = (bf16[512,256]{1,0:T(8,128)(2,1)}, bf16[512,256]{1,0:T(8,128)(2,1)}, u32[]{:S(2)}, u32[]{:S(2)}) collective-permute-start(bf16[512,256]{1,0:T(8,128)(2,1)} %convolution_convert_fusion.3), channel_id=1, source_target_pairs={{0,4},{4,0},{8,12},{12,8},{16,20},{20,16},{24,28},{28,24},{1,5},{5... | collective-permute-start | bytes 786440 | tf_op jit(solution)/shard_map/ppermute | solution.py:184
  110.4 6.8 %collective-permute-start.25 = (f32[4,4,640]{2,1,0:T(4,128)S(1)}, f32[4,4,640]{2,1,0:T(4,128)S(1)}, u32[]{:S(2)}, u32[]{:S(2)}) collective-permute-start(f32[4,4,640]{2,1,0:T(4,128)S(1)} %pad_maximum_fusion.18), channel_id=1, source_target_pairs={{0,16},{4,20},{8,24},{12,28},{16,0},{20,4},{24,8},{28,12},{1,17},{... | collective-permute-start | bytes 122888 | tf_op jit(solution)/shard_map/ppermute | solution.py:61
  113.9 14.7 %collective-permute-start.20 = (bf16[1280,256]{1,0:T(8,128)(2,1)}, bf16[1280,256]{1,0:T(8,128)(2,1)}, u32[]{:S(2)}, u32[]{:S(2)}) collective-permute-start(bf16[1280,256]{1,0:T(8,128)(2,1)} %collective-permute-done.19), channel_id=1, source_target_pairs={{8,0},{12,4},{16,24},{20,28},{9,1},{13,5},{17,25},{21,29},{10,2},{... | collective-permute-start | bytes 1966088 | tf_op jit(solution)/shard_map/ppermute | solution.py:181
  116.7 17.1 %collective-permute-start.23 = (bf16[512,256]{1,0:T(8,128)(2,1)}, bf16[512,256]{1,0:T(8,128)(2,1)}, u32[]{:S(2)}, u32[]{:S(2)}) collective-permute-start(bf16[512,256]{1,0:T(8,128)(2,1)} %convolution_convert_fusion.1), channel_id=1, source_target_pairs={{0,4},{4,0},{8,12},{12,8},{16,20},{20,16},{24,28},{28,24},{1,5},{5... | collective-permute-start | bytes 786440 | tf_op jit(solution)/shard_map/ppermute | solution.py:184
  117.2 0.6 copy-start.12
  121.4 8.3 %copy-start.3 = (bf16[1280,256]{1,0:T(8,128)(2,1)S(1)}, bf16[1280,256]{1,0:T(8,128)(2,1)}, u32[]{:S(2)}) copy-start(bf16[1280,256]{1,0:T(8,128)(2,1)} %copy-done.2) | copy-start | bytes 1966084
  132.3 6.5 %copy-start.4 = (bf16[512,256]{1,0:T(8,128)(2,1)S(1)}, bf16[512,256]{1,0:T(8,128)(2,1)}, u32[]{:S(2)}) copy-start(bf16[512,256]{1,0:T(8,128)(2,1)} %convolution_convert_fusion.7.refs_0_) | copy-start | bytes 786436
  132.3 6.5 %copy-start.5 = (bf16[512,256]{1,0:T(8,128)(2,1)S(1)}, bf16[512,256]{1,0:T(8,128)(2,1)}, u32[]{:S(2)}) copy-start(bf16[512,256]{1,0:T(8,128)(2,1)} %convolution_convert_fusion.6.refs_1_) | copy-start | bytes 786436
  132.4 6.5 %copy-start.6 = (bf16[512,256]{1,0:T(8,128)(2,1)S(1)}, bf16[512,256]{1,0:T(8,128)(2,1)}, u32[]{:S(2)}) copy-start(bf16[512,256]{1,0:T(8,128)(2,1)} %convolution_convert_fusion.5.refs_2_) | copy-start | bytes 786436
  132.4 6.4 %collective-permute-start.24 = (bf16[512,256]{1,0:T(8,128)(2,1)S(1)}, bf16[512,256]{1,0:T(8,128)(2,1)S(1)}, u32[]{:S(2)}, u32[]{:S(2)}) collective-permute-start(bf16[512,256]{1,0:T(8,128)(2,1)S(1)} %convolution_convert_fusion), channel_id=1, source_target_pairs={{0,4},{4,0},{8,12},{12,8},{16,20},{20,16},{24,28},{28,24},{1,5},{5... | collective-permute-start | bytes 786440 | tf_op jit(solution)/shard_map/ppermute | solution.py:184

commit v2 on v0

v2 whole, which is shorter than its diff:
```python
import jax
import jax.numpy as jnp
from jax import lax
from jax.experimental import pallas as pl
from jax.experimental.pallas import tpu as pltpu
from jax.sharding import PartitionSpec as P

HIGHEST = lax.Precision.HIGHEST
CHUNKS = 4
BLOCKS = 2


def onehot(values, count):
    return (values[:, None] == jnp.arange(count, dtype=jnp.int32)[None, :]).astype(jnp.float32)


def gated(grad_out, mod_gate, level_table, frame_ids, levels):
    marks = onehot(levels[0], level_table.shape[0])
    gate_frames = mod_gate[None, :] + jnp.dot(marks, level_table, precision=HIGHEST)
    frames = onehot(frame_ids[0], levels.shape[1])
    gate_tokens = jnp.dot(frames, gate_frames, precision=HIGHEST)
    return (gate_tokens * grad_out[0].astype(jnp.float32)).astype(jnp.bfloat16)


def frame_sums(grad_out, branch_out, frame_ids, levels):
    products = grad_out[0].astype(jnp.float32) * branch_out[0].astype(jnp.float32)
    return jnp.dot(onehot(frame_ids[0], levels.shape[1]).T, products, precision=HIGHEST)


def plain_body(grad_out, branch_out, down_weight, mod_gate, level_table, frame_ids, levels):
    scaled = gated(grad_out, mod_gate, level_table, frame_ids, levels)
    frame_part = frame_sums(grad_out, branch_out, frame_ids, levels)
    hidden_grad = lax.dot_general(
        lax.all_gather(scaled, "seq", axis=0, tiled=True),
        lax.all_gather(down_weight, "dp", axis=1, tiled=True),
        (((1,), (1,)), ((), ())),
        preferred_element_type=jnp.float32,
    ).astype(jnp.bfloat16)
    frame_grad = lax.psum_scatter(frame_part, "seq", scatter_dimension=1, tiled=True)
    marks = onehot(levels[0], level_table.shape[0])
    level_part = jnp.dot(marks.T, frame_grad, precision=HIGHEST)
    table_grad = lax.psum_scatter(level_part, "dp", scatter_dimension=0, tiled=True)
    return hidden_grad[None], frame_grad[None], table_grad


def split_terms(values):
    terms = []
    for _ in range(3):
        term = lax.reduce_precision(values, exponent_bits=8, mantissa_bits=7)
        terms.append(term.astype(jnp.bfloat16))
        values = values - term
    return terms


def with_frame_lines(tokens, frame_part, levels, seq):
    frame_count, width = frame_part.shape
    level_line = jnp.pad(levels.astype(jnp.bfloat16), ((0, 0), (0, width // seq - frame_count)))
    level_line = jnp.tile(level_line, (1, seq))
    lines = jnp.concatenate([*split_terms(frame_part), level_line], axis=0)
    lines = jnp.pad(lines, ((0, -lines.shape[0] % 16), (0, 0)))
    return jnp.concatenate([tokens, lines], axis=0)


def frames_of(me, rows, frame_count, width, pieces):
    lines = pieces[0][0].shape[0] - rows
    any_space = pl.BlockSpec(memory_space=pl.ANY)

    def kernel(place, *refs):
        result, held, sems = refs[8], refs[9], refs[10]
        below = pl.ds(rows, lines)
        columns = pl.ds(pl.multiple_of(place[0] * width, 128), width)
        copies = []
        for ref, (_, index) in zip(refs, pieces):
            source = ref if index is None else ref.at[index]
            copies.append(
                pltpu.make_async_copy(
                    source.at[below, columns], held.at[len(copies)], sems.at[len(copies)]
                )
            )
            copies[-1].start()
        for copy in copies:
            copy.wait()
        for clip in range(2):
            total = jnp.zeros((lines, width), jnp.float32)
            for index in range(4):
                total = total + held[4 * clip + index].astype(jnp.float32)
            sums = total[:frame_count]
            for term in (1, 2):
                sums = sums + total[term * frame_count : (term + 1) * frame_count]
            result[clip, :frame_count] = sums
            marks = held[4 * clip].astype(jnp.float32)
            result[clip, frame_count:] = marks[3 * frame_count : 3 * frame_count + 1]

    return pl.pallas_call(
        kernel,
        out_shape=jax.ShapeDtypeStruct((2, frame_count + 1, width), jnp.float32),
        in_specs=[pl.BlockSpec(memory_space=pltpu.SMEM)] + [any_space] * 8,
        out_specs=pl.BlockSpec(memory_space=pltpu.VMEM),
        scratch_shapes=[
            pltpu.VMEM((8, lines, width), jnp.bfloat16),
            pltpu.SemaphoreType.DMA((8,)),
        ],
        name="frame_lines",
    )(me.astype(jnp.int32).reshape(1), *[array for array, _ in pieces])


def clip_step(packed, dp, flip, gate):
    sent = after(packed, *gate)
    arrived = lax.ppermute(sent, "dp", [(i, i ^ flip) for i in range(dp)])
    return jnp.concatenate([packed, arrived], axis=0)


def table_of(packed, level_count):
    dp, lines, width = packed.shape
    frame_count = lines - 1
    owned = level_count // dp
    rows = (lax.axis_index("dp") * owned + jnp.arange(owned, dtype=jnp.int32)).astype(jnp.float32)
    sums = packed[:, :frame_count].reshape(dp * frame_count, width)
    marks = packed[:, frame_count, :frame_count].reshape(dp * frame_count)
    owners = (rows[:, None] == marks[None, :]).astype(jnp.float32)
    return jnp.dot(owners, sums, precision=HIGHEST)


def after(array, *earlier):
    return lax.optimization_barrier((array, *earlier))[0]


def slice_rows(upper, lower, count):
    rows, columns = upper.shape
    width = columns // count
    vmem = pl.BlockSpec(memory_space=pltpu.VMEM)

    def kernel(upper, lower, *results):
        for index, result in enumerate(results):
            chunk = pl.ds(index * width, width)
            result[:rows] = upper[:, chunk]
            result[rows:] = lower[:, chunk]

    return pl.pallas_call(
        kernel,
        out_shape=[jax.ShapeDtypeStruct((2 * rows, width), upper.dtype)] * count,
        in_specs=[vmem, vmem],
        out_specs=[vmem] * count,
        compiler_params=pltpu.CompilerParams(vmem_limit_bytes=16 << 20),
        name="slice_rows",
    )(upper, lower)


def gather_rows(y, is_mid, start, width, own, near, crossed, forwarded, last, offset):
    rows = own[0].shape[0]
    vmem = pl.BlockSpec(memory_space=pltpu.VMEM)
    parts = [*own, *near, *crossed[0], *crossed[1], *forwarded]

    def kernel(place, *refs):
        result = refs[len(parts) + 1]
        first = pl.multiple_of(place[0] * rows, 16)
        second = pl.multiple_of((1 - place[0]) * rows, 16)
        chunk = pl.ds(start, width)

        def put(block, index):
            base = 2 * rows * block
            result[pl.ds(pl.multiple_of(base + first, 16), rows), :] = refs[index][:, chunk]
            result[pl.ds(pl.multiple_of(base + second, 16), rows), :] = refs[index + 1][:, chunk]

        put(0, 0)
        put(1, 2)

        @pl.when(place[1] == 1)
        def _():
            put(2, 4)
            put(3, 6)

        @pl.when(place[1] == 0)
        def _():
            put(2, 8)
            final = refs[len(parts)]
            inner = pl.ds(offset, width)
            base = 6 * rows
            result[pl.ds(pl.multiple_of(base + first, 16), rows), :] = final[:rows, inner]
            result[pl.ds(pl.multiple_of(base + second, 16), rows), :] = final[rows:, inner]

    return pl.pallas_call(
        kernel,
        out_shape=jax.ShapeDtypeStruct((8 * rows, width), last.dtype),
        in_specs=[pl.BlockSpec(memory_space=pltpu.SMEM)] + [vmem] * (len(parts) + 1),
        out_specs=vmem,
        compiler_params=pltpu.CompilerParams(vmem_limit_bytes=24 << 20),
        name="gather_rows",
    )(jnp.stack([y, is_mid.astype(jnp.int32)]).astype(jnp.int32), *parts, last)


def order_pieces(me, rows, pieces):
    count, width = 4, pieces[0][0].shape[1]
    any_space = pl.BlockSpec(memory_space=pl.ANY)

    def kernel(place, *refs):
        result, sems = refs[count], refs[count + 1]
        sources = [
            ref if index is None else ref.at[index] for ref, (_, index) in zip(refs, pieces)
        ]
        copies = []
        for flip in range(count):
            start = pl.multiple_of((place[0] ^ flip) * rows, 128)
            source = sources[flip].at[pl.ds(0, rows)]
            copies.append(
                pltpu.make_async_copy(source, result.at[pl.ds(start, rows)], sems.at[flip])
            )
            copies[-1].start()
        for copy in copies:
            copy.wait()

    return pl.pallas_call(
        kernel,
        out_shape=jax.ShapeDtypeStruct((count * rows, width), pieces[0][0].dtype),
        in_specs=[pl.BlockSpec(memory_space=pltpu.SMEM)] + [any_space] * count,
        out_specs=pl.BlockSpec(memory_space=pltpu.VMEM),
        scratch_shapes=[pltpu.SemaphoreType.DMA((count,))],
        compiler_params=pltpu.CompilerParams(vmem_limit_bytes=16 << 20),
        name="order_pieces",
    )(me.astype(jnp.int32).reshape(1), *[array for array, _ in pieces])


def place_columns(y, half, starts, kept, received, earlier=None):
    count, rows = len(kept), kept[0].shape[0]
    vmem = pl.BlockSpec(memory_space=pltpu.VMEM)
    any_space = pl.BlockSpec(memory_space=pl.ANY)
    held = [] if earlier is None else [earlier]

    def kernel(place, *refs):
        result, sems = refs[2 * count + len(held)], refs[2 * count + len(held) + 1]
        copies = []
        for index, start in enumerate(starts):
            for side, first in ((0, place[0] * half), (1, (1 - place[0]) * half)):
                source = refs[side * count + index]
                column = pl.multiple_of(first + start, 128)
                target = result.at[:, pl.ds(column, source.shape[1])]
                copies.append(
                    pltpu.make_async_copy(source, target, sems.at[2 * index + side])
                )
                copies[-1].start()
        for copy in copies:
            copy.wait()

    return pl.pallas_call(
        kernel,
        out_shape=jax.ShapeDtypeStruct((rows, 2 * half), kept[0].dtype),
        in_specs=[pl.BlockSpec(memory_space=pltpu.SMEM)]
        + [vmem] * (2 * count)
        + [any_space] * len(held),
        out_specs=any_space,
        input_output_aliases={2 * count + 1: 0} if held else {},
        scratch_shapes=[pltpu.SemaphoreType.DMA((2 * count,))],
        compiler_params=pltpu.CompilerParams(vmem_limit_bytes=16 << 20),
        name="place_columns",
    )(y.astype(jnp.int32).reshape(1), *kept, *received, *held)


def staged_body(grad_out, branch_out, down_weight, mod_gate, level_table, frame_ids, levels):
    dp, seq = 8, 4
    clip, me = lax.axis_index("dp"), lax.axis_index("seq")
    z, y = clip // 2, clip % 2
    is_mid = jnp.logical_or(z == 1, z == 2)
    hidden, shard = down_weight.shape
    half = hidden // 2
    block = 2 * shard

    def along_z(array, pairs):
        perm = [(a * 2 + s, b * 2 + s) for a, b in pairs for s in range(2)]
        return lax.ppermute(array, "dp", perm)

    def over_y(array):
        return lax.ppermute(array, "dp", [(i, i ^ 1) for i in range(dp)])

    def over_seq(array, flip):
        return lax.ppermute(array, "seq", [(i, i ^ flip) for i in range(seq)])

    def ordered(flag, first, second, axis):
        swapped = jnp.concatenate([second, first], axis=axis)
        return jnp.where(flag, swapped, jnp.concatenate([first, second], axis=axis))

    weight = down_weight.T
    width = half // CHUNKS
    own_p = lax.dynamic_slice(weight, (0, y * half), (shard, half))
    sent = lax.dynamic_slice(weight, (0, (1 - y) * half), (shard, half))

    scaled = gated(grad_out, mod_gate, level_table, frame_ids, levels)
    frame_part = frame_sums(grad_out, branch_out, frame_ids, levels)
    order = [z, z ^ 1, jnp.where(is_mid, z ^ 3, z ^ 2), jnp.where(is_mid, z ^ 2, z ^ 3)]
    piece = scaled.shape[0]
    scaled = jnp.concatenate(
        [lax.dynamic_slice(scaled, (0, owner * block), (piece, block)) for owner in order], axis=1
    )
    tokens = with_frame_lines(scaled, frame_part, levels, seq)
    def to_near(own):
        return along_z(own, [(0, 1), (1, 0), (2, 3), (3, 2)])

    def across(block):
        return along_z(block, [(1, 2), (2, 1)])

    def outward(block):
        return along_z(block, [(1, 0), (2, 3)])

    own_q = over_y(sent)
    near_p = to_near(own_p)
    crossed_p = across(own_p)

    gate = (own_q, near_p, crossed_p)
    mine_x = over_seq(after(tokens, *gate), 2)
    theirs = over_y(after(tokens, *gate))
    near_q = to_near(after(own_q, *gate))
    crossed_q = across(after(own_q, *gate))
    crossed_near_p = across(after(near_p, *gate))
    forwarded_p = outward(after(crossed_p, *gate, mine_x))

    gate = (near_q, crossed_q, crossed_near_p, forwarded_p)
    theirs_x = over_seq(after(theirs, *gate), 2)
    three_core = over_seq(after(jnp.stack([tokens, mine_x, theirs]), *gate), 1)
    crossed_near_q = across(after(near_q, *gate))
    forwarded_q = outward(after(crossed_q, *gate))

    gate = (crossed_near_q, forwarded_q, three_core, theirs_x)
    theirs_x_core = over_seq(after(theirs_x, *gate), 1)
    clips = (
        ((tokens, None), (three_core, 0), (mine_x, None), (three_core, 1)),
        ((theirs, None), (three_core, 2), (theirs_x, None), (theirs_x_core, None)),
    )
    mine, other = order_pieces(me, piece, clips[0]), order_pieces(me, piece, clips[1])
    frame_count = levels.shape[1]
    columns = shard * dp // seq
    packed = frames_of(me, piece, frame_count, columns, clips[0] + clips[1])
    frame_grad = packed[0, :frame_count]

    blocks = slice_rows(after(crossed_near_p, *gate), after(crossed_near_q, *gate), BLOCKS)
    last = [outward(block) for block in blocks]
    each = CHUNKS // BLOCKS
    kept, received, products = [], [], []
    firsts = [position * width for position in range(CHUNKS)]
    packed = clip_step(packed, dp, 2, (theirs_x_core,))
    packed = clip_step(packed, dp, 4, (last[0],))
    for index in range(CHUNKS):
        block, offset = last[index // each], index % each * width
        own = after(own_p, *products[: 2 * each]) if index >= each else own_p
        full = gather_rows(
            y,
            is_mid,
            index * width,
            width,
            (own, own_q),
            (near_p, near_q),
            ((crossed_p, crossed_q), (crossed_near_p, crossed_near_q)),
            (forwarded_p, forwarded_q),
            block,
            offset,
        )
        if index == CHUNKS - 1:
            result = place_columns(y, half, firsts[:2], kept[:2], received[:2])
            table_grad = table_of(packed, level_table.shape[0])
            full = after(full, result, table_grad)
        part = jnp.dot(other, full, preferred_element_type=jnp.float32).astype(jnp.bfloat16)
        received.append(over_y(part))
        kept.append(jnp.dot(mine, full, preferred_element_type=jnp.float32).astype(jnp.bfloat16))
        products += [part, kept[-1]]
    hidden_grad = place_columns(y, half, firsts[2:], kept[2:], received[2:], result)
    return hidden_grad[None], frame_grad[None], table_grad


def solution(mesh):
    staged = mesh.shape["dp"] == 8 and mesh.shape["seq"] == 4
    return jax.shard_map(
        staged_body if staged else plain_body,
        mesh=mesh,
        in_specs=(
            P("dp", "seq", None),
            P("dp", "seq", None),
            P("seq", "dp"),
            P(),
            P(),
            P("dp", "seq"),
            P("dp", None),
        ),
        out_specs=(P("dp", None, "seq"), P("dp", None, "seq"), P("dp", "seq")),
        check_vma=False,
    )
```

time: 311 us -> 145 us (0.47)
  waiting for transfers between devices: 275 us -> 69 us
  starting transfers between devices: 0.16 us -> 28.9 us
  Pallas kernels: 0 us -> 15.7 us
  between operations: 14.5 us -> 1.43 us
  local copies, waits for them, and re-layouts: 2.71 us -> 12.9 us
    all_gather x2 -> x0, waiting for transfers between devices: 179 us -> none  [the longest x1 153 us: body(): weight_full = lax.all_gather(down_weight, 'dp', axis=1, tiled=True)]
    unnamed x6 -> x0, waiting for transfers between devices: 96.3 us -> none
    ppermute x0 -> x22, waiting for transfers between devices: none -> 69 us  [the longest x10 44.9 us: along_z(): return lax.ppermute(array, 'dp', perm)]
    ppermute x0 -> x22, starting transfers between devices: none -> 28.9 us  [the longest x10 15.8 us: along_z(): return lax.ppermute(array, 'dp', perm)]
    pallas_call x0 -> x10, Pallas kernels: none -> 15.7 us  [the longest x4 6.27 us: gather_rows(): pl.pallas_call(kernel, out_shape=jax.ShapeDtypeStruct((8 * rows, width),...]
    unnamed x18 -> x105, local copies, waits for them, and re-layouts: 2.71 us -> 9.14 us
    unnamed x1 -> x0, matrix products: 3.68 us -> none
    dynamic_slice x0 -> x2, local copies, waits for them, and re-layouts: none -> 3.59 us  [the longest x1 2.38 us: staged_body(): own_p = lax.dynamic_slice(weight, (0, y * half), (shard, half))]
  transfers between devices with their start and end apart: 4 -> 22, of which waited for: 4 -> 8; matrix products, arithmetic and copies ran while one was open for 1% -> 13% of each run, Pallas kernels for 0% -> 9%
where the time goes in v2:
time: 145 us; the launch traced here: 144 us
  waiting for transfers between devices  69 us (48%)
  starting transfers between devices  28.9 us (20%)
  Pallas kernels  15.7 us (11%)
  matrix products  15.4 us (11%)
  local copies, waits for them, and re-layouts  12.9 us (9%)
    ppermute x10, waiting for transfers between devices, along_z(): return lax.ppermute(array, 'dp', perm)  44.9 us
    ppermute x10, starting transfers between devices, along_z(): return lax.ppermute(array, 'dp', perm)  15.8 us
    ppermute x6, waiting for transfers between devices, over_y(): return lax.ppermute(array, 'dp', [(i, i ^ 1) for i in range(dp)])  13.8 us
    ppermute x4, waiting for transfers between devices, over_seq(): return lax.ppermute(array, 'seq', [(i, i ^ flip) for i in range(seq)])  10.3 us
    unnamed x105, local copies, waits for them, and re-layouts  9.14 us
    ppermute x6, starting transfers between devices, over_y(): return lax.ppermute(array, 'dp', [(i, i ^ 1) for i in range(dp)])  7.33 us
    pallas_call x4, Pallas kernels, gather_rows(): pl.pallas_call(kernel, out_shape=jax.ShapeDtypeStruct((8 * rows, width),...  6.27 us
    dot_general x4, matrix products, staged_body(): jnp.dot(other, full, preferred_element_type=jnp.float32)  5.48 us
  transfers between devices with their start and end apart: 22, of which 8 were waited for; matrix products, arithmetic and copies ran while one was open for 13% of the time, Pallas kernels for 9%

profile of v2, /device:TPU:0, one launch (start us, length us, event | category | flops | bytes accessed | tf_op | source)
XLA Modules:
  0.0 143.8 jit_solution(1773163610885050142)
XLA Ops:
  0.7 2.4 %dynamic-slice_bitcast_fusion = (bf16[320,1024]{1,0:T(8,128)(2,1)S(1)}, bf16[320,1024]{1,0:T(8,128)(2,1)}) fusion(bf16[2048,320]{0,1:T(8,128)(2,1)} %param.9, s32[]{:T(128)S(6)} %select_n.44, s32[]{:T(128)S(6)} %select_n.43), kind=kLoop, calls=%fused_computation.18 | loop fusion | bytes 2621448 | tf_op jit(solution)/shard_map/dynamic_slice | solution.py:283
  3.1 0.7 collective-permute-start.2
  3.8 5.9 %collective-permute-start.1 = (bf16[320,1024]{1,0:T(8,128)(2,1)S(1)}, bf16[320,1024]{1,0:T(8,128)(2,1)S(1)}, u32[]{:S(2)}, u32[]{:S(2)}) collective-permute-start(bf16[320,1024]{1,0:T(8,128)(2,1)S(1)} %get-tuple-element.32.refs_0_), channel_id=1, source_target_pairs={{0,8},{4,12},{8,0},{12,4},{16,24},{20,28},{24,16},{28,20},{1,9},{5... | collective-permute-start | bytes 1966088 | tf_op jit(solution)/shard_map/ppermute | solution.py:269
  9.7 1.5 %collective-permute-start = (bf16[320,1024]{1,0:T(8,128)(2,1)}, bf16[320,1024]{1,0:T(8,128)(2,1)}, u32[]{:S(2)}, u32[]{:S(2)}) collective-permute-start(bf16[320,1024]{1,0:T(8,128)(2,1)} %get-tuple-element.44), channel_id=1, source_target_pairs={{0,4},{4,0},{8,12},{12,8},{16,20},{20,16},{24,28},{28,24},{1,5},{5... | collective-permute-start | bytes 1966088 | tf_op jit(solution)/shard_map/ppermute | solution.py:272
  11.3 0.3 convolution_add_fusion
  11.6 1.8 %reduce-precision_convert_fusion.1 = (bf16[3,2560]{1,0:T(4,128)(2,1)S(1)}, bf16[3,2560]{1,0:T(4,128)(2,1)S(1)}, bf16[3,2560]{1,0:T(4,128)(2,1)S(1)}) fusion(bf16[1,128,2560]{2,1,0:T(8,128)(2,1)} %param.8, bf16[1,128,2560]{2,1,0:T(8,128)(2,1)S(1)} %copy-done.46, s32[128]{0:T(128)S(1)} %bitcast.58), kind=kOutput, calls=%fused_computation.34 | convolution fusion | flops 12841344 | bytes 1357312 | tf_op jit(solution)/shard_map/dot_general | solution.py:27
  13.4 1.6 %fusion = bf16[128,2560]{1,0:T(8,128)(2,1)} fusion(f32[3,2560]{1,0:T(4,128)S(1)} %convolution_add_fusion, bf16[1,128,2560]{2,1,0:T(8,128)(2,1)S(1)} %copy-done.46, s32[128]{0:T(128)S(1)} %bitcast.59), kind=kOutput, calls=%fused_computation.1 | convolution fusion | flops 12779904 | bytes 1341952 | tf_op jit(solution)/shard_map/dot_general | solution.py:21
  15.0 1.2 constant_dynamic-slice_fusion.3
  16.2 0.1 fusion.11
  16.4 9.5 %collective-permute-done.refs_1_ = bf16[320,1024]{1,0:T(8,128)(2,1)} collective-permute-done((bf16[320,1024]{1,0:T(8,128)(2,1)}, bf16[320,1024]{1,0:T(8,128)(2,1)}, u32[]{:S(2)}, u32[]{:S(2)}) %collective-permute-start) | collective-permute-done | bytes 655392 | tf_op jit(solution)/shard_map/ppermute | solution.py:272
  25.9 1.6 %collective-permute-start.3 = (bf16[144,2560]{1,0:T(8,128)(2,1)S(1)}, bf16[144,2560]{1,0:T(8,128)(2,1)S(1)}, u32[]{:S(2)}, u32[]{:S(2)}) collective-permute-start(bf16[144,2560]{1,0:T(8,128)(2,1)S(1)} %pad_maximum_fusion.1.refs_0_), channel_id=1, source_target_pairs={{0,2},{1,3},{2,0},{3,1},{4,6},{5,7},{6,4},{7,5},{8,10},{9,11},{10,... | collective-permute-start | bytes 2211848 | tf_op jit(solution)/shard_map/ppermute | solution.py:275
  27.5 1.5 %collective-permute-start.4 = (bf16[144,2560]{1,0:T(8,128)(2,1)S(1)}, bf16[144,2560]{1,0:T(8,128)(2,1)S(1)}, u32[]{:S(2)}, u32[]{:S(2)}) collective-permute-start(bf16[144,2560]{1,0:T(8,128)(2,1)S(1)} %pad_maximum_fusion.1.refs_0_), channel_id=1, source_target_pairs={{0,4},{4,0},{8,12},{12,8},{16,20},{20,16},{24,28},{28,24},{1,5},{5... | collective-permute-start | bytes 2211848 | tf_op jit(solution)/shard_map/ppermute | solution.py:272
  29.0 0.7 collective-permute-start.6
  29.7 2.1 %collective-permute-start.5 = (bf16[320,1024]{1,0:T(8,128)(2,1)}, bf16[320,1024]{1,0:T(8,128)(2,1)S(1)}, u32[]{:S(2)}, u32[]{:S(2)}) collective-permute-start(bf16[320,1024]{1,0:T(8,128)(2,1)} %collective-permute-done.refs_1_), channel_id=1, source_target_pairs={{0,8},{4,12},{8,0},{12,4},{16,24},{20,28},{24,16},{28,20},{1,9},{5... | collective-permute-start | bytes 1966088 | tf_op jit(solution)/shard_map/ppermute | solution.py:269
  31.8 0.7 collective-permute-start.7
  32.5 10.3 %collective-permute-done.3.refs_2_ = bf16[144,2560]{1,0:T(8,128)(2,1)S(1)} collective-permute-done((bf16[144,2560]{1,0:T(8,128)(2,1)S(1)}, bf16[144,2560]{1,0:T(8,128)(2,1)S(1)}, u32[]{:S(2)}, u32[]{:S(2)}) %collective-permute-start.3) | collective-permute-done | bytes 737312 | tf_op jit(solution)/shard_map/ppermute | solution.py:275
  42.7 1.3 collective-permute-start.8
  44.1 0.2 pad_maximum_fusion
  44.4 0.3 collective-permute-done.5.refs_3_
  44.7 14.0 %collective-permute-done.8.refs_8_ = bf16[320,1024]{1,0:T(8,128)(2,1)S(1)} collective-permute-done((bf16[320,1024]{1,0:T(8,128)(2,1)S(1)}, bf16[320,1024]{1,0:T(8,128)(2,1)S(1)}, u32[]{:S(2)}, u32[]{:S(2)}) %collective-permute-start.8) | collective-permute-done | bytes 655392 | tf_op jit(solution)/shard_map/ppermute | solution.py:269
  58.7 0.8 copy-done.21
  59.6 1.4 collective-permute-start.10
  61.0 0.7 collective-permute-start.11
  61.7 0.8 copy-done.18
  62.5 1.3 collective-permute-start.12
  63.8 0.8 copy-done.15
  64.7 16.6 %collective-permute-done.12.refs_9_ = bf16[320,1024]{1,0:T(8,128)(2,1)S(1)} collective-permute-done((bf16[320,1024]{1,0:T(8,128)(2,1)S(1)}, bf16[320,1024]{1,0:T(8,128)(2,1)S(1)}, u32[]{:S(2)}, u32[]{:S(2)}) %collective-permute-start.12) | collective-permute-done | bytes 655392 | tf_op jit(solution)/shard_map/ppermute | solution.py:269
  81.3 0.8 copy-done.24
  82.1 1.0 slice_rows.1
  83.2 0.8 copy-done.3
  84.0 0.8 copy-done.45
  84.9 1.3 collective-permute-start.14
  86.2 0.1 pad_add_fusion.place
  86.3 1.3 collective-permute-start.15
  87.6 1.1 copy-done.30
  88.7 1.1 copy-done.32
  89.9 0.9 order_pieces.2
  90.8 13.9 %collective-permute-done.14.refs_10_ = bf16[640,512]{1,0:T(8,128)(2,1)} collective-permute-done((bf16[640,512]{1,0:T(8,128)(2,1)}, bf16[640,512]{1,0:T(8,128)(2,1)}, u32[]{:S(2)}, u32[]{:S(2)}) %collective-permute-start.14) | collective-permute-done | bytes 655392 | tf_op jit(solution)/shard_map/ppermute | solution.py:269
  104.8 1.5 %gather_rows.5 = bf16[2560,256]{1,0:T(8,128)(2,1)S(1)} custom-call(s32[2]{0:T(128)S(1)} %pad_add_fusion.place, bf16[320,1024]{1,0:T(8,128)(2,1)S(1)} %copy-done.7, bf16[320,1024]{1,0:T(8,128)(2,1)} %collective-permute-done.refs_1_, bf16[320,1024]{1,0:T(8,128)(2,1)S(1)} %copy-done.13, bf16[320,1024]{1,0:T(8,128)(2,1)S(1)} %copy-done.19, ...), custom_call_target="tpu_custom_call" | custom-call | tf_op jit(solution)/shard_map/gather_rows/pallas_call | solution.py:182
  106.2 1.9 %gather_rows.4 = bf16[2560,256]{1,0:T(8,128)(2,1)S(1)} custom-call(s32[2]{0:T(128)S(1)} %pad_add_fusion.place, bf16[320,1024]{1,0:T(8,128)(2,1)S(1)} %copy-done.7, bf16[320,1024]{1,0:T(8,128)(2,1)} %collective-permute-done.refs_1_, bf16[320,1024]{1,0:T(8,128)(2,1)S(1)} %copy-done.13, bf16[320,1024]{1,0:T(8,128)(2,1)S(1)} %copy-done.19, ...), custom_call_target="tpu_custom_call" | custom-call | tf_op jit(solution)/shard_map/gather_rows/pallas_call | solution.py:182
  108.2 1.5 %convolution_convert_fusion.4.refs_1_ = bf16[512,256]{1,0:T(8,128)(2,1)} fusion(bf16[512,2560]{1,0:T(8,128)(2,1)S(1)} %order_pieces.2, bf16[2560,256]{1,0:T(8,128)(2,1)S(1)} %gather_rows.5), kind=kOutput, calls=%fused_computation.11 | convolution fusion | flops 671219712 | bytes 4194304 | tf_op jit(solution)/shard_map/dot_general | solution.py:361
  109.7 1.5 %convolution_convert_fusion.6.refs_0_ = bf16[512,256]{1,0:T(8,128)(2,1)} fusion(bf16[512,2560]{1,0:T(8,128)(2,1)S(1)} %order_pieces.2, bf16[2560,256]{1,0:T(8,128)(2,1)S(1)} %gather_rows.4), kind=kOutput, calls=%fused_computation.13 | convolution fusion | flops 671219712 | bytes 4194304 | tf_op jit(solution)/shard_map/dot_general | solution.py:361
  111.3 1.7 %frame_lines.1 = f32[2,4,640]{2,1,0:T(4,128)} custom-call(s32[1]{0:T(128)} %bitcast.1.place, bf16[144,2560]{1,0:T(8,128)(2,1)} %copy-done.29, bf16[3,144,2560]{2,1,0:T(8,128)(2,1)} %copy-done.1, bf16[144,2560]{1,0:T(8,128)(2,1)} %copy-done.31, bf16[3,144,2560]{2,1,0:T(8,128)(2,1)} %copy-done.1, bf16[144,2560]{1,0:T(8,128)(2,1)} %copy-done.27, ...), custom_call_target="tpu_custom_call" | custom-call | tf_op jit(solution)/shard_map/frame_lines/pallas_call | solution.py:94
  113.1 1.1 copy-done.28
  114.2 1.7 %order_pieces.3 = bf16[512,2560]{1,0:T(8,128)(2,1)S(1)} custom-call(s32[1]{0:T(128)} %bitcast.1.place, bf16[144,2560]{1,0:T(8,128)(2,1)S(1)} %copy-done.28, bf16[3,144,2560]{2,1,0:T(8,128)(2,1)S(1)} %copy-done.2, bf16[144,2560]{1,0:T(8,128)(2,1)} %collective-permute-done.10.refs_2_.refs_6_, bf16[144,2560]{1,0:T(8,128)(2,1)} %collective-permute-done.13.refs_3_.refs_7_), custom_call_target="tpu_custom_call" | custom-call | tf_op jit(solution)/shard_map/order_pieces/pallas_call | solution.py:212
  116.0 1.6 %convolution_convert_fusion.5 = bf16[512,256]{1,0:T(8,128)(2,1)} fusion(bf16[512,2560]{1,0:T(8,128)(2,1)S(1)} %order_pieces.3, bf16[2560,256]{1,0:T(8,128)(2,1)S(1)} %copy-done.41), kind=kOutput, calls=%fused_computation.12 | convolution fusion | flops 671219712 | bytes 4194304 | tf_op jit(solution)/shard_map/dot_general | solution.py:359
  117.6 1.6 %collective-permute-start.17 = (bf16[512,256]{1,0:T(8,128)(2,1)}, bf16[512,256]{1,0:T(8,128)(2,1)S(1)}, u32[]{:S(2)}, u32[]{:S(2)}) collective-permute-start(bf16[512,256]{1,0:T(8,128)(2,1)} %convolution_convert_fusion.5), channel_id=1, source_target_pairs={{0,4},{4,0},{8,12},{12,8},{16,20},{20,16},{24,28},{28,24},{1,5},{5... | collective-permute-start | bytes 786440 | tf_op jit(solution)/shard_map/ppermute | solution.py:272
  119.2 1.5 %convolution_convert_fusion.7 = bf16[512,256]{1,0:T(8,128)(2,1)} fusion(bf16[512,2560]{1,0:T(8,128)(2,1)S(1)} %order_pieces.3, bf16[2560,256]{1,0:T(8,128)(2,1)S(1)} %copy-done.39), kind=kOutput, calls=%fused_computation.14 | convolution fusion | flops 671219712 | bytes 4194304 | tf_op jit(solution)/shard_map/dot_general | solution.py:359
  120.7 0.6 collective-permute-start.16
  121.4 1.5 %gather_rows.6 = bf16[2560,256]{1,0:T(8,128)(2,1)S(1)} custom-call(s32[2]{0:T(128)S(1)} %pad_add_fusion.place, bf16[320,1024]{1,0:T(8,128)(2,1)S(1)} %copy-done.8, bf16[320,1024]{1,0:T(8,128)(2,1)} %collective-permute-done.refs_1_, bf16[320,1024]{1,0:T(8,128)(2,1)S(1)} %copy-done.14, bf16[320,1024]{1,0:T(8,128)(2,1)S(1)} %copy-done.20, ...), custom_call_target="tpu_custom_call" | custom-call | tf_op jit(solution)/shard_map/gather_rows/pallas_call | solution.py:182
  122.9 1.5 %convolution_convert_fusion.1 = bf16[512,256]{1,0:T(8,128)(2,1)} fusion(bf16[512,2560]{1,0:T(8,128)(2,1)S(1)} %order_pieces.3, bf16[2560,256]{1,0:T(8,128)(2,1)S(1)} %gather_rows.6), kind=kOutput, calls=%fused_computation.8 | convolution fusion | flops 671219712 | bytes 4194304 | tf_op jit(solution)/shard_map/dot_general | solution.py:359
  124.4 2.6 %collective-permute-start.19 = (f32[4,4,640]{2,1,0:T(4,128)S(1)}, f32[4,4,640]{2,1,0:T(4,128)S(1)}, u32[]{:S(2)}, u32[]{:S(2)}) collective-permute-start(f32[4,4,640]{2,1,0:T(4,128)S(1)} %pad_maximum_fusion.4), channel_id=1, source_target_pairs={{0,16},{4,20},{8,24},{12,28},{16,0},{20,4},{24,8},{28,12},{1,17},{... | collective-permute-start | bytes 122888 | tf_op jit(solution)/shard_map/ppermute | solution.py:109
  127.0 1.6 %convolution_convert_fusion.3.refs_0_ = bf16[512,256]{1,0:T(8,128)(2,1)} fusion(bf16[512,2560]{1,0:T(8,128)(2,1)S(1)} %copy-done.36, bf16[2560,256]{1,0:T(8,128)(2,1)S(1)} %gather_rows.6), kind=kOutput, calls=%fused_computation.10 | convolution fusion | flops 671219712 | bytes 4194304 | tf_op jit(solution)/shard_map/dot_general | solution.py:361
  128.6 0.6 copy.12
  129.2 0.8 collective-permute-start.20
  130.0 1.4 %gather_rows.7 = bf16[2560,256]{1,0:T(8,128)(2,1)S(1)} custom-call(s32[2]{0:T(128)S(1)} %pad_add_fusion.place, bf16[320,1024]{1,0:T(8,128)(2,1)S(1)} %copy-done.8, bf16[320,1024]{1,0:T(8,128)(2,1)} %collective-permute-done.refs_1_, bf16[320,1024]{1,0:T(8,128)(2,1)S(1)} %copy-done.14, bf16[320,1024]{1,0:T(8,128)(2,1)S(1)} %copy-done.20, ...), custom_call_target="tpu_custom_call" | custom-call | tf_op jit(solution)/shard_map/gather_rows/pallas_call | solution.py:182
  131.6 0.8 fusion.16
  132.5 2.1 %place_columns.2.refs_4_ = bf16[512,2048]{1,0:T(8,128)(2,1)} custom-call(s32[1]{0:T(128)} %bitcast.place, bf16[512,256]{1,0:T(8,128)(2,1)S(1)} %copy-done.43, bf16[512,256]{1,0:T(8,128)(2,1)S(1)} %copy-done.42, bf16[512,256]{1,0:T(8,128)(2,1)} %collective-permute-done.16.refs_2_, bf16[512,256]{1,0:T(8,128)(2,1)S(1)} %collective-permute-done.17.refs_3_), custom_call_target="tpu_custom_call" | custom-call | tf_op jit(solution)/shard_map/place_columns/pallas_call | solution.py:244
  134.6 0.8 convolution_convert_fusion
  135.5 1.3 collective-permute-start.21
  136.8 0.8 convolution_convert_fusion.2.refs_1_
  137.6 0.4 collective-permute-done.20.refs_2_
  138.1 3.8 %collective-permute-done.21.refs_3_ = bf16[512,256]{1,0:T(8,128)(2,1)S(1)} collective-permute-done((bf16[512,256]{1,0:T(8,128)(2,1)S(1)}, bf16[512,256]{1,0:T(8,128)(2,1)S(1)}, u32[]{:S(2)}, u32[]{:S(2)}) %collective-permute-start.21) | collective-permute-done | bytes 262176 | tf_op jit(solution)/shard_map/ppermute | solution.py:272
  141.9 1.9 %place_columns.3 = bf16[512,2048]{1,0:T(8,128)(2,1)} custom-call(s32[1]{0:T(128)} %bitcast.place, bf16[512,256]{1,0:T(8,128)(2,1)S(1)} %copy-done.44, bf16[512,256]{1,0:T(8,128)(2,1)S(1)} %convolution_convert_fusion.2.refs_1_, bf16[512,256]{1,0:T(8,128)(2,1)} %collective-permute-done.20.refs_2_, ...), custom_call_target="tpu_custom_call", output_to_operand_aliasing={{}: (5, {})} | custom-call | tf_op jit(solution)/shard_map/place_columns/pallas_call | solution.py:244
  (123 shorter events, 0.7 us)
Async XLA Ops:
  0.6 10.6 %copy-start = (f32[64,2560]{1,0:T(8,128)S(1)}, f32[64,2560]{1,0:T(8,128)}, u32[]{:S(2)}) copy-start(f32[64,2560]{1,0:T(8,128)} %param.11) | copy-start | bytes 1966084
  0.6 10.5 %copy-start.50 = (s32[1,3]{1,0:T(1,128)S(1)}, s32[1,3]{1,0:T(1,128)}, u32[]{:S(2)}) copy-start(s32[1,3]{1,0:T(1,128)} %param.13) | copy-start | bytes 40
  0.7 10.6 %copy-start.48 = (f32[2560]{0:T(1024)S(1)}, f32[2560]{0:T(1024)}, u32[]{:S(2)}) copy-start(f32[2560]{0:T(1024)} %param.10) | copy-start | bytes 30724
  0.7 10.9 %copy-start.46 = (bf16[1,128,2560]{2,1,0:T(8,128)(2,1)S(1)}, bf16[1,128,2560]{2,1,0:T(8,128)(2,1)}, u32[]{:S(2)}) copy-start(bf16[1,128,2560]{2,1,0:T(8,128)(2,1)} %param.7) | copy-start | bytes 1966084
  0.7 10.9 %copy-start.49 = (s32[1,128]{1,0:T(1,128)S(1)}, s32[1,128]{1,0:T(1,128)}, u32[]{:S(2)}) copy-start(s32[1,128]{1,0:T(1,128)} %param.12) | copy-start | bytes 1540
  3.1 11.9 %copy-start.6 = (bf16[320,1024]{1,0:T(8,128)(2,1)}, bf16[320,1024]{1,0:T(8,128)(2,1)S(1)}, u32[]{:S(2)}) copy-start(bf16[320,1024]{1,0:T(8,128)(2,1)S(1)} %get-tuple-element.32.refs_0_) | copy-start | bytes 1966084
  3.1 22.8 %collective-permute-start.2 = (bf16[320,1024]{1,0:T(8,128)(2,1)S(1)}, bf16[320,1024]{1,0:T(8,128)(2,1)S(1)}, u32[]{:S(2)}, u32[]{:S(2)}) collective-permute-start(bf16[320,1024]{1,0:T(8,128)(2,1)S(1)} %get-tuple-element.32.refs_0_), channel_id=1, source_target_pairs={{8,16},{12,20},{16,8},{20,12},{9,17},{13,21},{17,9},{21,13},{10,18... | collective-permute-start | bytes 1966088 | tf_op jit(solution)/shard_map/ppermute | solution.py:269
  3.8 22.1 %collective-permute-start.1 = (bf16[320,1024]{1,0:T(8,128)(2,1)S(1)}, bf16[320,1024]{1,0:T(8,128)(2,1)S(1)}, u32[]{:S(2)}, u32[]{:S(2)}) collective-permute-start(bf16[320,1024]{1,0:T(8,128)(2,1)S(1)} %get-tuple-element.32.refs_0_), channel_id=1, source_target_pairs={{0,8},{4,12},{8,0},{12,4},{16,24},{20,28},{24,16},{28,20},{1,9},{5... | collective-permute-start | bytes 1966088 | tf_op jit(solution)/shard_map/ppermute | solution.py:269
  9.7 16.2 %collective-permute-start = (bf16[320,1024]{1,0:T(8,128)(2,1)}, bf16[320,1024]{1,0:T(8,128)(2,1)}, u32[]{:S(2)}, u32[]{:S(2)}) collective-permute-start(bf16[320,1024]{1,0:T(8,128)(2,1)} %get-tuple-element.44), channel_id=1, source_target_pairs={{0,4},{4,0},{8,12},{12,8},{16,20},{20,16},{24,28},{28,24},{1,5},{5... | collective-permute-start | bytes 1966088 | tf_op jit(solution)/shard_map/ppermute | solution.py:272
  16.4 27.7 %copy-start.29 = (bf16[144,2560]{1,0:T(8,128)(2,1)}, bf16[144,2560]{1,0:T(8,128)(2,1)S(1)}, u32[]{:S(2)}) copy-start(bf16[144,2560]{1,0:T(8,128)(2,1)S(1)} %pad_maximum_fusion.1.refs_0_) | copy-start | bytes 2211844
  25.9 18.5 %copy-start.9 = (bf16[320,1024]{1,0:T(8,128)(2,1)}, bf16[320,1024]{1,0:T(8,128)(2,1)S(1)}, u32[]{:S(2)}) copy-start(bf16[320,1024]{1,0:T(8,128)(2,1)S(1)} %collective-permute-done.2.refs_4_) | copy-start | bytes 1966084
  25.9 18.5 %copy-start.12 = (bf16[320,1024]{1,0:T(8,128)(2,1)}, bf16[320,1024]{1,0:T(8,128)(2,1)S(1)}, u32[]{:S(2)}) copy-start(bf16[320,1024]{1,0:T(8,128)(2,1)S(1)} %collective-permute-done.1.refs_2_) | copy-start | bytes 1966084
  25.9 16.8 %collective-permute-start.3 = (bf16[144,2560]{1,0:T(8,128)(2,1)S(1)}, bf16[144,2560]{1,0:T(8,128)(2,1)S(1)}, u32[]{:S(2)}, u32[]{:S(2)}) collective-permute-start(bf16[144,2560]{1,0:T(8,128)(2,1)S(1)} %pad_maximum_fusion.1.refs_0_), channel_id=1, source_target_pairs={{0,2},{1,3},{2,0},{3,1},{4,6},{5,7},{6,4},{7,5},{8,10},{9,11},{10,... | collective-permute-start | bytes 2211848 | tf_op jit(solution)/shard_map/ppermute | solution.py:275
  27.5 16.6 %collective-permute-start.4 = (bf16[144,2560]{1,0:T(8,128)(2,1)S(1)}, bf16[144,2560]{1,0:T(8,128)(2,1)S(1)}, u32[]{:S(2)}, u32[]{:S(2)}) collective-permute-start(bf16[144,2560]{1,0:T(8,128)(2,1)S(1)} %pad_maximum_fusion.1.refs_0_), channel_id=1, source_target_pairs={{0,4},{4,0},{8,12},{12,8},{16,20},{20,16},{24,28},{28,24},{1,5},{5... | collective-permute-start | bytes 2211848 | tf_op jit(solution)/shard_map/ppermute | solution.py:272
  29.0 15.4 %collective-permute-start.6 = (bf16[320,1024]{1,0:T(8,128)(2,1)}, bf16[320,1024]{1,0:T(8,128)(2,1)S(1)}, u32[]{:S(2)}, u32[]{:S(2)}) collective-permute-start(bf16[320,1024]{1,0:T(8,128)(2,1)} %collective-permute-done.refs_1_), channel_id=1, source_target_pairs={{8,16},{12,20},{16,8},{20,12},{9,17},{13,21},{17,9},{21,13},{10,18... | collective-permute-start | bytes 1966088 | tf_op jit(solution)/shard_map/ppermute | solution.py:269
  29.7 15.0 %collective-permute-start.5 = (bf16[320,1024]{1,0:T(8,128)(2,1)}, bf16[320,1024]{1,0:T(8,128)(2,1)S(1)}, u32[]{:S(2)}, u32[]{:S(2)}) collective-permute-start(bf16[320,1024]{1,0:T(8,128)(2,1)} %collective-permute-done.refs_1_), channel_id=1, source_target_pairs={{0,8},{4,12},{8,0},{12,4},{16,24},{20,28},{24,16},{28,20},{1,9},{5... | collective-permute-start | bytes 1966088 | tf_op jit(solution)/shard_map/ppermute | solution.py:269
  31.8 12.9 %collective-permute-start.7 = (bf16[320,1024]{1,0:T(8,128)(2,1)S(1)}, bf16[320,1024]{1,0:T(8,128)(2,1)S(1)}, u32[]{:S(2)}, u32[]{:S(2)}) collective-permute-start(bf16[320,1024]{1,0:T(8,128)(2,1)S(1)} %collective-permute-done.1.refs_2_), channel_id=1, source_target_pairs={{8,16},{12,20},{16,8},{20,12},{9,17},{13,21},{17,9},{21,13},{10,18... | collective-permute-start | bytes 1966088 | tf_op jit(solution)/shard_map/ppermute | solution.py:269
  42.7 1.7 %copy-start.31 = (bf16[144,2560]{1,0:T(8,128)(2,1)}, bf16[144,2560]{1,0:T(8,128)(2,1)S(1)}, u32[]{:S(2)}) copy-start(bf16[144,2560]{1,0:T(8,128)(2,1)S(1)} %collective-permute-done.3.refs_2_) | copy-start | bytes 2211844
  42.7 16.0 %collective-permute-start.8 = (bf16[320,1024]{1,0:T(8,128)(2,1)S(1)}, bf16[320,1024]{1,0:T(8,128)(2,1)S(1)}, u32[]{:S(2)}, u32[]{:S(2)}) collective-permute-start(bf16[320,1024]{1,0:T(8,128)(2,1)S(1)} %collective-permute-done.2.refs_4_), channel_id=1, source_target_pairs={{8,0},{12,4},{16,24},{20,28},{9,1},{13,5},{17,25},{21,29},{10,2},{... | collective-permute-start | bytes 1966088 | tf_op jit(solution)/shard_map/ppermute | solution.py:269
  44.1 15.5 %copy-start.27 = (bf16[144,2560]{1,0:T(8,128)(2,1)}, bf16[144,2560]{1,0:T(8,128)(2,1)S(1)}, u32[]{:S(2)}) copy-start(bf16[144,2560]{1,0:T(8,128)(2,1)S(1)} %collective-permute-done.4.refs_0_.refs_4_) | copy-start | bytes 2211844
  59.6 22.6 %collective-permute-start.9 = (bf16[3,144,2560]{2,1,0:T(8,128)(2,1)S(1)}, bf16[3,144,2560]{2,1,0:T(8,128)(2,1)S(1)}, u32[]{:S(2)}, u32[]{:S(2)}) collective-permute-start(bf16[3,144,2560]{2,1,0:T(8,128)(2,1)S(1)} %pad_maximum_fusion), channel_id=1, source_target_pairs={{0,1},{1,0},{2,3},{3,2},{4,5},{5,4},{6,7},{7,6},{8,9},{9,8},{10,11... | collective-permute-start | bytes 6635528 | tf_op jit(solution)/shard_map/ppermute | solution.py:275
  59.6 22.6 %collective-permute-start.10 = (bf16[144,2560]{1,0:T(8,128)(2,1)S(1)}, bf16[144,2560]{1,0:T(8,128)(2,1)}, u32[]{:S(2)}, u32[]{:S(2)}) collective-permute-start(bf16[144,2560]{1,0:T(8,128)(2,1)S(1)} %collective-permute-done.4.refs_0_.refs_4_), channel_id=1, source_target_pairs={{0,2},{1,3},{2,0},{3,1},{4,6},{5,7},{6,4},{7,5},{8,10},{9,11},{10,... | collective-permute-start | bytes 2211848 | tf_op jit(solution)/shard_map/ppermute | solution.py:275
  61.0 3.7 %collective-permute-start.11 = (bf16[320,1024]{1,0:T(8,128)(2,1)S(1)}, bf16[320,1024]{1,0:T(8,128)(2,1)S(1)}, u32[]{:S(2)}, u32[]{:S(2)}) collective-permute-start(bf16[320,1024]{1,0:T(8,128)(2,1)S(1)} %collective-permute-done.5.refs_3_), channel_id=1, source_target_pairs={{8,16},{12,20},{16,8},{20,12},{9,17},{13,21},{17,9},{21,13},{10,18... | collective-permute-start | bytes 1966088 | tf_op jit(solution)/shard_map/ppermute | solution.py:269
  62.5 18.7 %collective-permute-start.12 = (bf16[320,1024]{1,0:T(8,128)(2,1)S(1)}, bf16[320,1024]{1,0:T(8,128)(2,1)S(1)}, u32[]{:S(2)}, u32[]{:S(2)}) collective-permute-start(bf16[320,1024]{1,0:T(8,128)(2,1)S(1)} %collective-permute-done.6.refs_5_), channel_id=1, source_target_pairs={{8,0},{12,4},{16,24},{20,28},{9,1},{13,5},{17,25},{21,29},{10,2},{... | collective-permute-start | bytes 1966088 | tf_op jit(solution)/shard_map/ppermute | solution.py:269
  82.1 8.6 %copy-start.1 = (bf16[3,144,2560]{2,1,0:T(8,128)(2,1)}, bf16[3,144,2560]{2,1,0:T(8,128)(2,1)S(1)}, u32[]{:S(2)}) copy-start(bf16[3,144,2560]{2,1,0:T(8,128)(2,1)S(1)} %collective-permute-done.9.refs_1_.refs_3_.refs_5_) | copy-start | bytes 6635524
  84.9 19.9 %collective-permute-start.14 = (bf16[640,512]{1,0:T(8,128)(2,1)}, bf16[640,512]{1,0:T(8,128)(2,1)}, u32[]{:S(2)}, u32[]{:S(2)}) collective-permute-start(bf16[640,512]{1,0:T(8,128)(2,1)} %get-tuple-element.31), channel_id=1, source_target_pairs={{8,0},{12,4},{16,24},{20,28},{9,1},{13,5},{17,25},{21,29},{10,2},{... | collective-permute-start | bytes 1966088 | tf_op jit(solution)/shard_map/ppermute | solution.py:269
  86.2 25.1 %collective-permute-start.13 = (bf16[144,2560]{1,0:T(8,128)(2,1)}, bf16[144,2560]{1,0:T(8,128)(2,1)}, u32[]{:S(2)}, u32[]{:S(2)}) collective-permute-start(bf16[144,2560]{1,0:T(8,128)(2,1)} %collective-permute-done.10.refs_2_.refs_6_), channel_id=1, source_target_pairs={{0,1},{1,0},{2,3},{3,2},{4,5},{5,4},{6,7},{7,6},{8,9},{9,8},{10,11... | collective-permute-start | bytes 2211848 | tf_op jit(solution)/shard_map/ppermute | solution.py:275
  86.3 35.0 %collective-permute-start.15 = (bf16[640,512]{1,0:T(8,128)(2,1)}, bf16[640,512]{1,0:T(8,128)(2,1)}, u32[]{:S(2)}, u32[]{:S(2)}) collective-permute-start(bf16[640,512]{1,0:T(8,128)(2,1)} %copy-done.45), channel_id=1, source_target_pairs={{8,0},{12,4},{16,24},{20,28},{9,1},{13,5},{17,25},{21,29},{10,2},{... | collective-permute-start | bytes 1966088 | tf_op jit(solution)/shard_map/ppermute | solution.py:269
  89.8 14.9 %copy-start.4 = (bf16[320,1024]{1,0:T(8,128)(2,1)S(1)}, bf16[320,1024]{1,0:T(8,128)(2,1)}, u32[]{:S(2)}) copy-start(bf16[320,1024]{1,0:T(8,128)(2,1)} %copy-done.3) | copy-start | bytes 1966084
  89.8 14.9 %copy-start.7 = (bf16[320,1024]{1,0:T(8,128)(2,1)S(1)}, bf16[320,1024]{1,0:T(8,128)(2,1)}, u32[]{:S(2)}) copy-start(bf16[320,1024]{1,0:T(8,128)(2,1)} %copy-done.6) | copy-start | bytes 1966084
  89.8 14.9 %copy-start.10 = (bf16[320,1024]{1,0:T(8,128)(2,1)S(1)}, bf16[320,1024]{1,0:T(8,128)(2,1)}, u32[]{:S(2)}) copy-start(bf16[320,1024]{1,0:T(8,128)(2,1)} %copy-done.9) | copy-start | bytes 1966084
  89.8 14.9 %copy-start.13 = (bf16[320,1024]{1,0:T(8,128)(2,1)S(1)}, bf16[320,1024]{1,0:T(8,128)(2,1)}, u32[]{:S(2)}) copy-start(bf16[320,1024]{1,0:T(8,128)(2,1)} %copy-done.12) | copy-start | bytes 1966084
  89.9 14.9 %copy-start.16 = (bf16[320,1024]{1,0:T(8,128)(2,1)S(1)}, bf16[320,1024]{1,0:T(8,128)(2,1)}, u32[]{:S(2)}) copy-start(bf16[320,1024]{1,0:T(8,128)(2,1)} %copy-done.15) | copy-start | bytes 1966084
  89.9 14.9 %copy-start.19 = (bf16[320,1024]{1,0:T(8,128)(2,1)S(1)}, bf16[320,1024]{1,0:T(8,128)(2,1)}, u32[]{:S(2)}) copy-start(bf16[320,1024]{1,0:T(8,128)(2,1)} %copy-done.18) | copy-start | bytes 1966084
  89.9 14.9 %copy-start.22 = (bf16[320,1024]{1,0:T(8,128)(2,1)S(1)}, bf16[320,1024]{1,0:T(8,128)(2,1)}, u32[]{:S(2)}) copy-start(bf16[320,1024]{1,0:T(8,128)(2,1)} %copy-done.21) | copy-start | bytes 1966084
  89.9 14.9 %copy-start.25 = (bf16[320,1024]{1,0:T(8,128)(2,1)S(1)}, bf16[320,1024]{1,0:T(8,128)(2,1)}, u32[]{:S(2)}) copy-start(bf16[320,1024]{1,0:T(8,128)(2,1)} %copy-done.24) | copy-start | bytes 1966084
  90.8 18.9 %copy-start.35 = (bf16[512,2560]{1,0:T(8,128)(2,1)}, bf16[512,2560]{1,0:T(8,128)(2,1)S(1)}, u32[]{:S(2)}) copy-start(bf16[512,2560]{1,0:T(8,128)(2,1)S(1)} %order_pieces.2) | copy-start | bytes 7864324
  106.2 1.9 %copy-start.40 = (bf16[2560,256]{1,0:T(8,128)(2,1)}, bf16[2560,256]{1,0:T(8,128)(2,1)S(1)}, u32[]{:S(2)}) copy-start(bf16[2560,256]{1,0:T(8,128)(2,1)S(1)} %gather_rows.5) | copy-start | bytes 3932164
  108.2 1.5 %copy-start.38 = (bf16[2560,256]{1,0:T(8,128)(2,1)}, bf16[2560,256]{1,0:T(8,128)(2,1)S(1)}, u32[]{:S(2)}) copy-start(bf16[2560,256]{1,0:T(8,128)(2,1)S(1)} %gather_rows.4) | copy-start | bytes 3932164
  111.3 1.8 %copy-start.2 = (bf16[3,144,2560]{2,1,0:T(8,128)(2,1)S(1)}, bf16[3,144,2560]{2,1,0:T(8,128)(2,1)}, u32[]{:S(2)}) copy-start(bf16[3,144,2560]{2,1,0:T(8,128)(2,1)} %copy-done.1) | copy-start | bytes 6635524
  113.0 11.4 %collective-permute-start.18 = (f32[2,4,640]{2,1,0:T(4,128)}, f32[2,4,640]{2,1,0:T(4,128)S(1)}, u32[]{:S(2)}, u32[]{:S(2)}) collective-permute-start(f32[2,4,640]{2,1,0:T(4,128)} %frame_lines.1), channel_id=1, source_target_pairs={{0,8},{4,12},{8,0},{12,4},{16,24},{20,28},{24,16},{28,20},{1,9},{5... | collective-permute-start | bytes 61448 | tf_op jit(solution)/shard_map/ppermute | solution.py:109
  114.2 1.7 %copy-start.41 = (bf16[2560,256]{1,0:T(8,128)(2,1)S(1)}, bf16[2560,256]{1,0:T(8,128)(2,1)}, u32[]{:S(2)}) copy-start(bf16[2560,256]{1,0:T(8,128)(2,1)} %copy-done.40) | copy-start | bytes 3932164
  115.9 6.9 %copy-start.33 = (bf16[512,2560]{1,0:T(8,128)(2,1)}, bf16[512,2560]{1,0:T(8,128)(2,1)S(1)}, u32[]{:S(2)}) copy-start(bf16[512,2560]{1,0:T(8,128)(2,1)S(1)} %order_pieces.3) | copy-start | bytes 7864324
  116.0 3.2 %copy-start.39 = (bf16[2560,256]{1,0:T(8,128)(2,1)S(1)}, bf16[2560,256]{1,0:T(8,128)(2,1)}, u32[]{:S(2)}) copy-start(bf16[2560,256]{1,0:T(8,128)(2,1)} %copy-done.38) | copy-start | bytes 3932164
  116.0 5.4 %copy-start.26 = (bf16[320,1024]{1,0:T(8,128)(2,1)S(1)}, bf16[320,1024]{1,0:T(8,128)(2,1)}, u32[]{:S(2)}) copy-start(bf16[320,1024]{1,0:T(8,128)(2,1)} %copy-done.24) | copy-start | bytes 1966084
  117.5 3.8 %copy-start.5 = (bf16[320,1024]{1,0:T(8,128)(2,1)S(1)}, bf16[320,1024]{1,0:T(8,128)(2,1)}, u32[]{:S(2)}) copy-start(bf16[320,1024]{1,0:T(8,128)(2,1)} %copy-done.3) | copy-start | bytes 1966084
  117.5 3.8 %copy-start.8 = (bf16[320,1024]{1,0:T(8,128)(2,1)S(1)}, bf16[320,1024]{1,0:T(8,128)(2,1)}, u32[]{:S(2)}) copy-start(bf16[320,1024]{1,0:T(8,128)(2,1)} %copy-done.6) | copy-start | bytes 1966084
  117.5 3.8 %copy-start.11 = (bf16[320,1024]{1,0:T(8,128)(2,1)S(1)}, bf16[320,1024]{1,0:T(8,128)(2,1)}, u32[]{:S(2)}) copy-start(bf16[320,1024]{1,0:T(8,128)(2,1)} %copy-done.9) | copy-start | bytes 1966084
  117.5 3.8 %copy-start.14 = (bf16[320,1024]{1,0:T(8,128)(2,1)S(1)}, bf16[320,1024]{1,0:T(8,128)(2,1)}, u32[]{:S(2)}) copy-start(bf16[320,1024]{1,0:T(8,128)(2,1)} %copy-done.12) | copy-start | bytes 1966084
  117.5 3.8 %copy-start.17 = (bf16[320,1024]{1,0:T(8,128)(2,1)S(1)}, bf16[320,1024]{1,0:T(8,128)(2,1)}, u32[]{:S(2)}) copy-start(bf16[320,1024]{1,0:T(8,128)(2,1)} %copy-done.15) | copy-start | bytes 1966084
  117.6 3.8 %copy-start.20 = (bf16[320,1024]{1,0:T(8,128)(2,1)S(1)}, bf16[320,1024]{1,0:T(8,128)(2,1)}, u32[]{:S(2)}) copy-start(bf16[320,1024]{1,0:T(8,128)(2,1)} %copy-done.18) | copy-start | bytes 1966084
  117.6 3.8 %copy-start.23 = (bf16[320,1024]{1,0:T(8,128)(2,1)S(1)}, bf16[320,1024]{1,0:T(8,128)(2,1)}, u32[]{:S(2)}) copy-start(bf16[320,1024]{1,0:T(8,128)(2,1)} %copy-done.21) | copy-start | bytes 1966084
  117.6 14.9 %collective-permute-start.17 = (bf16[512,256]{1,0:T(8,128)(2,1)}, bf16[512,256]{1,0:T(8,128)(2,1)S(1)}, u32[]{:S(2)}, u32[]{:S(2)}) collective-permute-start(bf16[512,256]{1,0:T(8,128)(2,1)} %convolution_convert_fusion.5), channel_id=1, source_target_pairs={{0,4},{4,0},{8,12},{12,8},{16,20},{20,16},{24,28},{28,24},{1,5},{5... | collective-permute-start | bytes 786440 | tf_op jit(solution)/shard_map/ppermute | solution.py:272
  120.7 11.8 %collective-permute-start.16 = (bf16[512,256]{1,0:T(8,128)(2,1)}, bf16[512,256]{1,0:T(8,128)(2,1)}, u32[]{:S(2)}, u32[]{:S(2)}) collective-permute-start(bf16[512,256]{1,0:T(8,128)(2,1)} %convolution_convert_fusion.7), channel_id=1, source_target_pairs={{0,4},{4,0},{8,12},{12,8},{16,20},{20,16},{24,28},{28,24},{1,5},{5... | collective-permute-start | bytes 786440 | tf_op jit(solution)/shard_map/ppermute | solution.py:272
  122.9 1.6 %copy-start.47 = (f32[2,4,640]{2,1,0:T(4,128)S(1)}, f32[2,4,640]{2,1,0:T(4,128)}, u32[]{:S(2)}) copy-start(f32[2,4,640]{2,1,0:T(4,128)} %frame_lines.1) | copy-start | bytes 61444
  122.9 4.2 %copy-start.36 = (bf16[512,2560]{1,0:T(8,128)(2,1)S(1)}, bf16[512,2560]{1,0:T(8,128)(2,1)}, u32[]{:S(2)}) copy-start(bf16[512,2560]{1,0:T(8,128)(2,1)} %copy-done.35) | copy-start | bytes 7864324
  124.4 7.0 %collective-permute-start.19 = (f32[4,4,640]{2,1,0:T(4,128)S(1)}, f32[4,4,640]{2,1,0:T(4,128)S(1)}, u32[]{:S(2)}, u32[]{:S(2)}) collective-permute-start(f32[4,4,640]{2,1,0:T(4,128)S(1)} %pad_maximum_fusion.4), channel_id=1, source_target_pairs={{0,16},{4,20},{8,24},{12,28},{16,0},{20,4},{24,8},{28,12},{1,17},{... | collective-permute-start | bytes 122888 | tf_op jit(solution)/shard_map/ppermute | solution.py:109
  129.2 3.3 %copy-start.42 = (bf16[512,256]{1,0:T(8,128)(2,1)S(1)}, bf16[512,256]{1,0:T(8,128)(2,1)}, u32[]{:S(2)}) copy-start(bf16[512,256]{1,0:T(8,128)(2,1)} %convolution_convert_fusion.4.refs_1_) | copy-start | bytes 786436
  129.2 3.3 %copy-start.43 = (bf16[512,256]{1,0:T(8,128)(2,1)S(1)}, bf16[512,256]{1,0:T(8,128)(2,1)}, u32[]{:S(2)}) copy-start(bf16[512,256]{1,0:T(8,128)(2,1)} %convolution_convert_fusion.6.refs_0_) | copy-start | bytes 786436
  129.2 8.8 %collective-permute-start.20 = (bf16[512,256]{1,0:T(8,128)(2,1)}, bf16[512,256]{1,0:T(8,128)(2,1)}, u32[]{:S(2)}, u32[]{:S(2)}) collective-permute-start(bf16[512,256]{1,0:T(8,128)(2,1)} %convolution_convert_fusion.1), channel_id=1, source_target_pairs={{0,4},{4,0},{8,12},{12,8},{16,20},{20,16},{24,28},{28,24},{1,5},{5... | collective-permute-start | bytes 786440 | tf_op jit(solution)/shard_map/ppermute | solution.py:272
  132.4 2.1 %copy-start.34 = (bf16[512,2560]{1,0:T(8,128)(2,1)S(1)}, bf16[512,2560]{1,0:T(8,128)(2,1)}, u32[]{:S(2)}) copy-start(bf16[512,2560]{1,0:T(8,128)(2,1)} %copy-done.33) | copy-start | bytes 7864324
  134.6 2.2 %copy-start.37 = (bf16[512,2560]{1,0:T(8,128)(2,1)S(1)}, bf16[512,2560]{1,0:T(8,128)(2,1)}, u32[]{:S(2)}) copy-start(bf16[512,2560]{1,0:T(8,128)(2,1)} %copy-done.35) | copy-start | bytes 7864324
  135.5 6.5 %copy-start.44 = (bf16[512,256]{1,0:T(8,128)(2,1)S(1)}, bf16[512,256]{1,0:T(8,128)(2,1)}, u32[]{:S(2)}) copy-start(bf16[512,256]{1,0:T(8,128)(2,1)} %convolution_convert_fusion.3.refs_0_) | copy-start | bytes 786436
  135.5 6.4 %collective-permute-start.21 = (bf16[512,256]{1,0:T(8,128)(2,1)S(1)}, bf16[512,256]{1,0:T(8,128)(2,1)S(1)}, u32[]{:S(2)}, u32[]{:S(2)}) collective-permute-start(bf16[512,256]{1,0:T(8,128)(2,1)S(1)} %convolution_convert_fusion), channel_id=1, source_target_pairs={{0,4},{4,0},{8,12},{12,8},{16,20},{20,16},{24,28},{28,24},{1,5},{5... | collective-permute-start | bytes 786440 | tf_op jit(solution)/shard_map/ppermute | solution.py:272
  (9 other events, 8.4 us)

commit v3 on v2

--- a/solution.py
+++ b/solution.py
@@ -7,7 +7,7 @@
 
 HIGHEST = lax.Precision.HIGHEST
 CHUNKS = 4
-BLOCKS = 2
+BLOCKS = (2, 1, 1)
 
 
 def onehot(values, count):
@@ -125,96 +125,114 @@
     return lax.optimization_barrier((array, *earlier))[0]
 
 
-def slice_rows(upper, lower, count):
-    rows, columns = upper.shape
-    width = columns // count
+def slice_rows(upper, lower, widths):
+    rows = upper.shape[0]
     vmem = pl.BlockSpec(memory_space=pltpu.VMEM)
 
     def kernel(upper, lower, *results):
         for index, result in enumerate(results):
-            chunk = pl.ds(index * width, width)
+            chunk = pl.ds(sum(widths[:index]), widths[index])
             result[:rows] = upper[:, chunk]
             result[rows:] = lower[:, chunk]
 
     return pl.pallas_call(
         kernel,
-        out_shape=[jax.ShapeDtypeStruct((2 * rows, width), upper.dtype)] * count,
+        out_shape=[jax.ShapeDtypeStruct((2 * rows, width), upper.dtype) for width in widths],
         in_specs=[vmem, vmem],
-        out_specs=[vmem] * count,
+        out_specs=[vmem] * len(widths),
         compiler_params=pltpu.CompilerParams(vmem_limit_bytes=16 << 20),
         name="slice_rows",
     )(upper, lower)
 
 
-def gather_rows(y, is_mid, start, width, own, near, crossed, forwarded, last, offset):
-    rows = own[0].shape[0]
+def block_rows(y, is_mid, blocks):
+    rows, width = blocks[0][0].shape
     vmem = pl.BlockSpec(memory_space=pltpu.VMEM)
-    parts = [*own, *near, *crossed[0], *crossed[1], *forwarded]
+    parts = [part for block in blocks for part in block]
 
     def kernel(place, *refs):
-        result = refs[len(parts) + 1]
+        result = refs[len(parts)]
         first = pl.multiple_of(place[0] * rows, 16)
         second = pl.multiple_of((1 - place[0]) * rows, 16)
-        chunk = pl.ds(start, width)
-
-        def put(block, index):
+
+        def put(block, upper, lower):
             base = 2 * rows * block
-            result[pl.ds(pl.multiple_of(base + first, 16), rows), :] = refs[index][:, chunk]
-            result[pl.ds(pl.multiple_of(base + second, 16), rows), :] = refs[index + 1][:, chunk]
-
-        put(0, 0)
-        put(1, 2)
-
-        @pl.when(place[1] == 1)
-        def _():
-            put(2, 4)
-            put(3, 6)
-
-        @pl.when(place[1] == 0)
-        def _():
-            put(2, 8)
-            final = refs[len(parts)]
-            inner = pl.ds(offset, width)
-            base = 6 * rows
-            result[pl.ds(pl.multiple_of(base + first, 16), rows), :] = final[:rows, inner]
-            result[pl.ds(pl.multiple_of(base + second, 16), rows), :] = final[rows:, inner]
-
-    return pl.pallas_call(
-        kernel,
-        out_shape=jax.ShapeDtypeStruct((8 * rows, width), last.dtype),
-        in_specs=[pl.BlockSpec(memory_space=pltpu.SMEM)] + [vmem] * (len(parts) + 1),
+            result[pl.ds(pl.multiple_of(base + first, 16), rows), :] = upper[...]
+            result[pl.ds(pl.multiple_of(base + second, 16), rows), :] = lower[...]
+
+        index = 0
+        for position, block in enumerate(blocks):
+            held = refs[index : index + len(block)]
+            index += len(block)
+            if len(block) == 2:
+                put(position, *held)
+            else:
+                pl.when(place[1] == 1)(lambda: put(position, *held[:2]))
+                pl.when(place[1] == 0)(lambda: put(position, *held[2:]))
+
+    return pl.pallas_call(
+        kernel,
+        out_shape=jax.ShapeDtypeStruct((2 * rows * len(blocks), width), parts[0].dtype),
+        in_specs=[pl.BlockSpec(memory_space=pltpu.SMEM)] + [vmem] * len(parts),
         out_specs=vmem,
         compiler_params=pltpu.CompilerParams(vmem_limit_bytes=24 << 20),
-        name="gather_rows",
-    )(jnp.stack([y, is_mid.astype(jnp.int32)]).astype(jnp.int32), *parts, last)
-
-
-def order_pieces(me, rows, pieces):
-    count, width = 4, pieces[0][0].shape[1]
+        name="block_rows",
+    )(jnp.stack([y, is_mid.astype(jnp.int32)]).astype(jnp.int32), *parts)
+
+
+def last_rows(y, is_mid, width, sent, arrived, offset):
+    rows = sent.shape[0] // 2
+    vmem = pl.BlockSpec(memory_space=pltpu.VMEM)
+
+    def kernel(place, sent, arrived, result):
+        def put(source):
+            first = pl.ds(pl.multiple_of(place[0] * rows, 16), rows)
+            second = pl.ds(pl.multiple_of((1 - place[0]) * rows, 16), rows)
+            result[first, :] = source[:rows, offset : offset + width]
+            result[second, :] = source[rows:, offset : offset + width]
+
+        pl.when(place[1] == 1)(lambda: put(sent))
+        pl.when(place[1] == 0)(lambda: put(arrived))
+
+    return pl.pallas_call(
+        kernel,
+        out_shape=jax.ShapeDtypeStruct((2 * rows, width), sent.dtype),
+        in_specs=[pl.BlockSpec(memory_space=pltpu.SMEM)] + [vmem] * 2,
+        out_specs=vmem,
+        compiler_params=pltpu.CompilerParams(vmem_limit_bytes=16 << 20),
+        name="last_rows",
+    )(jnp.stack([y, is_mid.astype(jnp.int32)]).astype(jnp.int32), sent, arrived)
+
+
+def order_pieces(me, rows, widths, pieces):
+    count, groups = 4, len(widths)
     any_space = pl.BlockSpec(memory_space=pl.ANY)
 
     def kernel(place, *refs):
-        result, sems = refs[count], refs[count + 1]
+        results, sems = refs[count : count + groups], refs[count + groups]
         sources = [
             ref if index is None else ref.at[index] for ref, (_, index) in zip(refs, pieces)
         ]
         copies = []
-        for flip in range(count):
-            start = pl.multiple_of((place[0] ^ flip) * rows, 128)
-            source = sources[flip].at[pl.ds(0, rows)]
-            copies.append(
-                pltpu.make_async_copy(source, result.at[pl.ds(start, rows)], sems.at[flip])
-            )
-            copies[-1].start()
+        for side, width in enumerate(widths):
+            columns = pl.ds(sum(widths[:side]), width)
+            for flip in range(count):
+                start = pl.multiple_of((place[0] ^ flip) * rows, 128)
+                source = sources[flip].at[pl.ds(0, rows), columns]
+                target = results[side].at[pl.ds(start, rows)]
+                copies.append(pltpu.make_async_copy(source, target, sems.at[side * count + flip]))
+                copies[-1].start()
         for copy in copies:
             copy.wait()
 
     return pl.pallas_call(
         kernel,
-        out_shape=jax.ShapeDtypeStruct((count * rows, width), pieces[0][0].dtype),
+        out_shape=[
+            jax.ShapeDtypeStruct((count * rows, width), pieces[0][0].dtype) for width in widths
+        ],
         in_specs=[pl.BlockSpec(memory_space=pltpu.SMEM)] + [any_space] * count,
-        out_specs=pl.BlockSpec(memory_space=pltpu.VMEM),
-        scratch_shapes=[pltpu.SemaphoreType.DMA((count,))],
+        out_specs=[pl.BlockSpec(memory_space=pltpu.VMEM)] * groups,
+        scratch_shapes=[pltpu.SemaphoreType.DMA((groups * count,))],
         compiler_params=pltpu.CompilerParams(vmem_limit_bytes=16 << 20),
         name="order_pieces",
     )(me.astype(jnp.int32).reshape(1), *[array for array, _ in pieces])
@@ -314,52 +332,71 @@
 
     gate = (near_q, crossed_q, crossed_near_p, forwarded_p)
     theirs_x = over_seq(after(theirs, *gate), 2)
-    three_core = over_seq(after(jnp.stack([tokens, mine_x, theirs]), *gate), 1)
     crossed_near_q = across(after(near_q, *gate))
     forwarded_q = outward(after(crossed_q, *gate))
 
-    gate = (crossed_near_q, forwarded_q, three_core, theirs_x)
+    own_rows = block_rows(y, is_mid, ((own_p, own_q), (near_p, near_q)))
+
+    gate = (crossed_near_q, forwarded_q, theirs_x)
+    three_core = over_seq(after(jnp.stack([tokens, mine_x, theirs]), *gate, own_rows), 1)
     theirs_x_core = over_seq(after(theirs_x, *gate), 1)
     clips = (
         ((tokens, None), (three_core, 0), (mine_x, None), (three_core, 1)),
         ((theirs, None), (three_core, 2), (theirs_x, None), (theirs_x_core, None)),
     )
-    mine, other = order_pieces(me, piece, clips[0]), order_pieces(me, piece, clips[1])
+    cuts = (2 * block, block, block)
+    mine = order_pieces(me, piece, cuts, clips[0])
+    other = order_pieces(me, piece, cuts, clips[1])
+    far = (after(crossed_p, three_core), crossed_q, forwarded_p, forwarded_q)
+    far_rows = block_rows(y, is_mid, (far,))
+
+    def first_sum(first, second):
+        return jnp.dot(first, own_rows, preferred_element_type=jnp.float32) + jnp.dot(
+            second, far_rows, preferred_element_type=jnp.float32
+        )
+
     frame_count = levels.shape[1]
     columns = shard * dp // seq
     packed = frames_of(me, piece, frame_count, columns, clips[0] + clips[1])
     frame_grad = packed[0, :frame_count]
-
-    blocks = slice_rows(after(crossed_near_p, *gate), after(crossed_near_q, *gate), BLOCKS)
-    last = [outward(block) for block in blocks]
-    each = CHUNKS // BLOCKS
-    kept, received, products = [], [], []
+    other_sum = first_sum(other[0], other[1])
+    mine_sum = first_sum(after(mine[0], packed), mine[1])
+
+    blocks = slice_rows(
+        after(crossed_near_p, *gate),
+        after(crossed_near_q, *gate),
+        [count * width for count in BLOCKS],
+    )
+    last = [outward(arrived) for arrived in blocks]
+    places = [
+        (sent, arrived, offset * width)
+        for sent, arrived, count in zip(blocks, last, BLOCKS)
+        for offset in range(count)
+    ]
     firsts = [position * width for position in range(CHUNKS)]
-    packed = clip_step(packed, dp, 2, (theirs_x_core,))
-    packed = clip_step(packed, dp, 4, (last[0],))
-    for index in range(CHUNKS):
-        block, offset = last[index // each], index % each * width
-        own = after(own_p, *products[: 2 * each]) if index >= each else own_p
-        full = gather_rows(
-            y,
-            is_mid,
-            index * width,
-            width,
-            (own, own_q),
-            (near_p, near_q),
-            ((crossed_p, crossed_q), (crossed_near_p, crossed_near_q)),
-            (forwarded_p, forwarded_q),
-            block,
-            offset,
-        )
-        if index == CHUNKS - 1:
-            result = place_columns(y, half, firsts[:2], kept[:2], received[:2])
-            table_grad = table_of(packed, level_table.shape[0])
-            full = after(full, result, table_grad)
-        part = jnp.dot(other, full, preferred_element_type=jnp.float32).astype(jnp.bfloat16)
-        received.append(over_y(part))
-        kept.append(jnp.dot(mine, full, preferred_element_type=jnp.float32).astype(jnp.bfloat16))
-        products += [part, kept[-1]]
+    kept, received, parts, rows = [], [], [], []
+
+    def finish(earlier, tokens_last, index):
+        product = jnp.dot(tokens_last, rows[index], preferred_element_type=jnp.float32)
+        return (earlier[:, firsts[index] : firsts[index] + width] + product).astype(jnp.bfloat16)
+
+    for index, (sent, arrived, offset) in enumerate(places):
+        if index < 2:
+            sent = after(sent, other_sum, mine_sum)
+        if index == 2:
+            packed = clip_step(packed, dp, 2, (parts[1],))
+            sent = after(sent, packed, *parts)
+        if index == 3:
+            packed = clip_step(packed, dp, 4, (parts[2],))
+            sent = after(sent, packed, *kept)
+        rows.append(last_rows(y, is_mid, width, sent, arrived, offset))
+        parts.append(finish(other_sum, other[2], index))
+        received.append(over_y(parts[index]))
+        if index % 2:
+            tokens_last = after(mine[2], parts[index])
+            kept += [finish(mine_sum, tokens_last, done) for done in (index - 1, index)]
+    table_grad = table_of(packed, level_table.shape[0])
+    result = place_columns(after(y, parts[-1]), half, firsts[:2], kept[:2], received[:2])
     hidden_grad = place_columns(y, half, firsts[2:], kept[2:], received[2:], result)
     return hidden_grad[None], frame_grad[None], table_grad
 

time: 145 us -> 136 us (0.938)
  waiting for transfers between devices: 69 us -> 49.6 us
  starting transfers between devices: 28.9 us -> 34.3 us
  other arithmetic: 0.58 us -> 3.9 us
    ppermute x10 -> x11, waiting for transfers between devices: 44.9 us -> 25.6 us  [along_z(): return lax.ppermute(array, 'dp', perm)]
    ppermute x2, waiting for transfers between devices: 0.01 us -> 4.32 us  [clip_step(): arrived = lax.ppermute(sent, 'dp', [(i, i ^ flip) for i in range(dp)])]
    ppermute x4, waiting for transfers between devices: 10.3 us -> 6.95 us  [over_seq(): return lax.ppermute(array, 'seq', [(i, i ^ flip) for i in range(seq)])]
    another operation x3, other arithmetic: 0.38 us -> 3.15 us  [the longest x2 3.07 us: staged_body(): jnp.stack([tokens, mine_x, theirs])]
    ppermute x2, starting transfers between devices: 2.68 us -> 5.06 us  [clip_step(): arrived = lax.ppermute(sent, 'dp', [(i, i ^ flip) for i in range(dp)])]
    ppermute x10 -> x11, starting transfers between devices: 15.8 us -> 17.9 us  [along_z(): return lax.ppermute(array, 'dp', perm)]
    pallas_call x2, Pallas kernels: 4.04 us -> 2 us  [place_columns(): pl.pallas_call(kernel, out_shape=jax.ShapeDtypeStruct((rows, 2 * half), k...]
    pallas_call x6 -> x8, Pallas kernels: 8.89 us -> 10.6 us  [the longest x4 4.91 us: last_rows(): pl.pallas_call(kernel, out_shape=jax.ShapeDtypeStruct((2 * rows, width),...]
  transfers between devices with their start and end apart: 22 -> 23, of which waited for: 8 -> 8; matrix products, arithmetic and copies ran while one was open for 13% -> 16% of each run, Pallas kernels for 9% -> 11%
where the time goes in v3:
time: 136 us; the launch traced here: 135 us
  waiting for transfers between devices  49.6 us (36%)
  starting transfers between devices  34.3 us (25%)
  Pallas kernels  16.4 us (12%)
  matrix products  15.2 us (11%)
  local copies, waits for them, and re-layouts  14.1 us (10%)
  other arithmetic  3.9 us (3%)
    ppermute x11, waiting for transfers between devices, along_z(): return lax.ppermute(array, 'dp', perm)  25.6 us
    ppermute x11, starting transfers between devices, along_z(): return lax.ppermute(array, 'dp', perm)  17.9 us
    ppermute x6, waiting for transfers between devices, over_y(): return lax.ppermute(array, 'dp', [(i, i ^ 1) for i in range(dp)])  12.8 us
    unnamed x69, local copies, waits for them, and re-layouts  9.63 us
    ppermute x6, starting transfers between devices, over_y(): return lax.ppermute(array, 'dp', [(i, i ^ 1) for i in range(dp)])  7.73 us
    ppermute x4, waiting for transfers between devices, over_seq(): return lax.ppermute(array, 'seq', [(i, i ^ flip) for i in range(seq)])  6.95 us
    dot_general x8, matrix products, finish(): jnp.dot(tokens_last, rows[index], preferred_element_type=jnp.float32)  6.72 us
    ppermute x2, starting transfers between devices, clip_step(): arrived = lax.ppermute(sent, 'dp', [(i, i ^ flip) for i in range(dp)])  5.06 us
  transfers between devices with their start and end apart: 23, of which 8 were waited for; matrix products, arithmetic and copies ran while one was open for 16% of the time, Pallas kernels for 11%

profile of v3, /device:TPU:0, one launch (start us, length us, event | category | flops | bytes accessed | tf_op | source)
XLA Modules:
  0.0 134.9 jit_solution(16557860113071286626)
XLA Ops:
  0.7 2.3 %dynamic-slice_bitcast_fusion = (bf16[320,1024]{1,0:T(8,128)(2,1)S(1)}, bf16[320,1024]{1,0:T(8,128)(2,1)}) fusion(bf16[2048,320]{0,1:T(8,128)(2,1)} %param.9, s32[]{:T(128)S(6)} %select_n.44, s32[]{:T(128)S(6)} %select_n.43), kind=kLoop, calls=%fused_computation.12 | loop fusion | bytes 2621448 | tf_op jit(solution)/shard_map/dynamic_slice | solution.py:301
  3.1 3.0 %collective-permute-start.1 = (bf16[320,1024]{1,0:T(8,128)(2,1)S(1)}, bf16[320,1024]{1,0:T(8,128)(2,1)}, u32[]{:S(2)}, u32[]{:S(2)}) collective-permute-start(bf16[320,1024]{1,0:T(8,128)(2,1)S(1)} %get-tuple-element.75.refs_0_), channel_id=1, source_target_pairs={{0,8},{4,12},{8,0},{12,4},{16,24},{20,28},{24,16},{28,20},{1,9},{5... | collective-permute-start | bytes 1966088 | tf_op jit(solution)/shard_map/ppermute | solution.py:287
  6.1 0.7 collective-permute-start.2
  6.8 1.6 %collective-permute-start = (bf16[320,1024]{1,0:T(8,128)(2,1)}, bf16[320,1024]{1,0:T(8,128)(2,1)}, u32[]{:S(2)}, u32[]{:S(2)}) collective-permute-start(bf16[320,1024]{1,0:T(8,128)(2,1)} %get-tuple-element.76), channel_id=1, source_target_pairs={{0,4},{4,0},{8,12},{12,8},{16,20},{20,16},{24,28},{28,24},{1,5},{5... | collective-permute-start | bytes 1966088 | tf_op jit(solution)/shard_map/ppermute | solution.py:290
  8.5 0.7 reduce-precision_convert_fusion.1
  9.5 0.7 fusion
  10.6 12.8 %collective-permute-done.refs_1_ = bf16[320,1024]{1,0:T(8,128)(2,1)} collective-permute-done((bf16[320,1024]{1,0:T(8,128)(2,1)}, bf16[320,1024]{1,0:T(8,128)(2,1)}, u32[]{:S(2)}, u32[]{:S(2)}) %collective-permute-start) | collective-permute-done | bytes 655392 | tf_op jit(solution)/shard_map/ppermute | solution.py:290
  23.4 0.8 copy-done.13
  24.2 1.5 %collective-permute-start.3 = (bf16[144,2560]{1,0:T(8,128)(2,1)S(1)}, bf16[144,2560]{1,0:T(8,128)(2,1)S(1)}, u32[]{:S(2)}, u32[]{:S(2)}) collective-permute-start(bf16[144,2560]{1,0:T(8,128)(2,1)S(1)} %pad_maximum_fusion.1.refs_0_), channel_id=1, source_target_pairs={{0,2},{1,3},{2,0},{3,1},{4,6},{5,7},{6,4},{7,5},{8,10},{9,11},{10,... | collective-permute-start | bytes 2211848 | tf_op jit(solution)/shard_map/ppermute | solution.py:293
  25.7 1.5 %collective-permute-start.4 = (bf16[144,2560]{1,0:T(8,128)(2,1)S(1)}, bf16[144,2560]{1,0:T(8,128)(2,1)S(1)}, u32[]{:S(2)}, u32[]{:S(2)}) collective-permute-start(bf16[144,2560]{1,0:T(8,128)(2,1)S(1)} %pad_maximum_fusion.1.refs_0_), channel_id=1, source_target_pairs={{0,4},{4,0},{8,12},{12,8},{16,20},{20,16},{24,28},{28,24},{1,5},{5... | collective-permute-start | bytes 2211848 | tf_op jit(solution)/shard_map/ppermute | solution.py:290
  27.2 4.1 %collective-permute-start.5 = (bf16[320,1024]{1,0:T(8,128)(2,1)}, bf16[320,1024]{1,0:T(8,128)(2,1)}, u32[]{:S(2)}, u32[]{:S(2)}) collective-permute-start(bf16[320,1024]{1,0:T(8,128)(2,1)} %collective-permute-done.refs_1_), channel_id=1, source_target_pairs={{0,8},{4,12},{8,0},{12,4},{16,24},{20,28},{24,16},{28,20},{1,9},{5... | collective-permute-start | bytes 1966088 | tf_op jit(solution)/shard_map/ppermute | solution.py:287
  31.3 1.5 %collective-permute-start.6 = (bf16[320,1024]{1,0:T(8,128)(2,1)}, bf16[320,1024]{1,0:T(8,128)(2,1)}, u32[]{:S(2)}, u32[]{:S(2)}) collective-permute-start(bf16[320,1024]{1,0:T(8,128)(2,1)} %collective-permute-done.refs_1_), channel_id=1, source_target_pairs={{8,16},{12,20},{16,8},{20,12},{9,17},{13,21},{17,9},{21,13},{10,18... | collective-permute-start | bytes 1966088 | tf_op jit(solution)/shard_map/ppermute | solution.py:287
  32.8 1.5 %collective-permute-start.7 = (bf16[320,1024]{1,0:T(8,128)(2,1)}, bf16[320,1024]{1,0:T(8,128)(2,1)}, u32[]{:S(2)}, u32[]{:S(2)}) collective-permute-start(bf16[320,1024]{1,0:T(8,128)(2,1)} %collective-permute-done.1.refs_2_), channel_id=1, source_target_pairs={{8,16},{12,20},{16,8},{20,12},{9,17},{13,21},{17,9},{21,13},{10,18... | collective-permute-start | bytes 1966088 | tf_op jit(solution)/shard_map/ppermute | solution.py:287
  34.3 6.9 %collective-permute-done.3.refs_2_ = bf16[144,2560]{1,0:T(8,128)(2,1)S(1)} collective-permute-done((bf16[144,2560]{1,0:T(8,128)(2,1)S(1)}, bf16[144,2560]{1,0:T(8,128)(2,1)S(1)}, u32[]{:S(2)}, u32[]{:S(2)}) %collective-permute-start.3) | collective-permute-done | bytes 737312 | tf_op jit(solution)/shard_map/ppermute | solution.py:293
  41.3 1.3 collective-permute-start.8
  42.7 1.6 %collective-permute-done.5.refs_3_ = bf16[320,1024]{1,0:T(8,128)(2,1)} collective-permute-done((bf16[320,1024]{1,0:T(8,128)(2,1)}, bf16[320,1024]{1,0:T(8,128)(2,1)}, u32[]{:S(2)}, u32[]{:S(2)}) %collective-permute-start.5) | collective-permute-done | bytes 655392 | tf_op jit(solution)/shard_map/ppermute | solution.py:287
  44.3 14.8 %collective-permute-done.8.refs_2_ = bf16[320,1024]{1,0:T(8,128)(2,1)} collective-permute-done((bf16[320,1024]{1,0:T(8,128)(2,1)}, bf16[320,1024]{1,0:T(8,128)(2,1)}, u32[]{:S(2)}, u32[]{:S(2)}) %collective-permute-start.8) | collective-permute-done | bytes 655392 | tf_op jit(solution)/shard_map/ppermute | solution.py:287
  59.1 0.7 collective-permute-start.9
  59.8 1.3 collective-permute-start.10
  61.1 1.6 %collective-permute-start.11 = (bf16[144,2560]{1,0:T(8,128)(2,1)S(1)}, bf16[144,2560]{1,0:T(8,128)(2,1)}, u32[]{:S(2)}, u32[]{:S(2)}) collective-permute-start(bf16[144,2560]{1,0:T(8,128)(2,1)S(1)} %collective-permute-done.4.refs_4_.refs_0_), channel_id=1, source_target_pairs={{0,2},{1,3},{2,0},{3,1},{4,6},{5,7},{6,4},{7,5},{8,10},{9,11},{10,... | collective-permute-start | bytes 2211848 | tf_op jit(solution)/shard_map/ppermute | solution.py:293
  62.7 1.2 fusion.61
  63.9 1.7 %block_rows.2 = bf16[1280,1024]{1,0:T(8,128)(2,1)S(1)} custom-call(s32[2]{0:T(128)S(1)} %pad_add_fusion.place, bf16[320,1024]{1,0:T(8,128)(2,1)S(1)} %get-tuple-element.75.refs_0_, bf16[320,1024]{1,0:T(8,128)(2,1)} %collective-permute-done.refs_1_, bf16[320,1024]{1,0:T(8,128)(2,1)} %collective-permute-done.1.refs_2_, ...), custom_call_target="tpu_custom_call" | custom-call | tf_op jit(solution)/shard_map/block_rows/pallas_call | solution.py:173
  65.7 1.8 %pad_maximum_fusion = bf16[3,144,2560]{2,1,0:T(8,128)(2,1)} fusion(bf16[1,144,2560]{2,1,0:T(8,128)(2,1)S(1)} %bitcast.64, bf16[1,144,2560]{2,1,0:T(8,128)(2,1)S(1)} %bitcast.65, bf16[1,144,2560]{2,1,0:T(8,128)(2,1)S(1)} %fusion.61), kind=kLoop, calls=%fused_computation.3 | loop fusion | flops 2211840 | bytes 4423680 | tf_op jit(solution)/shard_map/stack | solution.py:341
  67.8 0.8 copy-done.11
  68.7 9.1 %collective-permute-done.10.refs_3_ = bf16[320,1024]{1,0:T(8,128)(2,1)S(1)} collective-permute-done((bf16[320,1024]{1,0:T(8,128)(2,1)}, bf16[320,1024]{1,0:T(8,128)(2,1)S(1)}, u32[]{:S(2)}, u32[]{:S(2)}) %collective-permute-start.10) | collective-permute-done | bytes 655392 | tf_op jit(solution)/shard_map/ppermute | solution.py:287
  77.8 0.9 copy-done.15
  79.2 0.6 add_convert_fusion
  79.7 1.1 copy-done.12
  80.8 2.2 %slice_rows.1 = (bf16[640,512]{1,0:T(8,128)(2,1)}, bf16[640,256]{1,0:T(8,128)(2,1)}, bf16[640,256]{1,0:T(8,128)(2,1)}) custom-call(bf16[320,1024]{1,0:T(8,128)(2,1)} %collective-permute-done.7.upper, bf16[320,1024]{1,0:T(8,128)(2,1)S(1)} %copy-done.12), custom_call_target="tpu_custom_call" | custom-call | tf_op jit(solution)/shard_map/slice_rows/pallas_call | solution.py:138
  83.0 1.3 collective-permute-start.14
  84.3 1.3 collective-permute-start.16
  85.6 1.3 collective-permute-start.18
  86.9 1.7 %copy-done.8 = bf16[144,2560]{1,0:T(8,128)(2,1)S(1)} copy-done((bf16[144,2560]{1,0:T(8,128)(2,1)S(1)}, bf16[144,2560]{1,0:T(8,128)(2,1)}, u32[]{:S(2)}) %copy-start.8) | copy-done | bytes 737304
  89.0 1.0 copy-done.17
  90.1 0.8 copy-done.19
  90.9 1.6 %frame_lines.1 = f32[2,4,640]{2,1,0:T(4,128)} custom-call(s32[1]{0:T(128)} %bitcast.1.place, bf16[144,2560]{1,0:T(8,128)(2,1)} %copy-done.3, bf16[3,144,2560]{2,1,0:T(8,128)(2,1)} %copy-done.1, bf16[144,2560]{1,0:T(8,128)(2,1)} %copy-done.7, bf16[3,144,2560]{2,1,0:T(8,128)(2,1)} %copy-done.1, bf16[144,2560]{1,0:T(8,128)(2,1)} %copy-done.5, ...), custom_call_target="tpu_custom_call" | custom-call | tf_op jit(solution)/shard_map/frame_lines/pallas_call | solution.py:94
  92.6 1.5 %block_rows.3 = bf16[640,1024]{1,0:T(8,128)(2,1)S(1)} custom-call(s32[2]{0:T(128)S(1)} %pad_add_fusion.place, bf16[320,1024]{1,0:T(8,128)(2,1)S(1)} %copy-done.14, bf16[320,1024]{1,0:T(8,128)(2,1)} %collective-permute-done.6.refs_1_, bf16[320,1024]{1,0:T(8,128)(2,1)} %collective-permute-done.8.refs_2_, bf16[320,1024]{1,0:T(8,128)(2,1)S(1)} %copy-done.16), custom_call_target="tpu_custom_call" | custom-call | tf_op jit(solution)/shard_map/block_rows/pallas_call | solution.py:173
  94.1 1.0 fusion.29
  95.1 0.7 copy-done.10
  96.2 1.6 %convolution_add_fusion.2 = f32[512,1024]{1,0:T(8,128)S(1)} fusion(f32[512,1024]{1,0:T(8,128)S(1)} %fusion.29, bf16[512,1280]{1,0:T(8,128)(2,1)S(1)} %copy-done.18, bf16[1280,1024]{1,0:T(8,128)(2,1)S(1)} %copy-done.10), kind=kOutput, calls=%fused_computation.6 | convolution fusion | flops 1342701568 | bytes 8126464 | tf_op jit(solution)/shard_map/dot_general | solution.py:354
  98.0 2.1 %order_pieces.3 = (bf16[512,1280]{1,0:T(8,128)(2,1)S(1)}, bf16[512,640]{1,0:T(8,128)(2,1)S(1)}, bf16[512,640]{1,0:T(8,128)(2,1)S(1)}) custom-call(s32[1]{0:T(128)} %bitcast.1.place, bf16[144,2560]{1,0:T(8,128)(2,1)S(1)} %copy-done.6, bf16[3,144,2560]{2,1,0:T(8,128)(2,1)S(1)} %copy-done.2, bf16[144,2560]{1,0:T(8,128)(2,1)} %collective-permute-done.11.refs_6_.refs_2_, ...), custom_call_target="tpu_custom_call" | custom-call | tf_op jit(solution)/shard_map/order_pieces/pallas_call | solution.py:228
  100.1 1.0 fusion.30
  101.1 1.6 %convolution_add_fusion.1 = f32[512,1024]{1,0:T(8,128)S(1)} fusion(f32[512,1024]{1,0:T(8,128)S(1)} %fusion.30, bf16[512,1280]{1,0:T(8,128)(2,1)S(1)} %get-tuple-element.47, bf16[1280,1024]{1,0:T(8,128)(2,1)S(1)} %copy-done.10), kind=kOutput, calls=%fused_computation.5 | convolution fusion | flops 1342701568 | bytes 8126464 | tf_op jit(solution)/shard_map/dot_general | solution.py:354
  102.8 1.3 last_rows.4
  104.5 1.3 last_rows.5
  105.8 1.2 fusion.8
  107.5 4.8 %collective-permute-start.15 = (f32[2,4,640]{2,1,0:T(4,128)S(1)}, f32[2,4,640]{2,1,0:T(4,128)S(1)}, u32[]{:S(2)}, u32[]{:S(2)}) collective-permute-start(f32[2,4,640]{2,1,0:T(4,128)S(1)} %copy-done.29), channel_id=1, source_target_pairs={{0,8},{4,12},{8,0},{12,4},{16,24},{20,28},{24,16},{28,20},{1,9},{5... | collective-permute-start | bytes 61448 | tf_op jit(solution)/shard_map/ppermute | solution.py:109
  112.7 1.6 %collective-permute-start.21 = (bf16[512,256]{1,0:T(8,128)(2,1)}, bf16[512,256]{1,0:T(8,128)(2,1)S(1)}, u32[]{:S(2)}, u32[]{:S(2)}) collective-permute-start(bf16[512,256]{1,0:T(8,128)(2,1)} %get-tuple-element.73), channel_id=1, source_target_pairs={{0,4},{4,0},{8,12},{12,8},{16,20},{20,16},{24,28},{28,24},{1,5},{5... | collective-permute-start | bytes 786440 | tf_op jit(solution)/shard_map/ppermute | solution.py:290
  114.3 2.2 %collective-permute-done.15 = f32[2,4,640]{2,1,0:T(4,128)S(1)} collective-permute-done((f32[2,4,640]{2,1,0:T(4,128)S(1)}, f32[2,4,640]{2,1,0:T(4,128)S(1)}, u32[]{:S(2)}, u32[]{:S(2)}) %collective-permute-start.15) | collective-permute-done | bytes 20512 | tf_op jit(solution)/shard_map/ppermute | solution.py:109
  116.5 1.1 last_rows.6
  117.6 1.1 fusion.9
  119.4 0.6 copy.12
  120.0 1.5 %collective-permute-start.19 = (bf16[512,256]{1,0:T(8,128)(2,1)}, bf16[512,256]{1,0:T(8,128)(2,1)S(1)}, u32[]{:S(2)}, u32[]{:S(2)}) collective-permute-start(bf16[512,256]{1,0:T(8,128)(2,1)} %fusion.9), channel_id=1, source_target_pairs={{0,4},{4,0},{8,12},{12,8},{16,20},{20,16},{24,28},{28,24},{1,5},{5... | collective-permute-start | bytes 786440 | tf_op jit(solution)/shard_map/ppermute | solution.py:290
  121.5 2.2 %collective-permute-done.17 = f32[4,4,640]{2,1,0:T(4,128)S(1)} collective-permute-done((f32[4,4,640]{2,1,0:T(4,128)S(1)}, f32[4,4,640]{2,1,0:T(4,128)S(1)}, u32[]{:S(2)}, u32[]{:S(2)}) %collective-permute-start.17) | collective-permute-done | bytes 40992 | tf_op jit(solution)/shard_map/ppermute | solution.py:109
  123.7 1.1 last_rows.7
  125.2 1.0 collective-permute-start.20
  126.2 0.6 slice_reduce_fusion
  126.8 1.2 fusion.33
  128.0 0.7 reshape.42
  128.6 0.8 eq.71
  129.4 1.6 %fusion.24 = f32[8,640]{1,0:T(8,128)} fusion(f32[24,640]{1,0:T(8,128)} %reshape.42, f32[24]{0:T(128)S(1)} %eq.71, f32[8]{0:T(128)} %add_convert_fusion), kind=kOutput, calls=%fused_computation.50 | convolution fusion | flops 1474752 | bytes 82048 | tf_op jit(solution)/shard_map/dot_general | solution.py:121
  131.0 1.8 %fusion.5 = (bf16[512,256]{1,0:T(8,128)(2,1)S(1)}, bf16[512,256]{1,0:T(8,128)(2,1)S(1)}) fusion(f32[512,1024]{1,0:T(8,128)} %copy-done.28, f32[512,256]{1,0:T(8,128)} %fusion.33, bf16[512,640]{1,0:T(8,128)(2,1)S(1)} %get-tuple-element.61, bf16[640,256]{1,0:T(8,128)(2,1)S(1)} %last_rows.7), kind=kOutput, calls=%fused_computation.15 | convolution fusion | flops 168296448 | bytes 3080192 | tf_op jit(solution)/shard_map/dot_general | solution.py:380
  132.8 1.0 place_columns.2.refs_4_
  133.9 1.0 place_columns.3
  (95 shorter events, 5.0 us)
Async XLA Ops:
  0.6 8.5 %copy-start = (f32[64,2560]{1,0:T(8,128)S(1)}, f32[64,2560]{1,0:T(8,128)}, u32[]{:S(2)}) copy-start(f32[64,2560]{1,0:T(8,128)} %param.11) | copy-start | bytes 1966084
  0.6 7.7 %copy-start.32 = (s32[1,3]{1,0:T(1,128)S(1)}, s32[1,3]{1,0:T(1,128)}, u32[]{:S(2)}) copy-start(s32[1,3]{1,0:T(1,128)} %param.13) | copy-start | bytes 40
  0.7 7.8 %copy-start.27 = (bf16[1,128,2560]{2,1,0:T(8,128)(2,1)S(1)}, bf16[1,128,2560]{2,1,0:T(8,128)(2,1)}, u32[]{:S(2)}) copy-start(bf16[1,128,2560]{2,1,0:T(8,128)(2,1)} %param.8) | copy-start | bytes 1966084
  0.7 7.8 %copy-start.21 = (bf16[1,128,2560]{2,1,0:T(8,128)(2,1)S(1)}, bf16[1,128,2560]{2,1,0:T(8,128)(2,1)}, u32[]{:S(2)}) copy-start(bf16[1,128,2560]{2,1,0:T(8,128)(2,1)} %param.7) | copy-start | bytes 1966084
  0.7 7.8 %copy-start.31 = (s32[1,128]{1,0:T(1,128)S(1)}, s32[1,128]{1,0:T(1,128)}, u32[]{:S(2)}) copy-start(s32[1,128]{1,0:T(1,128)} %param.12) | copy-start | bytes 1540
  0.7 8.5 %copy-start.30 = (f32[2560]{0:T(1024)S(1)}, f32[2560]{0:T(1024)}, u32[]{:S(2)}) copy-start(f32[2560]{0:T(1024)} %param.10) | copy-start | bytes 30724
  3.1 20.3 %collective-permute-start.1 = (bf16[320,1024]{1,0:T(8,128)(2,1)S(1)}, bf16[320,1024]{1,0:T(8,128)(2,1)}, u32[]{:S(2)}, u32[]{:S(2)}) collective-permute-start(bf16[320,1024]{1,0:T(8,128)(2,1)S(1)} %get-tuple-element.75.refs_0_), channel_id=1, source_target_pairs={{0,8},{4,12},{8,0},{12,4},{16,24},{20,28},{24,16},{28,20},{1,9},{5... | collective-permute-start | bytes 1966088 | tf_op jit(solution)/shard_map/ppermute | solution.py:287
  6.1 17.3 %collective-permute-start.2 = (bf16[320,1024]{1,0:T(8,128)(2,1)S(1)}, bf16[320,1024]{1,0:T(8,128)(2,1)S(1)}, u32[]{:S(2)}, u32[]{:S(2)}) collective-permute-start(bf16[320,1024]{1,0:T(8,128)(2,1)S(1)} %get-tuple-element.75.refs_0_), channel_id=1, source_target_pairs={{8,16},{12,20},{16,8},{20,12},{9,17},{13,21},{17,9},{21,13},{10,18... | collective-permute-start | bytes 1966088 | tf_op jit(solution)/shard_map/ppermute | solution.py:287
  6.8 16.6 %collective-permute-start = (bf16[320,1024]{1,0:T(8,128)(2,1)}, bf16[320,1024]{1,0:T(8,128)(2,1)}, u32[]{:S(2)}, u32[]{:S(2)}) collective-permute-start(bf16[320,1024]{1,0:T(8,128)(2,1)} %get-tuple-element.76), channel_id=1, source_target_pairs={{0,4},{4,0},{8,12},{12,8},{16,20},{20,16},{24,28},{28,24},{1,5},{5... | collective-permute-start | bytes 1966088 | tf_op jit(solution)/shard_map/ppermute | solution.py:290
  10.4 30.9 %copy-start.22 = (bf16[128,640]{1,0:T(8,128)(2,1)}, bf16[128,640]{1,0:T(8,128)(2,1)S(1)}, u32[]{:S(2)}) copy-start(bf16[128,640]{1,0:T(8,128)(2,1)S(1)} %get-tuple-element.77) | copy-start | bytes 491524
  10.4 30.9 %copy-start.23 = (bf16[128,640]{1,0:T(8,128)(2,1)}, bf16[128,640]{1,0:T(8,128)(2,1)S(1)}, u32[]{:S(2)}) copy-start(bf16[128,640]{1,0:T(8,128)(2,1)S(1)} %get-tuple-element.78) | copy-start | bytes 491524
  10.4 30.9 %copy-start.24 = (bf16[128,640]{1,0:T(8,128)(2,1)}, bf16[128,640]{1,0:T(8,128)(2,1)S(1)}, u32[]{:S(2)}) copy-start(bf16[128,640]{1,0:T(8,128)(2,1)S(1)} %get-tuple-element.79) | copy-start | bytes 491524
  10.4 30.9 %copy-start.25 = (bf16[128,640]{1,0:T(8,128)(2,1)}, bf16[128,640]{1,0:T(8,128)(2,1)S(1)}, u32[]{:S(2)}) copy-start(bf16[128,640]{1,0:T(8,128)(2,1)S(1)} %get-tuple-element.80) | copy-start | bytes 491524
  10.5 30.8 %copy-start.26 = (bf16[16,2560]{1,0:T(8,128)(2,1)}, bf16[16,2560]{1,0:T(8,128)(2,1)S(1)}, u32[]{:S(2)}) copy-start(bf16[16,2560]{1,0:T(8,128)(2,1)S(1)} %fusion.19) | copy-start | bytes 245764
  10.6 55.0 %copy-start.3 = (bf16[144,2560]{1,0:T(8,128)(2,1)}, bf16[144,2560]{1,0:T(8,128)(2,1)S(1)}, u32[]{:S(2)}) copy-start(bf16[144,2560]{1,0:T(8,128)(2,1)S(1)} %pad_maximum_fusion.1.refs_0_) | copy-start | bytes 2211844
  23.4 0.8 copy-start.13
  24.2 17.0 %collective-permute-start.3 = (bf16[144,2560]{1,0:T(8,128)(2,1)S(1)}, bf16[144,2560]{1,0:T(8,128)(2,1)S(1)}, u32[]{:S(2)}, u32[]{:S(2)}) collective-permute-start(bf16[144,2560]{1,0:T(8,128)(2,1)S(1)} %pad_maximum_fusion.1.refs_0_), channel_id=1, source_target_pairs={{0,2},{1,3},{2,0},{3,1},{4,6},{5,7},{6,4},{7,5},{8,10},{9,11},{10,... | collective-permute-start | bytes 2211848 | tf_op jit(solution)/shard_map/ppermute | solution.py:293
  25.7 35.4 %collective-permute-start.4 = (bf16[144,2560]{1,0:T(8,128)(2,1)S(1)}, bf16[144,2560]{1,0:T(8,128)(2,1)S(1)}, u32[]{:S(2)}, u32[]{:S(2)}) collective-permute-start(bf16[144,2560]{1,0:T(8,128)(2,1)S(1)} %pad_maximum_fusion.1.refs_0_), channel_id=1, source_target_pairs={{0,4},{4,0},{8,12},{12,8},{16,20},{20,16},{24,28},{28,24},{1,5},{5... | collective-permute-start | bytes 2211848 | tf_op jit(solution)/shard_map/ppermute | solution.py:290
  27.2 17.1 %collective-permute-start.5 = (bf16[320,1024]{1,0:T(8,128)(2,1)}, bf16[320,1024]{1,0:T(8,128)(2,1)}, u32[]{:S(2)}, u32[]{:S(2)}) collective-permute-start(bf16[320,1024]{1,0:T(8,128)(2,1)} %collective-permute-done.refs_1_), channel_id=1, source_target_pairs={{0,8},{4,12},{8,0},{12,4},{16,24},{20,28},{24,16},{28,20},{1,9},{5... | collective-permute-start | bytes 1966088 | tf_op jit(solution)/shard_map/ppermute | solution.py:287
  31.3 13.0 %collective-permute-start.6 = (bf16[320,1024]{1,0:T(8,128)(2,1)}, bf16[320,1024]{1,0:T(8,128)(2,1)}, u32[]{:S(2)}, u32[]{:S(2)}) collective-permute-start(bf16[320,1024]{1,0:T(8,128)(2,1)} %collective-permute-done.refs_1_), channel_id=1, source_target_pairs={{8,16},{12,20},{16,8},{20,12},{9,17},{13,21},{17,9},{21,13},{10,18... | collective-permute-start | bytes 1966088 | tf_op jit(solution)/shard_map/ppermute | solution.py:287
  32.8 11.5 %collective-permute-start.7 = (bf16[320,1024]{1,0:T(8,128)(2,1)}, bf16[320,1024]{1,0:T(8,128)(2,1)}, u32[]{:S(2)}, u32[]{:S(2)}) collective-permute-start(bf16[320,1024]{1,0:T(8,128)(2,1)} %collective-permute-done.1.refs_2_), channel_id=1, source_target_pairs={{8,16},{12,20},{16,8},{20,12},{9,17},{13,21},{17,9},{21,13},{10,18... | collective-permute-start | bytes 1966088 | tf_op jit(solution)/shard_map/ppermute | solution.py:287
  41.3 24.3 %copy-start.7 = (bf16[144,2560]{1,0:T(8,128)(2,1)}, bf16[144,2560]{1,0:T(8,128)(2,1)S(1)}, u32[]{:S(2)}) copy-start(bf16[144,2560]{1,0:T(8,128)(2,1)S(1)} %collective-permute-done.3.refs_2_) | copy-start | bytes 2211844
  41.3 17.8 %collective-permute-start.8 = (bf16[320,1024]{1,0:T(8,128)(2,1)}, bf16[320,1024]{1,0:T(8,128)(2,1)}, u32[]{:S(2)}, u32[]{:S(2)}) collective-permute-start(bf16[320,1024]{1,0:T(8,128)(2,1)} %copy-done.13), channel_id=1, source_target_pairs={{8,0},{12,4},{16,24},{20,28},{9,1},{13,5},{17,25},{21,29},{10,2},{... | collective-permute-start | bytes 1966088 | tf_op jit(solution)/shard_map/ppermute | solution.py:287
  59.1 8.7 %collective-permute-start.9 = (bf16[320,1024]{1,0:T(8,128)(2,1)}, bf16[320,1024]{1,0:T(8,128)(2,1)S(1)}, u32[]{:S(2)}, u32[]{:S(2)}) collective-permute-start(bf16[320,1024]{1,0:T(8,128)(2,1)} %collective-permute-done.5.refs_3_), channel_id=1, source_target_pairs={{8,16},{12,20},{16,8},{20,12},{9,17},{13,21},{17,9},{21,13},{10,18... | collective-permute-start | bytes 1966088 | tf_op jit(solution)/shard_map/ppermute | solution.py:287
  59.8 17.9 %collective-permute-start.10 = (bf16[320,1024]{1,0:T(8,128)(2,1)}, bf16[320,1024]{1,0:T(8,128)(2,1)S(1)}, u32[]{:S(2)}, u32[]{:S(2)}) collective-permute-start(bf16[320,1024]{1,0:T(8,128)(2,1)} %collective-permute-done.6.refs_1_), channel_id=1, source_target_pairs={{8,0},{12,4},{16,24},{20,28},{9,1},{13,5},{17,25},{21,29},{10,2},{... | collective-permute-start | bytes 1966088 | tf_op jit(solution)/shard_map/ppermute | solution.py:287
  61.1 4.5 %copy-start.5 = (bf16[144,2560]{1,0:T(8,128)(2,1)}, bf16[144,2560]{1,0:T(8,128)(2,1)S(1)}, u32[]{:S(2)}) copy-start(bf16[144,2560]{1,0:T(8,128)(2,1)S(1)} %collective-permute-done.4.refs_4_.refs_0_) | copy-start | bytes 2211844
  61.1 17.5 %collective-permute-start.11 = (bf16[144,2560]{1,0:T(8,128)(2,1)S(1)}, bf16[144,2560]{1,0:T(8,128)(2,1)}, u32[]{:S(2)}, u32[]{:S(2)}) collective-permute-start(bf16[144,2560]{1,0:T(8,128)(2,1)S(1)} %collective-permute-done.4.refs_4_.refs_0_), channel_id=1, source_target_pairs={{0,2},{1,3},{2,0},{3,1},{4,6},{5,7},{6,4},{7,5},{8,10},{9,11},{10,... | collective-permute-start | bytes 2211848 | tf_op jit(solution)/shard_map/ppermute | solution.py:293
  65.6 2.2 %copy-start.9 = (bf16[1280,1024]{1,0:T(8,128)(2,1)}, bf16[1280,1024]{1,0:T(8,128)(2,1)S(1)}, u32[]{:S(2)}) copy-start(bf16[1280,1024]{1,0:T(8,128)(2,1)S(1)} %block_rows.2) | copy-start | bytes 7864324
  67.8 0.8 copy-start.11
  77.7 0.9 copy-start.15
  78.6 8.2 %collective-permute-start.12 = (bf16[3,144,2560]{2,1,0:T(8,128)(2,1)}, bf16[3,144,2560]{2,1,0:T(8,128)(2,1)S(1)}, u32[]{:S(2)}, u32[]{:S(2)}) collective-permute-start(bf16[3,144,2560]{2,1,0:T(8,128)(2,1)} %pad_maximum_fusion), channel_id=1, source_target_pairs={{0,1},{1,0},{2,3},{3,2},{4,5},{5,4},{6,7},{7,6},{8,9},{9,8},{10,11... | collective-permute-start | bytes 6635528 | tf_op jit(solution)/shard_map/ppermute | solution.py:293
  78.6 12.3 %collective-permute-start.13 = (bf16[144,2560]{1,0:T(8,128)(2,1)}, bf16[144,2560]{1,0:T(8,128)(2,1)}, u32[]{:S(2)}, u32[]{:S(2)}) collective-permute-start(bf16[144,2560]{1,0:T(8,128)(2,1)} %collective-permute-done.11.refs_6_.refs_2_), channel_id=1, source_target_pairs={{0,1},{1,0},{2,3},{3,2},{4,5},{5,4},{6,7},{7,6},{8,9},{9,8},{10,11... | collective-permute-start | bytes 2211848 | tf_op jit(solution)/shard_map/ppermute | solution.py:293
  79.2 7.7 %copy-start.4 = (bf16[144,2560]{1,0:T(8,128)(2,1)S(1)}, bf16[144,2560]{1,0:T(8,128)(2,1)}, u32[]{:S(2)}) copy-start(bf16[144,2560]{1,0:T(8,128)(2,1)} %copy-done.3) | copy-start | bytes 2211844
  79.7 1.1 copy-start.12
  83.0 19.8 %collective-permute-start.14 = (bf16[640,512]{1,0:T(8,128)(2,1)}, bf16[640,512]{1,0:T(8,128)(2,1)}, u32[]{:S(2)}, u32[]{:S(2)}) collective-permute-start(bf16[640,512]{1,0:T(8,128)(2,1)} %get-tuple-element.54.sent), channel_id=1, source_target_pairs={{8,0},{12,4},{16,24},{20,28},{9,1},{13,5},{17,25},{21,29},{10,2},{... | collective-permute-start | bytes 1966088 | tf_op jit(solution)/shard_map/ppermute | solution.py:287
  84.3 32.2 %collective-permute-start.16 = (bf16[640,256]{1,0:T(8,128)(2,1)}, bf16[640,256]{1,0:T(8,128)(2,1)}, u32[]{:S(2)}, u32[]{:S(2)}) collective-permute-start(bf16[640,256]{1,0:T(8,128)(2,1)} %get-tuple-element.57.sent), channel_id=1, source_target_pairs={{8,0},{12,4},{16,24},{20,28},{9,1},{13,5},{17,25},{21,29},{10,2},{... | collective-permute-start | bytes 983048 | tf_op jit(solution)/shard_map/ppermute | solution.py:287
  85.6 38.1 %collective-permute-start.18 = (bf16[640,256]{1,0:T(8,128)(2,1)}, bf16[640,256]{1,0:T(8,128)(2,1)}, u32[]{:S(2)}, u32[]{:S(2)}) collective-permute-start(bf16[640,256]{1,0:T(8,128)(2,1)} %get-tuple-element.60.sent), channel_id=1, source_target_pairs={{8,0},{12,4},{16,24},{20,28},{9,1},{13,5},{17,25},{21,29},{10,2},{... | collective-permute-start | bytes 983048 | tf_op jit(solution)/shard_map/ppermute | solution.py:287
  86.9 2.1 %copy-start.1 = (bf16[3,144,2560]{2,1,0:T(8,128)(2,1)}, bf16[3,144,2560]{2,1,0:T(8,128)(2,1)S(1)}, u32[]{:S(2)}) copy-start(bf16[3,144,2560]{2,1,0:T(8,128)(2,1)S(1)} %collective-permute-done.12.refs_1_.refs_3_.refs_5_) | copy-start | bytes 6635524
  86.9 1.7 %copy-start.8 = (bf16[144,2560]{1,0:T(8,128)(2,1)S(1)}, bf16[144,2560]{1,0:T(8,128)(2,1)}, u32[]{:S(2)}) copy-start(bf16[144,2560]{1,0:T(8,128)(2,1)} %copy-done.7) | copy-start | bytes 2211844
  89.0 1.1 copy-start.17
  90.1 0.8 copy-start.19
  90.9 1.7 %copy-start.14 = (bf16[320,1024]{1,0:T(8,128)(2,1)S(1)}, bf16[320,1024]{1,0:T(8,128)(2,1)}, u32[]{:S(2)}) copy-start(bf16[320,1024]{1,0:T(8,128)(2,1)} %copy-done.13) | copy-start | bytes 1966084
  90.9 1.7 %copy-start.16 = (bf16[320,1024]{1,0:T(8,128)(2,1)S(1)}, bf16[320,1024]{1,0:T(8,128)(2,1)}, u32[]{:S(2)}) copy-start(bf16[320,1024]{1,0:T(8,128)(2,1)} %copy-done.15) | copy-start | bytes 1966084
  92.6 1.5 %copy-start.20 = (bf16[512,640]{1,0:T(8,128)(2,1)S(1)}, bf16[512,640]{1,0:T(8,128)(2,1)}, u32[]{:S(2)}) copy-start(bf16[512,640]{1,0:T(8,128)(2,1)} %copy-done.19) | copy-start | bytes 1966084
  94.1 1.7 %copy-start.10 = (bf16[1280,1024]{1,0:T(8,128)(2,1)S(1)}, bf16[1280,1024]{1,0:T(8,128)(2,1)}, u32[]{:S(2)}) copy-start(bf16[1280,1024]{1,0:T(8,128)(2,1)} %copy-done.9) | copy-start | bytes 7864324
  94.1 2.1 %copy-start.18 = (bf16[512,1280]{1,0:T(8,128)(2,1)S(1)}, bf16[512,1280]{1,0:T(8,128)(2,1)}, u32[]{:S(2)}) copy-start(bf16[512,1280]{1,0:T(8,128)(2,1)} %copy-done.17) | copy-start | bytes 3932164
  96.2 1.6 %copy-start.2 = (bf16[3,144,2560]{2,1,0:T(8,128)(2,1)S(1)}, bf16[3,144,2560]{2,1,0:T(8,128)(2,1)}, u32[]{:S(2)}) copy-start(bf16[3,144,2560]{2,1,0:T(8,128)(2,1)} %copy-done.1) | copy-start | bytes 6635524
  96.2 1.8 %copy-start.6 = (bf16[144,2560]{1,0:T(8,128)(2,1)S(1)}, bf16[144,2560]{1,0:T(8,128)(2,1)}, u32[]{:S(2)}) copy-start(bf16[144,2560]{1,0:T(8,128)(2,1)} %copy-done.5) | copy-start | bytes 2211844
  98.0 21.0 %copy-start.28 = (f32[512,1024]{1,0:T(8,128)}, f32[512,1024]{1,0:T(8,128)S(1)}, u32[]{:S(2)}) copy-start(f32[512,1024]{1,0:T(8,128)S(1)} %convolution_add_fusion.2) | copy-start | bytes 6291460
  105.8 1.7 %copy-start.29 = (f32[2,4,640]{2,1,0:T(4,128)S(1)}, f32[2,4,640]{2,1,0:T(4,128)}, u32[]{:S(2)}) copy-start(f32[2,4,640]{2,1,0:T(4,128)} %frame_lines.1) | copy-start | bytes 61444
  107.0 25.8 %collective-permute-start.22 = (bf16[512,256]{1,0:T(8,128)(2,1)}, bf16[512,256]{1,0:T(8,128)(2,1)S(1)}, u32[]{:S(2)}, u32[]{:S(2)}) collective-permute-start(bf16[512,256]{1,0:T(8,128)(2,1)} %get-tuple-element.74), channel_id=1, source_target_pairs={{0,4},{4,0},{8,12},{12,8},{16,20},{20,16},{24,28},{28,24},{1,5},{5... | collective-permute-start | bytes 786440 | tf_op jit(solution)/shard_map/ppermute | solution.py:290
  107.5 9.0 %collective-permute-start.15 = (f32[2,4,640]{2,1,0:T(4,128)S(1)}, f32[2,4,640]{2,1,0:T(4,128)S(1)}, u32[]{:S(2)}, u32[]{:S(2)}) collective-permute-start(f32[2,4,640]{2,1,0:T(4,128)S(1)} %copy-done.29), channel_id=1, source_target_pairs={{0,8},{4,12},{8,0},{12,4},{16,24},{20,28},{24,16},{28,20},{1,9},{5... | collective-permute-start | bytes 61448 | tf_op jit(solution)/shard_map/ppermute | solution.py:109
  112.7 20.1 %collective-permute-start.21 = (bf16[512,256]{1,0:T(8,128)(2,1)}, bf16[512,256]{1,0:T(8,128)(2,1)S(1)}, u32[]{:S(2)}, u32[]{:S(2)}) collective-permute-start(bf16[512,256]{1,0:T(8,128)(2,1)} %get-tuple-element.73), channel_id=1, source_target_pairs={{0,4},{4,0},{8,12},{12,8},{16,20},{20,16},{24,28},{28,24},{1,5},{5... | collective-permute-start | bytes 786440 | tf_op jit(solution)/shard_map/ppermute | solution.py:290
  118.7 4.9 %collective-permute-start.17 = (f32[4,4,640]{2,1,0:T(4,128)S(1)}, f32[4,4,640]{2,1,0:T(4,128)S(1)}, u32[]{:S(2)}, u32[]{:S(2)}) collective-permute-start(f32[4,4,640]{2,1,0:T(4,128)S(1)} %pad_maximum_fusion.3), channel_id=1, source_target_pairs={{0,16},{4,20},{8,24},{12,28},{16,0},{20,4},{24,8},{28,12},{1,17},{... | collective-permute-start | bytes 122888 | tf_op jit(solution)/shard_map/ppermute | solution.py:109
  120.0 13.9 %collective-permute-start.19 = (bf16[512,256]{1,0:T(8,128)(2,1)}, bf16[512,256]{1,0:T(8,128)(2,1)S(1)}, u32[]{:S(2)}, u32[]{:S(2)}) collective-permute-start(bf16[512,256]{1,0:T(8,128)(2,1)} %fusion.9), channel_id=1, source_target_pairs={{0,4},{4,0},{8,12},{12,8},{16,20},{20,16},{24,28},{28,24},{1,5},{5... | collective-permute-start | bytes 786440 | tf_op jit(solution)/shard_map/ppermute | solution.py:290
  125.2 8.7 %collective-permute-start.20 = (bf16[512,256]{1,0:T(8,128)(2,1)S(1)}, bf16[512,256]{1,0:T(8,128)(2,1)S(1)}, u32[]{:S(2)}, u32[]{:S(2)}) collective-permute-start(bf16[512,256]{1,0:T(8,128)(2,1)S(1)} %fusion.11), channel_id=1, source_target_pairs={{0,4},{4,0},{8,12},{12,8},{16,20},{20,16},{24,28},{28,24},{1,5},{5... | collective-permute-start | bytes 786440 | tf_op jit(solution)/shard_map/ppermute | solution.py:290

commit v4 on v3

--- a/solution.py
+++ b/solution.py
@@ -360,7 +360,6 @@
     packed = frames_of(me, piece, frame_count, columns, clips[0] + clips[1])
     frame_grad = packed[0, :frame_count]
     other_sum = first_sum(other[0], other[1])
-    mine_sum = first_sum(after(mine[0], packed), mine[1])
 
     blocks = slice_rows(
         after(crossed_near_p, *gate),
@@ -374,7 +373,7 @@
         for offset in range(count)
     ]
     firsts = [position * width for position in range(CHUNKS)]
-    kept, received, parts, rows = [], [], [], []
+    received, parts, rows = [], [], []
 
     def finish(earlier, tokens_last, index):
         product = jnp.dot(tokens_last, rows[index], preferred_element_type=jnp.float32)
@@ -382,19 +381,20 @@
 
     for index, (sent, arrived, offset) in enumerate(places):
         if index < 2:
-            sent = after(sent, other_sum, mine_sum)
+            sent = after(sent, other_sum)
         if index == 2:
             packed = clip_step(packed, dp, 2, (parts[1],))
             sent = after(sent, packed, *parts)
         if index == 3:
             packed = clip_step(packed, dp, 4, (parts[2],))
-            sent = after(sent, packed, *kept)
+            sent = after(sent, packed, mine_sum)
         rows.append(last_rows(y, is_mid, width, sent, arrived, offset))
         parts.append(finish(other_sum, other[2], index))
         received.append(over_y(parts[index]))
-        if index % 2:
-            tokens_last = after(mine[2], parts[index])
-            kept += [finish(mine_sum, tokens_last, done) for done in (index - 1, index)]
+        if index == 1:
+            mine_sum = first_sum(after(mine[0], parts[1]), mine[1])
+    tokens_last = after(mine[2], parts[-1])
+    kept = [finish(mine_sum, tokens_last, index) for index in range(CHUNKS)]
     table_grad = table_of(packed, level_table.shape[0])
     result = place_columns(after(y, parts[-1]), half, firsts[:2], kept[:2], received[:2])
     hidden_grad = place_columns(y, half, firsts[2:], kept[2:], received[2:], result)

time: 136 us -> 134 us (0.985)
  waiting for transfers between devices: 49.6 us -> 58 us
  starting transfers between devices: 34.3 us -> 30.1 us
  local copies, waits for them, and re-layouts: 14.1 us -> 11.3 us
  matrix products: 15.2 us -> 12.5 us
    ppermute x11, waiting for transfers between devices: 25.6 us -> 32.1 us  [along_z(): return lax.ppermute(array, 'dp', perm)]
    ppermute x2, starting transfers between devices: 5.06 us -> 0.35 us  [clip_step(): arrived = lax.ppermute(sent, 'dp', [(i, i ^ flip) for i in range(dp)])]
    dot_general x8, matrix products: 6.72 us -> 3.81 us  [finish(): jnp.dot(tokens_last, rows[index], preferred_element_type=jnp.float32)]
    ppermute x6, waiting for transfers between devices: 12.8 us -> 14.6 us  [over_y(): return lax.ppermute(array, 'dp', [(i, i ^ 1) for i in range(dp)])]
    pallas_call x4, Pallas kernels: 4.91 us -> 3.4 us  [last_rows(): pl.pallas_call(kernel, out_shape=jax.ShapeDtypeStruct((2 * rows, width),...]
    unnamed x69 -> x77, local copies, waits for them, and re-layouts: 9.63 us -> 8.75 us
  transfers between devices with their start and end apart: 23 -> 23, of which waited for: 8 -> 9; matrix products, arithmetic and copies ran while one was open for 16% -> 13% of each run, Pallas kernels for 11% -> 11%
where the time goes in v4:
time: 134 us; the launch traced here: 133 us
  waiting for transfers between devices  58 us (43%)
  starting transfers between devices  30.1 us (22%)
  Pallas kernels  16.2 us (12%)
  matrix products  12.5 us (9%)
  local copies, waits for them, and re-layouts  11.3 us (8%)
  other arithmetic  3.33 us (2%)
  between operations  1.41 us (1%)
    ppermute x11, waiting for transfers between devices, along_z(): return lax.ppermute(array, 'dp', perm)  32.1 us
    ppermute x11, starting transfers between devices, along_z(): return lax.ppermute(array, 'dp', perm)  18.1 us
    ppermute x6, waiting for transfers between devices, over_y(): return lax.ppermute(array, 'dp', [(i, i ^ 1) for i in range(dp)])  14.6 us
    unnamed x77, local copies, waits for them, and re-layouts  8.75 us
    ppermute x6, starting transfers between devices, over_y(): return lax.ppermute(array, 'dp', [(i, i ^ 1) for i in range(dp)])  8.2 us
    ppermute x4, waiting for transfers between devices, over_seq(): return lax.ppermute(array, 'seq', [(i, i ^ flip) for i in range(seq)])  7.72 us
    pallas_call x2, Pallas kernels, block_rows(): pl.pallas_call(kernel, out_shape=jax.ShapeDtypeStruct((2 * rows * len(blo...  3.86 us
    dot_general x8, matrix products, finish(): jnp.dot(tokens_last, rows[index], preferred_element_type=jnp.float32)  3.81 us
  transfers between devices with their start and end apart: 23, of which 9 were waited for; matrix products, arithmetic and copies ran while one was open for 13% of the time, Pallas kernels for 11%

profile of v4, /device:TPU:0, one launch (start us, length us, event | category | flops | bytes accessed | tf_op | source)
XLA Modules:
  0.0 132.9 jit_solution(1960442419618806586)
XLA Ops:
  0.7 2.3 %dynamic-slice_bitcast_fusion = (bf16[320,1024]{1,0:T(8,128)(2,1)S(1)}, bf16[320,1024]{1,0:T(8,128)(2,1)}) fusion(bf16[2048,320]{0,1:T(8,128)(2,1)} %param.9, s32[]{:T(128)S(6)} %select_n.44, s32[]{:T(128)S(6)} %select_n.43), kind=kLoop, calls=%fused_computation.12 | loop fusion | bytes 2621448 | tf_op jit(solution)/shard_map/dynamic_slice | solution.py:301
  3.0 3.0 %collective-permute-start.1 = (bf16[320,1024]{1,0:T(8,128)(2,1)S(1)}, bf16[320,1024]{1,0:T(8,128)(2,1)S(1)}, u32[]{:S(2)}, u32[]{:S(2)}) collective-permute-start(bf16[320,1024]{1,0:T(8,128)(2,1)S(1)} %get-tuple-element.73.refs_0_), channel_id=1, source_target_pairs={{0,8},{4,12},{8,0},{12,4},{16,24},{20,28},{24,16},{28,20},{1,9},{5... | collective-permute-start | bytes 1966088 | tf_op jit(solution)/shard_map/ppermute | solution.py:287
  6.0 1.5 %collective-permute-start.2 = (bf16[320,1024]{1,0:T(8,128)(2,1)S(1)}, bf16[320,1024]{1,0:T(8,128)(2,1)}, u32[]{:S(2)}, u32[]{:S(2)}) collective-permute-start(bf16[320,1024]{1,0:T(8,128)(2,1)S(1)} %get-tuple-element.73.refs_0_), channel_id=1, source_target_pairs={{8,16},{12,20},{16,8},{20,12},{9,17},{13,21},{17,9},{21,13},{10,18... | collective-permute-start | bytes 1966088 | tf_op jit(solution)/shard_map/ppermute | solution.py:287
  7.5 1.5 %collective-permute-start = (bf16[320,1024]{1,0:T(8,128)(2,1)}, bf16[320,1024]{1,0:T(8,128)(2,1)}, u32[]{:S(2)}, u32[]{:S(2)}) collective-permute-start(bf16[320,1024]{1,0:T(8,128)(2,1)} %get-tuple-element.74), channel_id=1, source_target_pairs={{0,4},{4,0},{8,12},{12,8},{16,20},{20,16},{24,28},{28,24},{1,5},{5... | collective-permute-start | bytes 1966088 | tf_op jit(solution)/shard_map/ppermute | solution.py:290
  9.4 0.7 fusion
  10.2 1.8 %reduce-precision_convert_fusion.1 = (bf16[3,2560]{1,0:T(4,128)(2,1)S(1)}, bf16[3,2560]{1,0:T(4,128)(2,1)S(1)}, bf16[3,2560]{1,0:T(4,128)(2,1)S(1)}) fusion(bf16[1,128,2560]{2,1,0:T(8,128)(2,1)} %param.8, bf16[1,128,2560]{2,1,0:T(8,128)(2,1)S(1)} %copy-done.24, s32[128]{0:T(128)S(1)} %bitcast.70), kind=kOutput, calls=%fused_computation.43 | convolution fusion | flops 12841344 | bytes 1357312 | tf_op jit(solution)/shard_map/dot_general | solution.py:27
  12.3 11.7 %collective-permute-done.refs_1_ = bf16[320,1024]{1,0:T(8,128)(2,1)} collective-permute-done((bf16[320,1024]{1,0:T(8,128)(2,1)}, bf16[320,1024]{1,0:T(8,128)(2,1)}, u32[]{:S(2)}, u32[]{:S(2)}) %collective-permute-start) | collective-permute-done | bytes 655392 | tf_op jit(solution)/shard_map/ppermute | solution.py:290
  24.1 0.8 copy-done.22
  24.9 1.5 %collective-permute-start.3 = (bf16[144,2560]{1,0:T(8,128)(2,1)S(1)}, bf16[144,2560]{1,0:T(8,128)(2,1)S(1)}, u32[]{:S(2)}, u32[]{:S(2)}) collective-permute-start(bf16[144,2560]{1,0:T(8,128)(2,1)S(1)} %pad_maximum_fusion.1.refs_0_), channel_id=1, source_target_pairs={{0,2},{1,3},{2,0},{3,1},{4,6},{5,7},{6,4},{7,5},{8,10},{9,11},{10,... | collective-permute-start | bytes 2211848 | tf_op jit(solution)/shard_map/ppermute | solution.py:293
  26.4 1.5 %collective-permute-start.4 = (bf16[144,2560]{1,0:T(8,128)(2,1)S(1)}, bf16[144,2560]{1,0:T(8,128)(2,1)S(1)}, u32[]{:S(2)}, u32[]{:S(2)}) collective-permute-start(bf16[144,2560]{1,0:T(8,128)(2,1)S(1)} %pad_maximum_fusion.1.refs_0_), channel_id=1, source_target_pairs={{0,4},{4,0},{8,12},{12,8},{16,20},{20,16},{24,28},{28,24},{1,5},{5... | collective-permute-start | bytes 2211848 | tf_op jit(solution)/shard_map/ppermute | solution.py:290
  27.9 3.3 %collective-permute-start.5 = (bf16[320,1024]{1,0:T(8,128)(2,1)}, bf16[320,1024]{1,0:T(8,128)(2,1)}, u32[]{:S(2)}, u32[]{:S(2)}) collective-permute-start(bf16[320,1024]{1,0:T(8,128)(2,1)} %collective-permute-done.refs_1_), channel_id=1, source_target_pairs={{0,8},{4,12},{8,0},{12,4},{16,24},{20,28},{24,16},{28,20},{1,9},{5... | collective-permute-start | bytes 1966088 | tf_op jit(solution)/shard_map/ppermute | solution.py:287
  31.3 1.5 %collective-permute-start.6 = (bf16[320,1024]{1,0:T(8,128)(2,1)}, bf16[320,1024]{1,0:T(8,128)(2,1)}, u32[]{:S(2)}, u32[]{:S(2)}) collective-permute-start(bf16[320,1024]{1,0:T(8,128)(2,1)} %collective-permute-done.refs_1_), channel_id=1, source_target_pairs={{8,16},{12,20},{16,8},{20,12},{9,17},{13,21},{17,9},{21,13},{10,18... | collective-permute-start | bytes 1966088 | tf_op jit(solution)/shard_map/ppermute | solution.py:287
  32.7 1.5 %collective-permute-start.7 = (bf16[320,1024]{1,0:T(8,128)(2,1)}, bf16[320,1024]{1,0:T(8,128)(2,1)}, u32[]{:S(2)}, u32[]{:S(2)}) collective-permute-start(bf16[320,1024]{1,0:T(8,128)(2,1)} %copy-done.22), channel_id=1, source_target_pairs={{8,16},{12,20},{16,8},{20,12},{9,17},{13,21},{17,9},{21,13},{10,18... | collective-permute-start | bytes 1966088 | tf_op jit(solution)/shard_map/ppermute | solution.py:287
  34.2 7.7 %collective-permute-done.3.refs_2_ = bf16[144,2560]{1,0:T(8,128)(2,1)S(1)} collective-permute-done((bf16[144,2560]{1,0:T(8,128)(2,1)S(1)}, bf16[144,2560]{1,0:T(8,128)(2,1)S(1)}, u32[]{:S(2)}, u32[]{:S(2)}) %collective-permute-start.3) | collective-permute-done | bytes 737312 | tf_op jit(solution)/shard_map/ppermute | solution.py:293
  42.0 1.3 collective-permute-start.8
  43.4 0.9 collective-permute-done.5.refs_3_
  44.3 14.8 %collective-permute-done.8.refs_2_ = bf16[320,1024]{1,0:T(8,128)(2,1)} collective-permute-done((bf16[320,1024]{1,0:T(8,128)(2,1)}, bf16[320,1024]{1,0:T(8,128)(2,1)}, u32[]{:S(2)}, u32[]{:S(2)}) %collective-permute-start.8) | collective-permute-done | bytes 655392 | tf_op jit(solution)/shard_map/ppermute | solution.py:287
  59.0 1.5 %collective-permute-start.11 = (bf16[144,2560]{1,0:T(8,128)(2,1)S(1)}, bf16[144,2560]{1,0:T(8,128)(2,1)}, u32[]{:S(2)}, u32[]{:S(2)}) collective-permute-start(bf16[144,2560]{1,0:T(8,128)(2,1)S(1)} %collective-permute-done.4.refs_0_.refs_4_), channel_id=1, source_target_pairs={{0,2},{1,3},{2,0},{3,1},{4,6},{5,7},{6,4},{7,5},{8,10},{9,11},{10,... | collective-permute-start | bytes 2211848 | tf_op jit(solution)/shard_map/ppermute | solution.py:293
  60.5 1.3 collective-permute-start.10
  61.8 0.7 collective-permute-start.9
  62.5 1.3 fusion.62
  63.8 1.5 %block_rows.2 = bf16[1280,1024]{1,0:T(8,128)(2,1)S(1)} custom-call(s32[2]{0:T(128)S(1)} %pad_add_fusion.place, bf16[320,1024]{1,0:T(8,128)(2,1)S(1)} %get-tuple-element.73.refs_0_, bf16[320,1024]{1,0:T(8,128)(2,1)} %collective-permute-done.refs_1_, bf16[320,1024]{1,0:T(8,128)(2,1)S(1)} %copy-done.23, bf16[320,1024]{1,0:T(8,128)(2,1)} %collective-permute-done.5.refs_3_), custom_call_target="tpu_custom_call" | custom-call | tf_op jit(solution)/shard_map/block_rows/pallas_call | solution.py:173
  65.3 1.8 %pad_maximum_fusion = bf16[3,144,2560]{2,1,0:T(8,128)(2,1)} fusion(bf16[1,144,2560]{2,1,0:T(8,128)(2,1)S(1)} %bitcast.65, bf16[1,144,2560]{2,1,0:T(8,128)(2,1)S(1)} %bitcast.64, bf16[1,144,2560]{2,1,0:T(8,128)(2,1)S(1)} %fusion.62), kind=kLoop, calls=%fused_computation.3 | loop fusion | flops 2211840 | bytes 4423680 | tf_op jit(solution)/shard_map/stack | solution.py:341
  67.5 8.4 %collective-permute-done.10.refs_3_ = bf16[320,1024]{1,0:T(8,128)(2,1)S(1)} collective-permute-done((bf16[320,1024]{1,0:T(8,128)(2,1)}, bf16[320,1024]{1,0:T(8,128)(2,1)S(1)}, u32[]{:S(2)}, u32[]{:S(2)}) %collective-permute-start.10) | collective-permute-done | bytes 655392 | tf_op jit(solution)/shard_map/ppermute | solution.py:287
  75.9 0.8 copy-done.20
  76.7 0.8 copy-done.18
  77.6 0.5 collective-permute-start.13
  78.1 1.1 copy-done.19
  79.2 2.0 %slice_rows.1 = (bf16[640,512]{1,0:T(8,128)(2,1)S(1)}, bf16[640,256]{1,0:T(8,128)(2,1)}, bf16[640,256]{1,0:T(8,128)(2,1)}) custom-call(bf16[320,1024]{1,0:T(8,128)(2,1)} %collective-permute-done.7.upper, bf16[320,1024]{1,0:T(8,128)(2,1)S(1)} %copy-done.19), custom_call_target="tpu_custom_call" | custom-call | tf_op jit(solution)/shard_map/slice_rows/pallas_call | solution.py:138
  81.2 1.3 collective-permute-start.14
  82.5 1.3 collective-permute-start.16
  83.8 1.4 %collective-permute-start.18 = (bf16[640,256]{1,0:T(8,128)(2,1)}, bf16[640,256]{1,0:T(8,128)(2,1)}, u32[]{:S(2)}, u32[]{:S(2)}) collective-permute-start(bf16[640,256]{1,0:T(8,128)(2,1)} %get-tuple-element.58.sent), channel_id=1, source_target_pairs={{8,0},{12,4},{16,24},{20,28},{9,1},{13,5},{17,25},{21,29},{10,2},{... | collective-permute-start | bytes 983048 | tf_op jit(solution)/shard_map/ppermute | solution.py:287
  85.3 2.4 %block_rows.3 = bf16[640,1024]{1,0:T(8,128)(2,1)S(1)} custom-call(s32[2]{0:T(128)S(1)} %pad_add_fusion.place, bf16[320,1024]{1,0:T(8,128)(2,1)} %collective-permute-done.2.refs_0_, bf16[320,1024]{1,0:T(8,128)(2,1)} %collective-permute-done.6.refs_1_, bf16[320,1024]{1,0:T(8,128)(2,1)} %collective-permute-done.8.refs_2_, bf16[320,1024]{1,0:T(8,128)(2,1)S(1)} %copy-done.21), custom_call_target="tpu_custom_call" | custom-call | tf_op jit(solution)/shard_map/block_rows/pallas_call | solution.py:173
  87.7 1.8 %order_pieces.3 = (bf16[512,1280]{1,0:T(8,128)(2,1)S(1)}, bf16[512,640]{1,0:T(8,128)(2,1)S(1)}, bf16[512,640]{1,0:T(8,128)(2,1)S(1)}) custom-call(s32[1]{0:T(128)} %bitcast.1.place, bf16[144,2560]{1,0:T(8,128)(2,1)S(1)} %copy-done.8, bf16[3,144,2560]{2,1,0:T(8,128)(2,1)S(1)} %collective-permute-done.12.refs_1_.refs_3_.refs_5_, ...), custom_call_target="tpu_custom_call" | custom-call | tf_op jit(solution)/shard_map/order_pieces/pallas_call | solution.py:228
  89.6 1.0 fusion.29
  90.5 0.7 copy-done.14
  91.3 1.5 %convolution_add_fusion.2 = f32[512,1024]{1,0:T(8,128)S(1)} fusion(f32[512,1024]{1,0:T(8,128)S(1)} %fusion.29, bf16[512,1280]{1,0:T(8,128)(2,1)S(1)} %get-tuple-element.42, bf16[1280,1024]{1,0:T(8,128)(2,1)S(1)} %copy-done.14), kind=kOutput, calls=%fused_computation.6 | convolution fusion | flops 1342701568 | bytes 8126464 | tf_op jit(solution)/shard_map/dot_general | solution.py:354
  92.9 8.0 %collective-permute-done.14.arrived = bf16[640,512]{1,0:T(8,128)(2,1)S(1)} collective-permute-done((bf16[640,512]{1,0:T(8,128)(2,1)S(1)}, bf16[640,512]{1,0:T(8,128)(2,1)S(1)}, u32[]{:S(2)}, u32[]{:S(2)}) %collective-permute-start.14) | collective-permute-done | bytes 655392 | tf_op jit(solution)/shard_map/ppermute | solution.py:287
  100.9 0.6 last_rows.4
  101.9 0.6 last_rows.5
  102.5 1.2 fusion.8
  103.7 1.5 %collective-permute-start.22 = (bf16[512,256]{1,0:T(8,128)(2,1)}, bf16[512,256]{1,0:T(8,128)(2,1)}, u32[]{:S(2)}, u32[]{:S(2)}) collective-permute-start(bf16[512,256]{1,0:T(8,128)(2,1)} %get-tuple-element.72), channel_id=1, source_target_pairs={{0,4},{4,0},{8,12},{12,8},{16,20},{20,16},{24,28},{28,24},{1,5},{5... | collective-permute-start | bytes 786440 | tf_op jit(solution)/shard_map/ppermute | solution.py:290
  105.2 1.7 %frame_lines.1 = f32[2,4,640]{2,1,0:T(4,128)} custom-call(s32[1]{0:T(128)} %bitcast.1.place, bf16[144,2560]{1,0:T(8,128)(2,1)} %copy-done.3, bf16[3,144,2560]{2,1,0:T(8,128)(2,1)} %copy-done.1, bf16[144,2560]{1,0:T(8,128)(2,1)} %copy-done.5, bf16[3,144,2560]{2,1,0:T(8,128)(2,1)} %copy-done.1, bf16[144,2560]{1,0:T(8,128)(2,1)} %copy-done.7, ...), custom_call_target="tpu_custom_call" | custom-call | tf_op jit(solution)/shard_map/frame_lines/pallas_call | solution.py:94
  107.0 1.1 copy-done.4
  108.1 1.1 copy-done.6
  109.2 0.4 order_pieces.2
  109.7 0.9 copy-done.17
  110.5 1.0 fusion.31
  111.6 0.6 collective-permute-start.21
  112.1 2.6 %collective-permute-done.15 = f32[2,4,640]{2,1,0:T(4,128)S(1)} collective-permute-done((f32[2,4,640]{2,1,0:T(4,128)}, f32[2,4,640]{2,1,0:T(4,128)S(1)}, u32[]{:S(2)}, u32[]{:S(2)}) %collective-permute-start.15) | collective-permute-done | bytes 20512 | tf_op jit(solution)/shard_map/ppermute | solution.py:109
  114.8 1.1 last_rows.6
  115.9 0.4 fusion.9
  116.6 1.5 %convolution_add_fusion.1 = f32[512,1024]{1,0:T(8,128)S(1)} fusion(f32[512,1024]{1,0:T(8,128)S(1)} %fusion.31, bf16[512,1280]{1,0:T(8,128)(2,1)S(1)} %get-tuple-element.50, bf16[1280,1024]{1,0:T(8,128)(2,1)S(1)} %copy-done.15), kind=kOutput, calls=%fused_computation.5 | convolution fusion | flops 1342701568 | bytes 8126464 | tf_op jit(solution)/shard_map/dot_general | solution.py:354
  118.1 0.6 copy.12
  118.7 1.5 %collective-permute-start.19 = (bf16[512,256]{1,0:T(8,128)(2,1)S(1)}, bf16[512,256]{1,0:T(8,128)(2,1)S(1)}, u32[]{:S(2)}, u32[]{:S(2)}) collective-permute-start(bf16[512,256]{1,0:T(8,128)(2,1)S(1)} %fusion.9), channel_id=1, source_target_pairs={{0,4},{4,0},{8,12},{12,8},{16,20},{20,16},{24,28},{28,24},{1,5},{5... | collective-permute-start | bytes 786440 | tf_op jit(solution)/shard_map/ppermute | solution.py:290
  120.2 1.0 collective-permute-done.17
  121.3 1.1 last_rows.7
  122.4 0.4 fusion.10
  124.1 1.6 %collective-permute-start.20 = (bf16[512,256]{1,0:T(8,128)(2,1)S(1)}, bf16[512,256]{1,0:T(8,128)(2,1)S(1)}, u32[]{:S(2)}, u32[]{:S(2)}) collective-permute-start(bf16[512,256]{1,0:T(8,128)(2,1)S(1)} %fusion.10), channel_id=1, source_target_pairs={{0,4},{4,0},{8,12},{12,8},{16,20},{20,16},{24,28},{28,24},{1,5},{5... | collective-permute-start | bytes 786440 | tf_op jit(solution)/shard_map/ppermute | solution.py:290
  125.7 0.4 fusion.5
  126.3 0.8 fusion.24
  127.1 1.9 %place_columns.2.refs_4_ = bf16[512,2048]{1,0:T(8,128)(2,1)} custom-call(s32[1]{0:T(128)} %bitcast.13.place, bf16[512,256]{1,0:T(8,128)(2,1)S(1)} %get-tuple-element.68.refs_0_, bf16[512,256]{1,0:T(8,128)(2,1)S(1)} %get-tuple-element.67.refs_1_, bf16[512,256]{1,0:T(8,128)(2,1)S(1)} %collective-permute-done.21.refs_2_, ...), custom_call_target="tpu_custom_call" | custom-call | tf_op jit(solution)/shard_map/place_columns/pallas_call | solution.py:262
  129.0 2.9 %collective-permute-done.20.refs_3_ = bf16[512,256]{1,0:T(8,128)(2,1)S(1)} collective-permute-done((bf16[512,256]{1,0:T(8,128)(2,1)S(1)}, bf16[512,256]{1,0:T(8,128)(2,1)S(1)}, u32[]{:S(2)}, u32[]{:S(2)}) %collective-permute-start.20) | collective-permute-done | bytes 262176 | tf_op jit(solution)/shard_map/ppermute | solution.py:290
  131.9 1.0 place_columns.3
  (103 shorter events, 3.4 us)
Async XLA Ops:
  0.6 8.4 %copy-start = (f32[64,2560]{1,0:T(8,128)S(1)}, f32[64,2560]{1,0:T(8,128)}, u32[]{:S(2)}) copy-start(f32[64,2560]{1,0:T(8,128)} %param.11) | copy-start | bytes 1966084
  0.6 8.4 %copy-start.36 = (s32[1,3]{1,0:T(1,128)S(1)}, s32[1,3]{1,0:T(1,128)}, u32[]{:S(2)}) copy-start(s32[1,3]{1,0:T(1,128)} %param.13) | copy-start | bytes 40
  0.7 8.4 %copy-start.34 = (f32[2560]{0:T(1024)S(1)}, f32[2560]{0:T(1024)}, u32[]{:S(2)}) copy-start(f32[2560]{0:T(1024)} %param.10) | copy-start | bytes 30724
  0.7 8.7 %copy-start.24 = (bf16[1,128,2560]{2,1,0:T(8,128)(2,1)S(1)}, bf16[1,128,2560]{2,1,0:T(8,128)(2,1)}, u32[]{:S(2)}) copy-start(bf16[1,128,2560]{2,1,0:T(8,128)(2,1)} %param.7) | copy-start | bytes 1966084
  0.7 8.7 %copy-start.35 = (s32[1,128]{1,0:T(1,128)S(1)}, s32[1,128]{1,0:T(1,128)}, u32[]{:S(2)}) copy-start(s32[1,128]{1,0:T(1,128)} %param.12) | copy-start | bytes 1540
  3.0 21.0 %collective-permute-start.1 = (bf16[320,1024]{1,0:T(8,128)(2,1)S(1)}, bf16[320,1024]{1,0:T(8,128)(2,1)S(1)}, u32[]{:S(2)}, u32[]{:S(2)}) collective-permute-start(bf16[320,1024]{1,0:T(8,128)(2,1)S(1)} %get-tuple-element.73.refs_0_), channel_id=1, source_target_pairs={{0,8},{4,12},{8,0},{12,4},{16,24},{20,28},{24,16},{28,20},{1,9},{5... | collective-permute-start | bytes 1966088 | tf_op jit(solution)/shard_map/ppermute | solution.py:287
  6.0 18.0 %collective-permute-start.2 = (bf16[320,1024]{1,0:T(8,128)(2,1)S(1)}, bf16[320,1024]{1,0:T(8,128)(2,1)}, u32[]{:S(2)}, u32[]{:S(2)}) collective-permute-start(bf16[320,1024]{1,0:T(8,128)(2,1)S(1)} %get-tuple-element.73.refs_0_), channel_id=1, source_target_pairs={{8,16},{12,20},{16,8},{20,12},{9,17},{13,21},{17,9},{21,13},{10,18... | collective-permute-start | bytes 1966088 | tf_op jit(solution)/shard_map/ppermute | solution.py:287
  7.5 16.5 %collective-permute-start = (bf16[320,1024]{1,0:T(8,128)(2,1)}, bf16[320,1024]{1,0:T(8,128)(2,1)}, u32[]{:S(2)}, u32[]{:S(2)}) collective-permute-start(bf16[320,1024]{1,0:T(8,128)(2,1)} %get-tuple-element.74), channel_id=1, source_target_pairs={{0,4},{4,0},{8,12},{12,8},{16,20},{20,16},{24,28},{28,24},{1,5},{5... | collective-permute-start | bytes 1966088 | tf_op jit(solution)/shard_map/ppermute | solution.py:290
  12.1 29.8 %copy-start.25 = (bf16[128,640]{1,0:T(8,128)(2,1)}, bf16[128,640]{1,0:T(8,128)(2,1)S(1)}, u32[]{:S(2)}) copy-start(bf16[128,640]{1,0:T(8,128)(2,1)S(1)} %get-tuple-element.75) | copy-start | bytes 491524
  12.1 29.8 %copy-start.26 = (bf16[128,640]{1,0:T(8,128)(2,1)}, bf16[128,640]{1,0:T(8,128)(2,1)S(1)}, u32[]{:S(2)}) copy-start(bf16[128,640]{1,0:T(8,128)(2,1)S(1)} %get-tuple-element.76) | copy-start | bytes 491524
  12.2 29.8 %copy-start.27 = (bf16[128,640]{1,0:T(8,128)(2,1)}, bf16[128,640]{1,0:T(8,128)(2,1)S(1)}, u32[]{:S(2)}) copy-start(bf16[128,640]{1,0:T(8,128)(2,1)S(1)} %get-tuple-element.77) | copy-start | bytes 491524
  12.2 29.8 %copy-start.28 = (bf16[128,640]{1,0:T(8,128)(2,1)}, bf16[128,640]{1,0:T(8,128)(2,1)S(1)}, u32[]{:S(2)}) copy-start(bf16[128,640]{1,0:T(8,128)(2,1)S(1)} %get-tuple-element.78) | copy-start | bytes 491524
  12.3 29.7 %copy-start.31 = (bf16[16,2560]{1,0:T(8,128)(2,1)}, bf16[16,2560]{1,0:T(8,128)(2,1)S(1)}, u32[]{:S(2)}) copy-start(bf16[16,2560]{1,0:T(8,128)(2,1)S(1)} %fusion.19) | copy-start | bytes 245764
  12.3 52.9 %copy-start.3 = (bf16[144,2560]{1,0:T(8,128)(2,1)}, bf16[144,2560]{1,0:T(8,128)(2,1)S(1)}, u32[]{:S(2)}) copy-start(bf16[144,2560]{1,0:T(8,128)(2,1)S(1)} %pad_maximum_fusion.1.refs_0_) | copy-start | bytes 2211844
  24.1 0.8 copy-start.22
  24.9 17.0 %collective-permute-start.3 = (bf16[144,2560]{1,0:T(8,128)(2,1)S(1)}, bf16[144,2560]{1,0:T(8,128)(2,1)S(1)}, u32[]{:S(2)}, u32[]{:S(2)}) collective-permute-start(bf16[144,2560]{1,0:T(8,128)(2,1)S(1)} %pad_maximum_fusion.1.refs_0_), channel_id=1, source_target_pairs={{0,2},{1,3},{2,0},{3,1},{4,6},{5,7},{6,4},{7,5},{8,10},{9,11},{10,... | collective-permute-start | bytes 2211848 | tf_op jit(solution)/shard_map/ppermute | solution.py:293
  26.4 17.9 %collective-permute-start.4 = (bf16[144,2560]{1,0:T(8,128)(2,1)S(1)}, bf16[144,2560]{1,0:T(8,128)(2,1)S(1)}, u32[]{:S(2)}, u32[]{:S(2)}) collective-permute-start(bf16[144,2560]{1,0:T(8,128)(2,1)S(1)} %pad_maximum_fusion.1.refs_0_), channel_id=1, source_target_pairs={{0,4},{4,0},{8,12},{12,8},{16,20},{20,16},{24,28},{28,24},{1,5},{5... | collective-permute-start | bytes 2211848 | tf_op jit(solution)/shard_map/ppermute | solution.py:290
  27.9 16.3 %collective-permute-start.5 = (bf16[320,1024]{1,0:T(8,128)(2,1)}, bf16[320,1024]{1,0:T(8,128)(2,1)}, u32[]{:S(2)}, u32[]{:S(2)}) collective-permute-start(bf16[320,1024]{1,0:T(8,128)(2,1)} %collective-permute-done.refs_1_), channel_id=1, source_target_pairs={{0,8},{4,12},{8,0},{12,4},{16,24},{20,28},{24,16},{28,20},{1,9},{5... | collective-permute-start | bytes 1966088 | tf_op jit(solution)/shard_map/ppermute | solution.py:287
  31.3 13.0 %collective-permute-start.6 = (bf16[320,1024]{1,0:T(8,128)(2,1)}, bf16[320,1024]{1,0:T(8,128)(2,1)}, u32[]{:S(2)}, u32[]{:S(2)}) collective-permute-start(bf16[320,1024]{1,0:T(8,128)(2,1)} %collective-permute-done.refs_1_), channel_id=1, source_target_pairs={{8,16},{12,20},{16,8},{20,12},{9,17},{13,21},{17,9},{21,13},{10,18... | collective-permute-start | bytes 1966088 | tf_op jit(solution)/shard_map/ppermute | solution.py:287
  32.7 11.5 %collective-permute-start.7 = (bf16[320,1024]{1,0:T(8,128)(2,1)}, bf16[320,1024]{1,0:T(8,128)(2,1)}, u32[]{:S(2)}, u32[]{:S(2)}) collective-permute-start(bf16[320,1024]{1,0:T(8,128)(2,1)} %copy-done.22), channel_id=1, source_target_pairs={{8,16},{12,20},{16,8},{20,12},{9,17},{13,21},{17,9},{21,13},{10,18... | collective-permute-start | bytes 1966088 | tf_op jit(solution)/shard_map/ppermute | solution.py:287
  42.0 23.3 %copy-start.5 = (bf16[144,2560]{1,0:T(8,128)(2,1)}, bf16[144,2560]{1,0:T(8,128)(2,1)S(1)}, u32[]{:S(2)}) copy-start(bf16[144,2560]{1,0:T(8,128)(2,1)S(1)} %collective-permute-done.3.refs_2_) | copy-start | bytes 2211844
  42.0 17.1 %collective-permute-start.8 = (bf16[320,1024]{1,0:T(8,128)(2,1)}, bf16[320,1024]{1,0:T(8,128)(2,1)}, u32[]{:S(2)}, u32[]{:S(2)}) collective-permute-start(bf16[320,1024]{1,0:T(8,128)(2,1)} %collective-permute-done.2.refs_0_), channel_id=1, source_target_pairs={{8,0},{12,4},{16,24},{20,28},{9,1},{13,5},{17,25},{21,29},{10,2},{... | collective-permute-start | bytes 1966088 | tf_op jit(solution)/shard_map/ppermute | solution.py:287
  43.3 20.5 %copy-start.23 = (bf16[320,1024]{1,0:T(8,128)(2,1)S(1)}, bf16[320,1024]{1,0:T(8,128)(2,1)}, u32[]{:S(2)}) copy-start(bf16[320,1024]{1,0:T(8,128)(2,1)} %copy-done.22) | copy-start | bytes 1966084
  44.3 21.0 %copy-start.7 = (bf16[144,2560]{1,0:T(8,128)(2,1)}, bf16[144,2560]{1,0:T(8,128)(2,1)S(1)}, u32[]{:S(2)}) copy-start(bf16[144,2560]{1,0:T(8,128)(2,1)S(1)} %collective-permute-done.4.refs_0_.refs_4_) | copy-start | bytes 2211844
  59.0 18.5 %collective-permute-start.11 = (bf16[144,2560]{1,0:T(8,128)(2,1)S(1)}, bf16[144,2560]{1,0:T(8,128)(2,1)}, u32[]{:S(2)}, u32[]{:S(2)}) collective-permute-start(bf16[144,2560]{1,0:T(8,128)(2,1)S(1)} %collective-permute-done.4.refs_0_.refs_4_), channel_id=1, source_target_pairs={{0,2},{1,3},{2,0},{3,1},{4,6},{5,7},{6,4},{7,5},{8,10},{9,11},{10,... | collective-permute-start | bytes 2211848 | tf_op jit(solution)/shard_map/ppermute | solution.py:293
  60.5 15.3 %collective-permute-start.10 = (bf16[320,1024]{1,0:T(8,128)(2,1)}, bf16[320,1024]{1,0:T(8,128)(2,1)S(1)}, u32[]{:S(2)}, u32[]{:S(2)}) collective-permute-start(bf16[320,1024]{1,0:T(8,128)(2,1)} %collective-permute-done.6.refs_1_), channel_id=1, source_target_pairs={{8,0},{12,4},{16,24},{20,28},{9,1},{13,5},{17,25},{21,29},{10,2},{... | collective-permute-start | bytes 1966088 | tf_op jit(solution)/shard_map/ppermute | solution.py:287
  61.8 14.9 %collective-permute-start.9 = (bf16[320,1024]{1,0:T(8,128)(2,1)}, bf16[320,1024]{1,0:T(8,128)(2,1)S(1)}, u32[]{:S(2)}, u32[]{:S(2)}) collective-permute-start(bf16[320,1024]{1,0:T(8,128)(2,1)} %collective-permute-done.5.refs_3_), channel_id=1, source_target_pairs={{8,16},{12,20},{16,8},{20,12},{9,17},{13,21},{17,9},{21,13},{10,18... | collective-permute-start | bytes 1966088 | tf_op jit(solution)/shard_map/ppermute | solution.py:287
  65.3 2.2 %copy-start.13 = (bf16[1280,1024]{1,0:T(8,128)(2,1)}, bf16[1280,1024]{1,0:T(8,128)(2,1)S(1)}, u32[]{:S(2)}) copy-start(bf16[1280,1024]{1,0:T(8,128)(2,1)S(1)} %block_rows.2) | copy-start | bytes 7864324
  75.9 0.8 copy-start.20
  76.7 0.8 copy-start.18
  77.6 7.7 %collective-permute-start.12 = (bf16[3,144,2560]{2,1,0:T(8,128)(2,1)}, bf16[3,144,2560]{2,1,0:T(8,128)(2,1)S(1)}, u32[]{:S(2)}, u32[]{:S(2)}) collective-permute-start(bf16[3,144,2560]{2,1,0:T(8,128)(2,1)} %pad_maximum_fusion), channel_id=1, source_target_pairs={{0,1},{1,0},{2,3},{3,2},{4,5},{5,4},{6,7},{7,6},{8,9},{9,8},{10,11... | collective-permute-start | bytes 6635528 | tf_op jit(solution)/shard_map/ppermute | solution.py:293
  77.6 10.1 %collective-permute-start.13 = (bf16[144,2560]{1,0:T(8,128)(2,1)}, bf16[144,2560]{1,0:T(8,128)(2,1)}, u32[]{:S(2)}, u32[]{:S(2)}) collective-permute-start(bf16[144,2560]{1,0:T(8,128)(2,1)} %collective-permute-done.11.refs_2_.refs_6_), channel_id=1, source_target_pairs={{0,1},{1,0},{2,3},{3,2},{4,5},{5,4},{6,7},{7,6},{8,9},{9,8},{10,11... | collective-permute-start | bytes 2211848 | tf_op jit(solution)/shard_map/ppermute | solution.py:293
  78.1 1.1 copy-start.19
  79.2 6.1 %copy-start.21 = (bf16[320,1024]{1,0:T(8,128)(2,1)S(1)}, bf16[320,1024]{1,0:T(8,128)(2,1)}, u32[]{:S(2)}) copy-start(bf16[320,1024]{1,0:T(8,128)(2,1)} %copy-done.20) | copy-start | bytes 1966084
  81.2 19.7 %collective-permute-start.14 = (bf16[640,512]{1,0:T(8,128)(2,1)S(1)}, bf16[640,512]{1,0:T(8,128)(2,1)S(1)}, u32[]{:S(2)}, u32[]{:S(2)}) collective-permute-start(bf16[640,512]{1,0:T(8,128)(2,1)S(1)} %get-tuple-element.49.sent), channel_id=1, source_target_pairs={{8,0},{12,4},{16,24},{20,28},{9,1},{13,5},{17,25},{21,29},{10,2},{... | collective-permute-start | bytes 1966088 | tf_op jit(solution)/shard_map/ppermute | solution.py:287
  82.5 32.2 %collective-permute-start.16 = (bf16[640,256]{1,0:T(8,128)(2,1)}, bf16[640,256]{1,0:T(8,128)(2,1)}, u32[]{:S(2)}, u32[]{:S(2)}) collective-permute-start(bf16[640,256]{1,0:T(8,128)(2,1)} %get-tuple-element.56.sent), channel_id=1, source_target_pairs={{8,0},{12,4},{16,24},{20,28},{9,1},{13,5},{17,25},{21,29},{10,2},{... | collective-permute-start | bytes 983048 | tf_op jit(solution)/shard_map/ppermute | solution.py:287
  83.8 3.9 %copy-start.8 = (bf16[144,2560]{1,0:T(8,128)(2,1)S(1)}, bf16[144,2560]{1,0:T(8,128)(2,1)}, u32[]{:S(2)}) copy-start(bf16[144,2560]{1,0:T(8,128)(2,1)} %copy-done.7) | copy-start | bytes 2211844
  83.8 37.4 %collective-permute-start.18 = (bf16[640,256]{1,0:T(8,128)(2,1)}, bf16[640,256]{1,0:T(8,128)(2,1)}, u32[]{:S(2)}, u32[]{:S(2)}) collective-permute-start(bf16[640,256]{1,0:T(8,128)(2,1)} %get-tuple-element.58.sent), channel_id=1, source_target_pairs={{8,0},{12,4},{16,24},{20,28},{9,1},{13,5},{17,25},{21,29},{10,2},{... | collective-permute-start | bytes 983048 | tf_op jit(solution)/shard_map/ppermute | solution.py:287
  85.3 2.4 %copy-start.1 = (bf16[3,144,2560]{2,1,0:T(8,128)(2,1)}, bf16[3,144,2560]{2,1,0:T(8,128)(2,1)S(1)}, u32[]{:S(2)}) copy-start(bf16[3,144,2560]{2,1,0:T(8,128)(2,1)S(1)} %collective-permute-done.12.refs_1_.refs_3_.refs_5_) | copy-start | bytes 6635524
  87.7 1.9 %copy-start.16 = (bf16[640,1024]{1,0:T(8,128)(2,1)}, bf16[640,1024]{1,0:T(8,128)(2,1)S(1)}, u32[]{:S(2)}) copy-start(bf16[640,1024]{1,0:T(8,128)(2,1)S(1)} %block_rows.3) | copy-start | bytes 3932164
  89.6 1.7 %copy-start.14 = (bf16[1280,1024]{1,0:T(8,128)(2,1)S(1)}, bf16[1280,1024]{1,0:T(8,128)(2,1)}, u32[]{:S(2)}) copy-start(bf16[1280,1024]{1,0:T(8,128)(2,1)} %copy-done.13) | copy-start | bytes 7864324
  92.8 9.6 %copy-start.29 = (f32[512,1024]{1,0:T(8,128)}, f32[512,1024]{1,0:T(8,128)S(1)}, u32[]{:S(2)}) copy-start(f32[512,1024]{1,0:T(8,128)S(1)} %convolution_add_fusion.2) | copy-start | bytes 6291460
  101.5 1.0 copy-start.9
  102.5 1.2 copy-start.11
  103.7 23.4 %collective-permute-start.22 = (bf16[512,256]{1,0:T(8,128)(2,1)}, bf16[512,256]{1,0:T(8,128)(2,1)}, u32[]{:S(2)}, u32[]{:S(2)}) collective-permute-start(bf16[512,256]{1,0:T(8,128)(2,1)} %get-tuple-element.72), channel_id=1, source_target_pairs={{0,4},{4,0},{8,12},{12,8},{16,20},{20,16},{24,28},{28,24},{1,5},{5... | collective-permute-start | bytes 786440 | tf_op jit(solution)/shard_map/ppermute | solution.py:290
  105.2 1.8 %copy-start.2 = (bf16[3,144,2560]{2,1,0:T(8,128)(2,1)S(1)}, bf16[3,144,2560]{2,1,0:T(8,128)(2,1)}, u32[]{:S(2)}) copy-start(bf16[3,144,2560]{2,1,0:T(8,128)(2,1)} %copy-done.1) | copy-start | bytes 6635524
  106.9 7.8 %collective-permute-start.15 = (f32[2,4,640]{2,1,0:T(4,128)}, f32[2,4,640]{2,1,0:T(4,128)S(1)}, u32[]{:S(2)}, u32[]{:S(2)}) collective-permute-start(f32[2,4,640]{2,1,0:T(4,128)} %frame_lines.1), channel_id=1, source_target_pairs={{0,8},{4,12},{8,0},{12,4},{16,24},{20,28},{24,16},{28,20},{1,9},{5... | collective-permute-start | bytes 61448 | tf_op jit(solution)/shard_map/ppermute | solution.py:109
  107.0 1.1 copy-start.4
  108.1 1.1 copy-start.6
  109.2 1.3 copy-start.17
  110.5 1.0 copy-start.32
  110.5 4.2 %copy-start.33 = (f32[2,4,640]{2,1,0:T(4,128)S(1)}, f32[2,4,640]{2,1,0:T(4,128)}, u32[]{:S(2)}) copy-start(f32[2,4,640]{2,1,0:T(4,128)} %frame_lines.1) | copy-start | bytes 61444
  110.5 5.3 %copy-start.30 = (f32[512,1024]{1,0:T(8,128)S(1)}, f32[512,1024]{1,0:T(8,128)}, u32[]{:S(2)}) copy-start(f32[512,1024]{1,0:T(8,128)} %copy-done.29) | copy-start | bytes 6291460
  111.5 5.0 %copy-start.15 = (bf16[1280,1024]{1,0:T(8,128)(2,1)S(1)}, bf16[1280,1024]{1,0:T(8,128)(2,1)}, u32[]{:S(2)}) copy-start(bf16[1280,1024]{1,0:T(8,128)(2,1)} %copy-done.13) | copy-start | bytes 7864324
  111.6 15.5 %collective-permute-start.21 = (bf16[512,256]{1,0:T(8,128)(2,1)S(1)}, bf16[512,256]{1,0:T(8,128)(2,1)S(1)}, u32[]{:S(2)}, u32[]{:S(2)}) collective-permute-start(bf16[512,256]{1,0:T(8,128)(2,1)S(1)} %copy-done.32), channel_id=1, source_target_pairs={{0,4},{4,0},{8,12},{12,8},{16,20},{20,16},{24,28},{28,24},{1,5},{5... | collective-permute-start | bytes 786440 | tf_op jit(solution)/shard_map/ppermute | solution.py:290
  116.3 5.0 %collective-permute-start.17 = (f32[4,4,640]{2,1,0:T(4,128)S(1)}, f32[4,4,640]{2,1,0:T(4,128)S(1)}, u32[]{:S(2)}, u32[]{:S(2)}) collective-permute-start(f32[4,4,640]{2,1,0:T(4,128)S(1)} %pad_maximum_fusion.3), channel_id=1, source_target_pairs={{0,16},{4,20},{8,24},{12,28},{16,0},{20,4},{24,8},{28,12},{1,17},{... | collective-permute-start | bytes 122888 | tf_op jit(solution)/shard_map/ppermute | solution.py:109
  118.7 10.3 %collective-permute-start.19 = (bf16[512,256]{1,0:T(8,128)(2,1)S(1)}, bf16[512,256]{1,0:T(8,128)(2,1)S(1)}, u32[]{:S(2)}, u32[]{:S(2)}) collective-permute-start(bf16[512,256]{1,0:T(8,128)(2,1)S(1)} %fusion.9), channel_id=1, source_target_pairs={{0,4},{4,0},{8,12},{12,8},{16,20},{20,16},{24,28},{28,24},{1,5},{5... | collective-permute-start | bytes 786440 | tf_op jit(solution)/shard_map/ppermute | solution.py:290
  122.8 1.0 copy-start.12
  123.2 2.5 %copy-start.10 = (bf16[640,256]{1,0:T(8,128)(2,1)S(1)}, bf16[640,256]{1,0:T(8,128)(2,1)}, u32[]{:S(2)}) copy-start(bf16[640,256]{1,0:T(8,128)(2,1)} %copy-done.9) | copy-start | bytes 983044
  124.1 7.8 %collective-permute-start.20 = (bf16[512,256]{1,0:T(8,128)(2,1)S(1)}, bf16[512,256]{1,0:T(8,128)(2,1)S(1)}, u32[]{:S(2)}, u32[]{:S(2)}) collective-permute-start(bf16[512,256]{1,0:T(8,128)(2,1)S(1)} %fusion.10), channel_id=1, source_target_pairs={{0,4},{4,0},{8,12},{12,8},{16,20},{20,16},{24,28},{28,24},{1,5},{5... | collective-permute-start | bytes 786440 | tf_op jit(solution)/shard_map/ppermute | solution.py:290

commit v5 on v4

--- a/solution.py
+++ b/solution.py
@@ -387,7 +387,7 @@
             sent = after(sent, packed, *parts)
         if index == 3:
             packed = clip_step(packed, dp, 4, (parts[2],))
-            sent = after(sent, packed, mine_sum)
+            sent = after(sent, mine_sum)
         rows.append(last_rows(y, is_mid, width, sent, arrived, offset))
         parts.append(finish(other_sum, other[2], index))
         received.append(over_y(parts[index]))

time: 134 us -> 137 us (1.022)
    unnamed x77 -> x75, local copies, waits for them, and re-layouts: 8.75 us -> 9.48 us
where the time goes in v5:
time: 137 us; the launch traced here: 136 us
  waiting for transfers between devices  58.8 us (43%)
  starting transfers between devices  30.8 us (22%)
  Pallas kernels  16.2 us (12%)
  matrix products  13.8 us (10%)
  local copies, waits for them, and re-layouts  12 us (9%)
  other arithmetic  3.35 us (2%)
  between operations  1.41 us (1%)
    ppermute x11, waiting for transfers between devices, along_z(): return lax.ppermute(array, 'dp', perm)  32.8 us
    ppermute x11, starting transfers between devices, along_z(): return lax.ppermute(array, 'dp', perm)  18.1 us
    ppermute x6, waiting for transfers between devices, over_y(): return lax.ppermute(array, 'dp', [(i, i ^ 1) for i in range(dp)])  14.5 us
    unnamed x75, local copies, waits for them, and re-layouts  9.48 us
    ppermute x6, starting transfers between devices, over_y(): return lax.ppermute(array, 'dp', [(i, i ^ 1) for i in range(dp)])  8.23 us
    ppermute x4, waiting for transfers between devices, over_seq(): return lax.ppermute(array, 'seq', [(i, i ^ flip) for i in range(seq)])  7.72 us
    dot_general x8, matrix products, finish(): jnp.dot(tokens_last, rows[index], preferred_element_type=jnp.float32)  5.06 us
    pallas_call x2, Pallas kernels, block_rows(): pl.pallas_call(kernel, out_shape=jax.ShapeDtypeStruct((2 * rows * len(blo...  3.86 us
  transfers between devices with their start and end apart: 23, of which 9 were waited for; matrix products, arithmetic and copies ran while one was open for 13% of the time, Pallas kernels for 11%

profile of v5, /device:TPU:0, one launch (start us, length us, event | category | flops | bytes accessed | tf_op | source)
XLA Modules:
  0.0 136.3 jit_solution(5918201761235092007)
XLA Ops:
  0.7 2.3 %dynamic-slice_bitcast_fusion = (bf16[320,1024]{1,0:T(8,128)(2,1)S(1)}, bf16[320,1024]{1,0:T(8,128)(2,1)}) fusion(bf16[2048,320]{0,1:T(8,128)(2,1)} %param.9, s32[]{:T(128)S(6)} %select_n.44, s32[]{:T(128)S(6)} %select_n.43), kind=kLoop, calls=%fused_computation.12 | loop fusion | bytes 2621448 | tf_op jit(solution)/shard_map/dynamic_slice | solution.py:301
  3.0 3.0 %collective-permute-start.1 = (bf16[320,1024]{1,0:T(8,128)(2,1)S(1)}, bf16[320,1024]{1,0:T(8,128)(2,1)S(1)}, u32[]{:S(2)}, u32[]{:S(2)}) collective-permute-start(bf16[320,1024]{1,0:T(8,128)(2,1)S(1)} %get-tuple-element.75.refs_0_), channel_id=1, source_target_pairs={{0,8},{4,12},{8,0},{12,4},{16,24},{20,28},{24,16},{28,20},{1,9},{5... | collective-permute-start | bytes 1966088 | tf_op jit(solution)/shard_map/ppermute | solution.py:287
  6.0 1.5 %collective-permute-start.2 = (bf16[320,1024]{1,0:T(8,128)(2,1)S(1)}, bf16[320,1024]{1,0:T(8,128)(2,1)}, u32[]{:S(2)}, u32[]{:S(2)}) collective-permute-start(bf16[320,1024]{1,0:T(8,128)(2,1)S(1)} %get-tuple-element.75.refs_0_), channel_id=1, source_target_pairs={{8,16},{12,20},{16,8},{20,12},{9,17},{13,21},{17,9},{21,13},{10,18... | collective-permute-start | bytes 1966088 | tf_op jit(solution)/shard_map/ppermute | solution.py:287
  7.5 1.5 %collective-permute-start = (bf16[320,1024]{1,0:T(8,128)(2,1)}, bf16[320,1024]{1,0:T(8,128)(2,1)}, u32[]{:S(2)}, u32[]{:S(2)}) collective-permute-start(bf16[320,1024]{1,0:T(8,128)(2,1)} %get-tuple-element.76), channel_id=1, source_target_pairs={{0,4},{4,0},{8,12},{12,8},{16,20},{20,16},{24,28},{28,24},{1,5},{5... | collective-permute-start | bytes 1966088 | tf_op jit(solution)/shard_map/ppermute | solution.py:290
  9.4 0.7 fusion
  10.2 1.8 %reduce-precision_convert_fusion.1 = (bf16[3,2560]{1,0:T(4,128)(2,1)S(1)}, bf16[3,2560]{1,0:T(4,128)(2,1)S(1)}, bf16[3,2560]{1,0:T(4,128)(2,1)S(1)}) fusion(bf16[1,128,2560]{2,1,0:T(8,128)(2,1)} %param.8, bf16[1,128,2560]{2,1,0:T(8,128)(2,1)S(1)} %copy-done.24, s32[128]{0:T(128)S(1)} %bitcast.68), kind=kOutput, calls=%fused_computation.44 | convolution fusion | flops 12841344 | bytes 1357312 | tf_op jit(solution)/shard_map/dot_general | solution.py:27
  12.3 11.7 %collective-permute-done.refs_1_ = bf16[320,1024]{1,0:T(8,128)(2,1)} collective-permute-done((bf16[320,1024]{1,0:T(8,128)(2,1)}, bf16[320,1024]{1,0:T(8,128)(2,1)}, u32[]{:S(2)}, u32[]{:S(2)}) %collective-permute-start) | collective-permute-done | bytes 655392 | tf_op jit(solution)/shard_map/ppermute | solution.py:290
  24.1 0.8 copy-done.22
  24.9 1.5 %collective-permute-start.3 = (bf16[144,2560]{1,0:T(8,128)(2,1)S(1)}, bf16[144,2560]{1,0:T(8,128)(2,1)S(1)}, u32[]{:S(2)}, u32[]{:S(2)}) collective-permute-start(bf16[144,2560]{1,0:T(8,128)(2,1)S(1)} %pad_maximum_fusion.1.refs_0_), channel_id=1, source_target_pairs={{0,2},{1,3},{2,0},{3,1},{4,6},{5,7},{6,4},{7,5},{8,10},{9,11},{10,... | collective-permute-start | bytes 2211848 | tf_op jit(solution)/shard_map/ppermute | solution.py:293
  26.4 1.5 %collective-permute-start.4 = (bf16[144,2560]{1,0:T(8,128)(2,1)S(1)}, bf16[144,2560]{1,0:T(8,128)(2,1)S(1)}, u32[]{:S(2)}, u32[]{:S(2)}) collective-permute-start(bf16[144,2560]{1,0:T(8,128)(2,1)S(1)} %pad_maximum_fusion.1.refs_0_), channel_id=1, source_target_pairs={{0,4},{4,0},{8,12},{12,8},{16,20},{20,16},{24,28},{28,24},{1,5},{5... | collective-permute-start | bytes 2211848 | tf_op jit(solution)/shard_map/ppermute | solution.py:290
  27.9 3.3 %collective-permute-start.5 = (bf16[320,1024]{1,0:T(8,128)(2,1)}, bf16[320,1024]{1,0:T(8,128)(2,1)}, u32[]{:S(2)}, u32[]{:S(2)}) collective-permute-start(bf16[320,1024]{1,0:T(8,128)(2,1)} %collective-permute-done.refs_1_), channel_id=1, source_target_pairs={{0,8},{4,12},{8,0},{12,4},{16,24},{20,28},{24,16},{28,20},{1,9},{5... | collective-permute-start | bytes 1966088 | tf_op jit(solution)/shard_map/ppermute | solution.py:287
  31.3 1.5 %collective-permute-start.6 = (bf16[320,1024]{1,0:T(8,128)(2,1)}, bf16[320,1024]{1,0:T(8,128)(2,1)}, u32[]{:S(2)}, u32[]{:S(2)}) collective-permute-start(bf16[320,1024]{1,0:T(8,128)(2,1)} %collective-permute-done.refs_1_), channel_id=1, source_target_pairs={{8,16},{12,20},{16,8},{20,12},{9,17},{13,21},{17,9},{21,13},{10,18... | collective-permute-start | bytes 1966088 | tf_op jit(solution)/shard_map/ppermute | solution.py:287
  32.7 1.5 %collective-permute-start.7 = (bf16[320,1024]{1,0:T(8,128)(2,1)}, bf16[320,1024]{1,0:T(8,128)(2,1)}, u32[]{:S(2)}, u32[]{:S(2)}) collective-permute-start(bf16[320,1024]{1,0:T(8,128)(2,1)} %copy-done.22), channel_id=1, source_target_pairs={{8,16},{12,20},{16,8},{20,12},{9,17},{13,21},{17,9},{21,13},{10,18... | collective-permute-start | bytes 1966088 | tf_op jit(solution)/shard_map/ppermute | solution.py:287
  34.2 7.7 %collective-permute-done.3.refs_2_ = bf16[144,2560]{1,0:T(8,128)(2,1)S(1)} collective-permute-done((bf16[144,2560]{1,0:T(8,128)(2,1)S(1)}, bf16[144,2560]{1,0:T(8,128)(2,1)S(1)}, u32[]{:S(2)}, u32[]{:S(2)}) %collective-permute-start.3) | collective-permute-done | bytes 737312 | tf_op jit(solution)/shard_map/ppermute | solution.py:293
  42.0 1.3 collective-permute-start.8
  43.4 0.9 collective-permute-done.5.refs_3_
  44.3 14.8 %collective-permute-done.8.refs_2_ = bf16[320,1024]{1,0:T(8,128)(2,1)} collective-permute-done((bf16[320,1024]{1,0:T(8,128)(2,1)}, bf16[320,1024]{1,0:T(8,128)(2,1)}, u32[]{:S(2)}, u32[]{:S(2)}) %collective-permute-start.8) | collective-permute-done | bytes 655392 | tf_op jit(solution)/shard_map/ppermute | solution.py:287
  59.0 1.5 %collective-permute-start.11 = (bf16[144,2560]{1,0:T(8,128)(2,1)S(1)}, bf16[144,2560]{1,0:T(8,128)(2,1)}, u32[]{:S(2)}, u32[]{:S(2)}) collective-permute-start(bf16[144,2560]{1,0:T(8,128)(2,1)S(1)} %collective-permute-done.4.refs_0_.refs_4_), channel_id=1, source_target_pairs={{0,2},{1,3},{2,0},{3,1},{4,6},{5,7},{6,4},{7,5},{8,10},{9,11},{10,... | collective-permute-start | bytes 2211848 | tf_op jit(solution)/shard_map/ppermute | solution.py:293
  60.5 1.3 collective-permute-start.10
  61.8 0.7 collective-permute-start.9
  62.5 1.3 fusion.63
  63.8 1.5 %block_rows.2 = bf16[1280,1024]{1,0:T(8,128)(2,1)S(1)} custom-call(s32[2]{0:T(128)S(1)} %pad_add_fusion.place, bf16[320,1024]{1,0:T(8,128)(2,1)S(1)} %get-tuple-element.75.refs_0_, bf16[320,1024]{1,0:T(8,128)(2,1)} %collective-permute-done.refs_1_, bf16[320,1024]{1,0:T(8,128)(2,1)S(1)} %copy-done.23, bf16[320,1024]{1,0:T(8,128)(2,1)} %collective-permute-done.5.refs_3_), custom_call_target="tpu_custom_call" | custom-call | tf_op jit(solution)/shard_map/block_rows/pallas_call | solution.py:173
  65.3 1.8 %pad_maximum_fusion = bf16[3,144,2560]{2,1,0:T(8,128)(2,1)} fusion(bf16[1,144,2560]{2,1,0:T(8,128)(2,1)S(1)} %bitcast.64, bf16[1,144,2560]{2,1,0:T(8,128)(2,1)S(1)} %bitcast.63, bf16[1,144,2560]{2,1,0:T(8,128)(2,1)S(1)} %fusion.63), kind=kLoop, calls=%fused_computation.3 | loop fusion | flops 2211840 | bytes 4423680 | tf_op jit(solution)/shard_map/stack | solution.py:341
  67.5 8.4 %collective-permute-done.10.refs_3_ = bf16[320,1024]{1,0:T(8,128)(2,1)S(1)} collective-permute-done((bf16[320,1024]{1,0:T(8,128)(2,1)}, bf16[320,1024]{1,0:T(8,128)(2,1)S(1)}, u32[]{:S(2)}, u32[]{:S(2)}) %collective-permute-start.10) | collective-permute-done | bytes 655392 | tf_op jit(solution)/shard_map/ppermute | solution.py:287
  75.9 0.8 copy-done.20
  76.7 0.8 copy-done.18
  77.6 0.5 collective-permute-start.13
  78.1 1.1 copy-done.19
  79.2 2.0 %slice_rows.1 = (bf16[640,512]{1,0:T(8,128)(2,1)S(1)}, bf16[640,256]{1,0:T(8,128)(2,1)}, bf16[640,256]{1,0:T(8,128)(2,1)}) custom-call(bf16[320,1024]{1,0:T(8,128)(2,1)} %collective-permute-done.7.upper, bf16[320,1024]{1,0:T(8,128)(2,1)S(1)} %copy-done.19), custom_call_target="tpu_custom_call" | custom-call | tf_op jit(solution)/shard_map/slice_rows/pallas_call | solution.py:138
  81.2 1.3 collective-permute-start.14
  82.5 1.3 collective-permute-start.17
  83.8 1.4 %collective-permute-start.15 = (bf16[640,256]{1,0:T(8,128)(2,1)}, bf16[640,256]{1,0:T(8,128)(2,1)}, u32[]{:S(2)}, u32[]{:S(2)}) collective-permute-start(bf16[640,256]{1,0:T(8,128)(2,1)} %get-tuple-element.54.sent), channel_id=1, source_target_pairs={{8,0},{12,4},{16,24},{20,28},{9,1},{13,5},{17,25},{21,29},{10,2},{... | collective-permute-start | bytes 983048 | tf_op jit(solution)/shard_map/ppermute | solution.py:287
  85.3 2.4 %block_rows.3 = bf16[640,1024]{1,0:T(8,128)(2,1)S(1)} custom-call(s32[2]{0:T(128)S(1)} %pad_add_fusion.place, bf16[320,1024]{1,0:T(8,128)(2,1)} %collective-permute-done.2.refs_0_, bf16[320,1024]{1,0:T(8,128)(2,1)} %collective-permute-done.6.refs_1_, bf16[320,1024]{1,0:T(8,128)(2,1)} %collective-permute-done.8.refs_2_, bf16[320,1024]{1,0:T(8,128)(2,1)S(1)} %copy-done.21), custom_call_target="tpu_custom_call" | custom-call | tf_op jit(solution)/shard_map/block_rows/pallas_call | solution.py:173
  87.7 1.8 %order_pieces.3 = (bf16[512,1280]{1,0:T(8,128)(2,1)S(1)}, bf16[512,640]{1,0:T(8,128)(2,1)S(1)}, bf16[512,640]{1,0:T(8,128)(2,1)S(1)}) custom-call(s32[1]{0:T(128)} %bitcast.1.place, bf16[144,2560]{1,0:T(8,128)(2,1)S(1)} %copy-done.8, bf16[3,144,2560]{2,1,0:T(8,128)(2,1)S(1)} %collective-permute-done.12.refs_1_.refs_3_.refs_5_, ...), custom_call_target="tpu_custom_call" | custom-call | tf_op jit(solution)/shard_map/order_pieces/pallas_call | solution.py:228
  89.6 1.0 fusion.29
  90.5 0.7 copy-done.14
  91.3 1.5 %convolution_add_fusion.2 = f32[512,1024]{1,0:T(8,128)S(1)} fusion(f32[512,1024]{1,0:T(8,128)S(1)} %fusion.29, bf16[512,1280]{1,0:T(8,128)(2,1)S(1)} %get-tuple-element.42, bf16[1280,1024]{1,0:T(8,128)(2,1)S(1)} %copy-done.14), kind=kOutput, calls=%fused_computation.6 | convolution fusion | flops 1342701568 | bytes 8126464 | tf_op jit(solution)/shard_map/dot_general | solution.py:354
  92.9 8.0 %collective-permute-done.14.arrived = bf16[640,512]{1,0:T(8,128)(2,1)S(1)} collective-permute-done((bf16[640,512]{1,0:T(8,128)(2,1)S(1)}, bf16[640,512]{1,0:T(8,128)(2,1)S(1)}, u32[]{:S(2)}, u32[]{:S(2)}) %collective-permute-start.14) | collective-permute-done | bytes 655392 | tf_op jit(solution)/shard_map/ppermute | solution.py:287
  100.9 0.6 last_rows.4
  101.9 0.6 last_rows.6
  102.5 1.2 fusion.9
  103.7 1.5 %collective-permute-start.21 = (bf16[512,256]{1,0:T(8,128)(2,1)}, bf16[512,256]{1,0:T(8,128)(2,1)}, u32[]{:S(2)}, u32[]{:S(2)}) collective-permute-start(bf16[512,256]{1,0:T(8,128)(2,1)} %get-tuple-element.74), channel_id=1, source_target_pairs={{0,4},{4,0},{8,12},{12,8},{16,20},{20,16},{24,28},{28,24},{1,5},{5... | collective-permute-start | bytes 786440 | tf_op jit(solution)/shard_map/ppermute | solution.py:290
  105.2 1.7 %frame_lines.1 = f32[2,4,640]{2,1,0:T(4,128)} custom-call(s32[1]{0:T(128)} %bitcast.1.place, bf16[144,2560]{1,0:T(8,128)(2,1)} %copy-done.3, bf16[3,144,2560]{2,1,0:T(8,128)(2,1)} %copy-done.1, bf16[144,2560]{1,0:T(8,128)(2,1)} %copy-done.5, bf16[3,144,2560]{2,1,0:T(8,128)(2,1)} %copy-done.1, bf16[144,2560]{1,0:T(8,128)(2,1)} %copy-done.7, ...), custom_call_target="tpu_custom_call" | custom-call | tf_op jit(solution)/shard_map/frame_lines/pallas_call | solution.py:94
  107.0 1.1 copy-done.4
  108.1 1.1 copy-done.6
  109.2 0.4 order_pieces.2
  109.6 0.9 copy-done.17
  110.5 1.0 fusion.31
  111.5 0.7 copy-done.15
  112.3 1.5 %convolution_add_fusion.1 = f32[512,1024]{1,0:T(8,128)S(1)} fusion(f32[512,1024]{1,0:T(8,128)S(1)} %fusion.31, bf16[512,1280]{1,0:T(8,128)(2,1)S(1)} %get-tuple-element.50, bf16[1280,1024]{1,0:T(8,128)(2,1)S(1)} %copy-done.15), kind=kOutput, calls=%fused_computation.5 | convolution fusion | flops 1342701568 | bytes 8126464 | tf_op jit(solution)/shard_map/dot_general | solution.py:354
  113.8 0.8 collective-permute-done.15.arrived
  114.6 1.1 last_rows.5
  116.1 1.6 %collective-permute-start.20 = (bf16[512,256]{1,0:T(8,128)(2,1)S(1)}, bf16[512,256]{1,0:T(8,128)(2,1)S(1)}, u32[]{:S(2)}, u32[]{:S(2)}) collective-permute-start(bf16[512,256]{1,0:T(8,128)(2,1)S(1)} %copy-done.32), channel_id=1, source_target_pairs={{0,4},{4,0},{8,12},{12,8},{16,20},{20,16},{24,28},{28,24},{1,5},{5... | collective-permute-start | bytes 786440 | tf_op jit(solution)/shard_map/ppermute | solution.py:290
  117.7 0.6 copy.12
  118.4 1.1 last_rows.7
  119.5 1.6 %fusion.7 = (bf16[512,256]{1,0:T(8,128)(2,1)S(1)}, bf16[512,256]{1,0:T(8,128)(2,1)S(1)}) fusion(f32[512,1024]{1,0:T(8,128)} %copy-done.30, f32[512,256]{1,0:T(8,128)S(1)} %fusion.32, bf16[512,640]{1,0:T(8,128)(2,1)S(1)} %get-tuple-element.45, bf16[640,256]{1,0:T(8,128)(2,1)S(1)} %last_rows.7), kind=kOutput, calls=%fused_computation.19 | convolution fusion | flops 168296448 | bytes 3080192 | tf_op jit(solution)/shard_map/dot_general | solution.py:379
  122.5 0.6 collective-permute-start.18
  123.0 1.5 %collective-permute-start.19 = (bf16[512,256]{1,0:T(8,128)(2,1)S(1)}, bf16[512,256]{1,0:T(8,128)(2,1)S(1)}, u32[]{:S(2)}, u32[]{:S(2)}) collective-permute-start(bf16[512,256]{1,0:T(8,128)(2,1)S(1)} %get-tuple-element.72), channel_id=1, source_target_pairs={{0,4},{4,0},{8,12},{12,8},{16,20},{20,16},{24,28},{28,24},{1,5},{5... | collective-permute-start | bytes 786440 | tf_op jit(solution)/shard_map/ppermute | solution.py:290
  124.6 0.9 collective-permute-start.22
  125.9 3.7 %collective-permute-done.22 = f32[4,4,640]{2,1,0:T(4,128)S(1)} collective-permute-done((f32[4,4,640]{2,1,0:T(4,128)S(1)}, f32[4,4,640]{2,1,0:T(4,128)S(1)}, u32[]{:S(2)}, u32[]{:S(2)}) %collective-permute-start.22) | collective-permute-done | bytes 40992 | tf_op jit(solution)/shard_map/ppermute | solution.py:109
  129.8 0.8 fusion.24
  130.6 1.9 %place_columns.2.refs_4_ = bf16[512,2048]{1,0:T(8,128)(2,1)} custom-call(s32[1]{0:T(128)} %bitcast.13.place, bf16[512,256]{1,0:T(8,128)(2,1)S(1)} %get-tuple-element.68.refs_0_, bf16[512,256]{1,0:T(8,128)(2,1)S(1)} %get-tuple-element.67.refs_1_, bf16[512,256]{1,0:T(8,128)(2,1)S(1)} %collective-permute-done.20.refs_2_, ...), custom_call_target="tpu_custom_call" | custom-call | tf_op jit(solution)/shard_map/place_columns/pallas_call | solution.py:262
  132.6 2.8 %collective-permute-done.19.refs_3_ = bf16[512,256]{1,0:T(8,128)(2,1)S(1)} collective-permute-done((bf16[512,256]{1,0:T(8,128)(2,1)S(1)}, bf16[512,256]{1,0:T(8,128)(2,1)S(1)}, u32[]{:S(2)}, u32[]{:S(2)}) %collective-permute-start.19) | collective-permute-done | bytes 262176 | tf_op jit(solution)/shard_map/ppermute | solution.py:290
  135.3 1.0 place_columns.3
  (101 shorter events, 3.8 us)
Async XLA Ops:
  0.6 8.4 %copy-start = (f32[64,2560]{1,0:T(8,128)S(1)}, f32[64,2560]{1,0:T(8,128)}, u32[]{:S(2)}) copy-start(f32[64,2560]{1,0:T(8,128)} %param.11) | copy-start | bytes 1966084
  0.6 8.4 %copy-start.35 = (s32[1,3]{1,0:T(1,128)S(1)}, s32[1,3]{1,0:T(1,128)}, u32[]{:S(2)}) copy-start(s32[1,3]{1,0:T(1,128)} %param.13) | copy-start | bytes 40
  0.7 8.4 %copy-start.33 = (f32[2560]{0:T(1024)S(1)}, f32[2560]{0:T(1024)}, u32[]{:S(2)}) copy-start(f32[2560]{0:T(1024)} %param.10) | copy-start | bytes 30724
  0.7 8.7 %copy-start.24 = (bf16[1,128,2560]{2,1,0:T(8,128)(2,1)S(1)}, bf16[1,128,2560]{2,1,0:T(8,128)(2,1)}, u32[]{:S(2)}) copy-start(bf16[1,128,2560]{2,1,0:T(8,128)(2,1)} %param.7) | copy-start | bytes 1966084
  0.7 8.7 %copy-start.34 = (s32[1,128]{1,0:T(1,128)S(1)}, s32[1,128]{1,0:T(1,128)}, u32[]{:S(2)}) copy-start(s32[1,128]{1,0:T(1,128)} %param.12) | copy-start | bytes 1540
  3.0 21.0 %collective-permute-start.1 = (bf16[320,1024]{1,0:T(8,128)(2,1)S(1)}, bf16[320,1024]{1,0:T(8,128)(2,1)S(1)}, u32[]{:S(2)}, u32[]{:S(2)}) collective-permute-start(bf16[320,1024]{1,0:T(8,128)(2,1)S(1)} %get-tuple-element.75.refs_0_), channel_id=1, source_target_pairs={{0,8},{4,12},{8,0},{12,4},{16,24},{20,28},{24,16},{28,20},{1,9},{5... | collective-permute-start | bytes 1966088 | tf_op jit(solution)/shard_map/ppermute | solution.py:287
  6.0 18.0 %collective-permute-start.2 = (bf16[320,1024]{1,0:T(8,128)(2,1)S(1)}, bf16[320,1024]{1,0:T(8,128)(2,1)}, u32[]{:S(2)}, u32[]{:S(2)}) collective-permute-start(bf16[320,1024]{1,0:T(8,128)(2,1)S(1)} %get-tuple-element.75.refs_0_), channel_id=1, source_target_pairs={{8,16},{12,20},{16,8},{20,12},{9,17},{13,21},{17,9},{21,13},{10,18... | collective-permute-start | bytes 1966088 | tf_op jit(solution)/shard_map/ppermute | solution.py:287
  7.5 16.5 %collective-permute-start = (bf16[320,1024]{1,0:T(8,128)(2,1)}, bf16[320,1024]{1,0:T(8,128)(2,1)}, u32[]{:S(2)}, u32[]{:S(2)}) collective-permute-start(bf16[320,1024]{1,0:T(8,128)(2,1)} %get-tuple-element.76), channel_id=1, source_target_pairs={{0,4},{4,0},{8,12},{12,8},{16,20},{20,16},{24,28},{28,24},{1,5},{5... | collective-permute-start | bytes 1966088 | tf_op jit(solution)/shard_map/ppermute | solution.py:290
  12.1 29.8 %copy-start.25 = (bf16[128,640]{1,0:T(8,128)(2,1)}, bf16[128,640]{1,0:T(8,128)(2,1)S(1)}, u32[]{:S(2)}) copy-start(bf16[128,640]{1,0:T(8,128)(2,1)S(1)} %get-tuple-element.77) | copy-start | bytes 491524
  12.1 29.8 %copy-start.26 = (bf16[128,640]{1,0:T(8,128)(2,1)}, bf16[128,640]{1,0:T(8,128)(2,1)S(1)}, u32[]{:S(2)}) copy-start(bf16[128,640]{1,0:T(8,128)(2,1)S(1)} %get-tuple-element.78) | copy-start | bytes 491524
  12.2 29.8 %copy-start.27 = (bf16[128,640]{1,0:T(8,128)(2,1)}, bf16[128,640]{1,0:T(8,128)(2,1)S(1)}, u32[]{:S(2)}) copy-start(bf16[128,640]{1,0:T(8,128)(2,1)S(1)} %get-tuple-element.79) | copy-start | bytes 491524
  12.2 29.8 %copy-start.28 = (bf16[128,640]{1,0:T(8,128)(2,1)}, bf16[128,640]{1,0:T(8,128)(2,1)S(1)}, u32[]{:S(2)}) copy-start(bf16[128,640]{1,0:T(8,128)(2,1)S(1)} %get-tuple-element.80) | copy-start | bytes 491524
  12.3 29.7 %copy-start.29 = (bf16[16,2560]{1,0:T(8,128)(2,1)}, bf16[16,2560]{1,0:T(8,128)(2,1)S(1)}, u32[]{:S(2)}) copy-start(bf16[16,2560]{1,0:T(8,128)(2,1)S(1)} %fusion.19) | copy-start | bytes 245764
  12.3 52.9 %copy-start.3 = (bf16[144,2560]{1,0:T(8,128)(2,1)}, bf16[144,2560]{1,0:T(8,128)(2,1)S(1)}, u32[]{:S(2)}) copy-start(bf16[144,2560]{1,0:T(8,128)(2,1)S(1)} %pad_maximum_fusion.1.refs_0_) | copy-start | bytes 2211844
  24.1 0.8 copy-start.22
  24.9 17.0 %collective-permute-start.3 = (bf16[144,2560]{1,0:T(8,128)(2,1)S(1)}, bf16[144,2560]{1,0:T(8,128)(2,1)S(1)}, u32[]{:S(2)}, u32[]{:S(2)}) collective-permute-start(bf16[144,2560]{1,0:T(8,128)(2,1)S(1)} %pad_maximum_fusion.1.refs_0_), channel_id=1, source_target_pairs={{0,2},{1,3},{2,0},{3,1},{4,6},{5,7},{6,4},{7,5},{8,10},{9,11},{10,... | collective-permute-start | bytes 2211848 | tf_op jit(solution)/shard_map/ppermute | solution.py:293
  26.4 17.9 %collective-permute-start.4 = (bf16[144,2560]{1,0:T(8,128)(2,1)S(1)}, bf16[144,2560]{1,0:T(8,128)(2,1)S(1)}, u32[]{:S(2)}, u32[]{:S(2)}) collective-permute-start(bf16[144,2560]{1,0:T(8,128)(2,1)S(1)} %pad_maximum_fusion.1.refs_0_), channel_id=1, source_target_pairs={{0,4},{4,0},{8,12},{12,8},{16,20},{20,16},{24,28},{28,24},{1,5},{5... | collective-permute-start | bytes 2211848 | tf_op jit(solution)/shard_map/ppermute | solution.py:290
  27.9 16.3 %collective-permute-start.5 = (bf16[320,1024]{1,0:T(8,128)(2,1)}, bf16[320,1024]{1,0:T(8,128)(2,1)}, u32[]{:S(2)}, u32[]{:S(2)}) collective-permute-start(bf16[320,1024]{1,0:T(8,128)(2,1)} %collective-permute-done.refs_1_), channel_id=1, source_target_pairs={{0,8},{4,12},{8,0},{12,4},{16,24},{20,28},{24,16},{28,20},{1,9},{5... | collective-permute-start | bytes 1966088 | tf_op jit(solution)/shard_map/ppermute | solution.py:287
  31.3 13.0 %collective-permute-start.6 = (bf16[320,1024]{1,0:T(8,128)(2,1)}, bf16[320,1024]{1,0:T(8,128)(2,1)}, u32[]{:S(2)}, u32[]{:S(2)}) collective-permute-start(bf16[320,1024]{1,0:T(8,128)(2,1)} %collective-permute-done.refs_1_), channel_id=1, source_target_pairs={{8,16},{12,20},{16,8},{20,12},{9,17},{13,21},{17,9},{21,13},{10,18... | collective-permute-start | bytes 1966088 | tf_op jit(solution)/shard_map/ppermute | solution.py:287
  32.7 11.5 %collective-permute-start.7 = (bf16[320,1024]{1,0:T(8,128)(2,1)}, bf16[320,1024]{1,0:T(8,128)(2,1)}, u32[]{:S(2)}, u32[]{:S(2)}) collective-permute-start(bf16[320,1024]{1,0:T(8,128)(2,1)} %copy-done.22), channel_id=1, source_target_pairs={{8,16},{12,20},{16,8},{20,12},{9,17},{13,21},{17,9},{21,13},{10,18... | collective-permute-start | bytes 1966088 | tf_op jit(solution)/shard_map/ppermute | solution.py:287
  42.0 23.3 %copy-start.5 = (bf16[144,2560]{1,0:T(8,128)(2,1)}, bf16[144,2560]{1,0:T(8,128)(2,1)S(1)}, u32[]{:S(2)}) copy-start(bf16[144,2560]{1,0:T(8,128)(2,1)S(1)} %collective-permute-done.3.refs_2_) | copy-start | bytes 2211844
  42.0 17.1 %collective-permute-start.8 = (bf16[320,1024]{1,0:T(8,128)(2,1)}, bf16[320,1024]{1,0:T(8,128)(2,1)}, u32[]{:S(2)}, u32[]{:S(2)}) collective-permute-start(bf16[320,1024]{1,0:T(8,128)(2,1)} %collective-permute-done.2.refs_0_), channel_id=1, source_target_pairs={{8,0},{12,4},{16,24},{20,28},{9,1},{13,5},{17,25},{21,29},{10,2},{... | collective-permute-start | bytes 1966088 | tf_op jit(solution)/shard_map/ppermute | solution.py:287
  43.3 20.5 %copy-start.23 = (bf16[320,1024]{1,0:T(8,128)(2,1)S(1)}, bf16[320,1024]{1,0:T(8,128)(2,1)}, u32[]{:S(2)}) copy-start(bf16[320,1024]{1,0:T(8,128)(2,1)} %copy-done.22) | copy-start | bytes 1966084
  44.3 21.0 %copy-start.7 = (bf16[144,2560]{1,0:T(8,128)(2,1)}, bf16[144,2560]{1,0:T(8,128)(2,1)S(1)}, u32[]{:S(2)}) copy-start(bf16[144,2560]{1,0:T(8,128)(2,1)S(1)} %collective-permute-done.4.refs_0_.refs_4_) | copy-start | bytes 2211844
  59.0 18.5 %collective-permute-start.11 = (bf16[144,2560]{1,0:T(8,128)(2,1)S(1)}, bf16[144,2560]{1,0:T(8,128)(2,1)}, u32[]{:S(2)}, u32[]{:S(2)}) collective-permute-start(bf16[144,2560]{1,0:T(8,128)(2,1)S(1)} %collective-permute-done.4.refs_0_.refs_4_), channel_id=1, source_target_pairs={{0,2},{1,3},{2,0},{3,1},{4,6},{5,7},{6,4},{7,5},{8,10},{9,11},{10,... | collective-permute-start | bytes 2211848 | tf_op jit(solution)/shard_map/ppermute | solution.py:293
  60.5 15.3 %collective-permute-start.10 = (bf16[320,1024]{1,0:T(8,128)(2,1)}, bf16[320,1024]{1,0:T(8,128)(2,1)S(1)}, u32[]{:S(2)}, u32[]{:S(2)}) collective-permute-start(bf16[320,1024]{1,0:T(8,128)(2,1)} %collective-permute-done.6.refs_1_), channel_id=1, source_target_pairs={{8,0},{12,4},{16,24},{20,28},{9,1},{13,5},{17,25},{21,29},{10,2},{... | collective-permute-start | bytes 1966088 | tf_op jit(solution)/shard_map/ppermute | solution.py:287
  61.8 14.9 %collective-permute-start.9 = (bf16[320,1024]{1,0:T(8,128)(2,1)}, bf16[320,1024]{1,0:T(8,128)(2,1)S(1)}, u32[]{:S(2)}, u32[]{:S(2)}) collective-permute-start(bf16[320,1024]{1,0:T(8,128)(2,1)} %collective-permute-done.5.refs_3_), channel_id=1, source_target_pairs={{8,16},{12,20},{16,8},{20,12},{9,17},{13,21},{17,9},{21,13},{10,18... | collective-permute-start | bytes 1966088 | tf_op jit(solution)/shard_map/ppermute | solution.py:287
  65.3 2.2 %copy-start.13 = (bf16[1280,1024]{1,0:T(8,128)(2,1)}, bf16[1280,1024]{1,0:T(8,128)(2,1)S(1)}, u32[]{:S(2)}) copy-start(bf16[1280,1024]{1,0:T(8,128)(2,1)S(1)} %block_rows.2) | copy-start | bytes 7864324
  75.9 0.8 copy-start.20
  76.7 0.8 copy-start.18
  77.6 7.7 %collective-permute-start.12 = (bf16[3,144,2560]{2,1,0:T(8,128)(2,1)}, bf16[3,144,2560]{2,1,0:T(8,128)(2,1)S(1)}, u32[]{:S(2)}, u32[]{:S(2)}) collective-permute-start(bf16[3,144,2560]{2,1,0:T(8,128)(2,1)} %pad_maximum_fusion), channel_id=1, source_target_pairs={{0,1},{1,0},{2,3},{3,2},{4,5},{5,4},{6,7},{7,6},{8,9},{9,8},{10,11... | collective-permute-start | bytes 6635528 | tf_op jit(solution)/shard_map/ppermute | solution.py:293
  77.6 10.1 %collective-permute-start.13 = (bf16[144,2560]{1,0:T(8,128)(2,1)}, bf16[144,2560]{1,0:T(8,128)(2,1)}, u32[]{:S(2)}, u32[]{:S(2)}) collective-permute-start(bf16[144,2560]{1,0:T(8,128)(2,1)} %collective-permute-done.11.refs_2_.refs_6_), channel_id=1, source_target_pairs={{0,1},{1,0},{2,3},{3,2},{4,5},{5,4},{6,7},{7,6},{8,9},{9,8},{10,11... | collective-permute-start | bytes 2211848 | tf_op jit(solution)/shard_map/ppermute | solution.py:293
  78.1 1.1 copy-start.19
  79.2 6.1 %copy-start.21 = (bf16[320,1024]{1,0:T(8,128)(2,1)S(1)}, bf16[320,1024]{1,0:T(8,128)(2,1)}, u32[]{:S(2)}) copy-start(bf16[320,1024]{1,0:T(8,128)(2,1)} %copy-done.20) | copy-start | bytes 1966084
  81.2 19.7 %collective-permute-start.14 = (bf16[640,512]{1,0:T(8,128)(2,1)S(1)}, bf16[640,512]{1,0:T(8,128)(2,1)S(1)}, u32[]{:S(2)}, u32[]{:S(2)}) collective-permute-start(bf16[640,512]{1,0:T(8,128)(2,1)S(1)} %get-tuple-element.49.sent), channel_id=1, source_target_pairs={{8,0},{12,4},{16,24},{20,28},{9,1},{13,5},{17,25},{21,29},{10,2},{... | collective-permute-start | bytes 1966088 | tf_op jit(solution)/shard_map/ppermute | solution.py:287
  82.5 35.8 %collective-permute-start.17 = (bf16[640,256]{1,0:T(8,128)(2,1)}, bf16[640,256]{1,0:T(8,128)(2,1)}, u32[]{:S(2)}, u32[]{:S(2)}) collective-permute-start(bf16[640,256]{1,0:T(8,128)(2,1)} %get-tuple-element.58.sent), channel_id=1, source_target_pairs={{8,0},{12,4},{16,24},{20,28},{9,1},{13,5},{17,25},{21,29},{10,2},{... | collective-permute-start | bytes 983048 | tf_op jit(solution)/shard_map/ppermute | solution.py:287
  83.8 3.9 %copy-start.8 = (bf16[144,2560]{1,0:T(8,128)(2,1)S(1)}, bf16[144,2560]{1,0:T(8,128)(2,1)}, u32[]{:S(2)}) copy-start(bf16[144,2560]{1,0:T(8,128)(2,1)} %copy-done.7) | copy-start | bytes 2211844
  83.8 30.8 %collective-permute-start.15 = (bf16[640,256]{1,0:T(8,128)(2,1)}, bf16[640,256]{1,0:T(8,128)(2,1)}, u32[]{:S(2)}, u32[]{:S(2)}) collective-permute-start(bf16[640,256]{1,0:T(8,128)(2,1)} %get-tuple-element.54.sent), channel_id=1, source_target_pairs={{8,0},{12,4},{16,24},{20,28},{9,1},{13,5},{17,25},{21,29},{10,2},{... | collective-permute-start | bytes 983048 | tf_op jit(solution)/shard_map/ppermute | solution.py:287
  85.3 2.4 %copy-start.1 = (bf16[3,144,2560]{2,1,0:T(8,128)(2,1)}, bf16[3,144,2560]{2,1,0:T(8,128)(2,1)S(1)}, u32[]{:S(2)}) copy-start(bf16[3,144,2560]{2,1,0:T(8,128)(2,1)S(1)} %collective-permute-done.12.refs_1_.refs_3_.refs_5_) | copy-start | bytes 6635524
  87.7 1.9 %copy-start.16 = (bf16[640,1024]{1,0:T(8,128)(2,1)}, bf16[640,1024]{1,0:T(8,128)(2,1)S(1)}, u32[]{:S(2)}) copy-start(bf16[640,1024]{1,0:T(8,128)(2,1)S(1)} %block_rows.3) | copy-start | bytes 3932164
  89.5 1.7 %copy-start.14 = (bf16[1280,1024]{1,0:T(8,128)(2,1)S(1)}, bf16[1280,1024]{1,0:T(8,128)(2,1)}, u32[]{:S(2)}) copy-start(bf16[1280,1024]{1,0:T(8,128)(2,1)} %copy-done.13) | copy-start | bytes 7864324
  92.8 9.6 %copy-start.30 = (f32[512,1024]{1,0:T(8,128)}, f32[512,1024]{1,0:T(8,128)S(1)}, u32[]{:S(2)}) copy-start(f32[512,1024]{1,0:T(8,128)S(1)} %convolution_add_fusion.2) | copy-start | bytes 6291460
  101.5 1.0 copy-start.9
  102.5 1.2 copy-start.11
  103.7 26.9 %collective-permute-start.21 = (bf16[512,256]{1,0:T(8,128)(2,1)}, bf16[512,256]{1,0:T(8,128)(2,1)}, u32[]{:S(2)}, u32[]{:S(2)}) collective-permute-start(bf16[512,256]{1,0:T(8,128)(2,1)} %get-tuple-element.74), channel_id=1, source_target_pairs={{0,4},{4,0},{8,12},{12,8},{16,20},{20,16},{24,28},{28,24},{1,5},{5... | collective-permute-start | bytes 786440 | tf_op jit(solution)/shard_map/ppermute | solution.py:290
  105.2 1.8 %copy-start.2 = (bf16[3,144,2560]{2,1,0:T(8,128)(2,1)S(1)}, bf16[3,144,2560]{2,1,0:T(8,128)(2,1)}, u32[]{:S(2)}) copy-start(bf16[3,144,2560]{2,1,0:T(8,128)(2,1)} %copy-done.1) | copy-start | bytes 6635524
  106.9 11.4 %collective-permute-start.16 = (f32[2,4,640]{2,1,0:T(4,128)}, f32[2,4,640]{2,1,0:T(4,128)S(1)}, u32[]{:S(2)}, u32[]{:S(2)}) collective-permute-start(f32[2,4,640]{2,1,0:T(4,128)} %frame_lines.1), channel_id=1, source_target_pairs={{0,8},{4,12},{8,0},{12,4},{16,24},{20,28},{24,16},{28,20},{1,9},{5... | collective-permute-start | bytes 61448 | tf_op jit(solution)/shard_map/ppermute | solution.py:109
  107.0 1.1 copy-start.4
  108.1 1.1 copy-start.6
  109.2 1.3 copy-start.17
  110.5 1.7 %copy-start.15 = (bf16[1280,1024]{1,0:T(8,128)(2,1)S(1)}, bf16[1280,1024]{1,0:T(8,128)(2,1)}, u32[]{:S(2)}) copy-start(bf16[1280,1024]{1,0:T(8,128)(2,1)} %copy-done.13) | copy-start | bytes 7864324
  113.8 2.3 %copy-start.31 = (f32[2,4,640]{2,1,0:T(4,128)S(1)}, f32[2,4,640]{2,1,0:T(4,128)}, u32[]{:S(2)}) copy-start(f32[2,4,640]{2,1,0:T(4,128)} %frame_lines.1) | copy-start | bytes 61444
  113.8 2.3 %copy-start.32 = (bf16[512,256]{1,0:T(8,128)(2,1)S(1)}, bf16[512,256]{1,0:T(8,128)(2,1)}, u32[]{:S(2)}) copy-start(bf16[512,256]{1,0:T(8,128)(2,1)} %get-tuple-element.73) | copy-start | bytes 786436
  116.1 14.5 %collective-permute-start.20 = (bf16[512,256]{1,0:T(8,128)(2,1)S(1)}, bf16[512,256]{1,0:T(8,128)(2,1)S(1)}, u32[]{:S(2)}, u32[]{:S(2)}) collective-permute-start(bf16[512,256]{1,0:T(8,128)(2,1)S(1)} %copy-done.32), channel_id=1, source_target_pairs={{0,4},{4,0},{8,12},{12,8},{16,20},{20,16},{24,28},{28,24},{1,5},{5... | collective-permute-start | bytes 786440 | tf_op jit(solution)/shard_map/ppermute | solution.py:290
  121.1 1.0 copy-start.12
  121.5 4.0 %copy-start.10 = (bf16[640,256]{1,0:T(8,128)(2,1)S(1)}, bf16[640,256]{1,0:T(8,128)(2,1)}, u32[]{:S(2)}) copy-start(bf16[640,256]{1,0:T(8,128)(2,1)} %copy-done.9) | copy-start | bytes 983044
  122.5 10.1 %collective-permute-start.18 = (bf16[512,256]{1,0:T(8,128)(2,1)S(1)}, bf16[512,256]{1,0:T(8,128)(2,1)S(1)}, u32[]{:S(2)}, u32[]{:S(2)}) collective-permute-start(bf16[512,256]{1,0:T(8,128)(2,1)S(1)} %get-tuple-element.71), channel_id=1, source_target_pairs={{0,4},{4,0},{8,12},{12,8},{16,20},{20,16},{24,28},{28,24},{1,5},{5... | collective-permute-start | bytes 786440 | tf_op jit(solution)/shard_map/ppermute | solution.py:290
  123.0 12.3 %collective-permute-start.19 = (bf16[512,256]{1,0:T(8,128)(2,1)S(1)}, bf16[512,256]{1,0:T(8,128)(2,1)S(1)}, u32[]{:S(2)}, u32[]{:S(2)}) collective-permute-start(bf16[512,256]{1,0:T(8,128)(2,1)S(1)} %get-tuple-element.72), channel_id=1, source_target_pairs={{0,4},{4,0},{8,12},{12,8},{16,20},{20,16},{24,28},{28,24},{1,5},{5... | collective-permute-start | bytes 786440 | tf_op jit(solution)/shard_map/ppermute | solution.py:290
  124.6 5.1 %collective-permute-start.22 = (f32[4,4,640]{2,1,0:T(4,128)S(1)}, f32[4,4,640]{2,1,0:T(4,128)S(1)}, u32[]{:S(2)}, u32[]{:S(2)}) collective-permute-start(f32[4,4,640]{2,1,0:T(4,128)S(1)} %pad_maximum_fusion.4), channel_id=1, source_target_pairs={{0,16},{4,20},{8,24},{12,28},{16,0},{20,4},{24,8},{28,12},{1,17},{... | collective-permute-start | bytes 122888 | tf_op jit(solution)/shard_map/ppermute | solution.py:109
